TPU v7x, 128 devices: a whole 4x4x4 slice. The times are simulated.
128 devices in a mesh: dp: 32 (over z_lo, x, y), expert: 4 (over z_hi, core).
Axes of the slice: x: 4, y: 4, z: 4 (z_hi: 2, z_lo: 2; z = z_hi * 2 + z_lo), core: 2. Of those that a mesh axis runs over, the one named last changes fastest.
Arguments:
- tokens: bfloat16 [16384, 4096], P(('dp', 'expert')), may hold values from -24 to 24
- cotangent: bfloat16 [16384, 4096], P(('dp', 'expert')), may hold values from -0.59765625 to 0.59765625
- routes: int32 [16384, 8], P(('dp', 'expert')), may hold values from 0 to 127, as said below
- route_gates: float32 [16384, 8], P(('dp', 'expert')), may hold values from 0.05 to 0.4
- gate_up: bfloat16 [4, 4096, 1536], P('expert'), may hold values from -0.09375 to 0.09375
- down_proj: bfloat16 [4, 768, 4096], P('expert'), may hold values from -0.21875 to 0.21875
Outputs:
- token_grad: bfloat16 [16384, 4096], P(('dp', 'expert'))
- gate_up_grad: bfloat16 [4, 4096, 1536], P('expert', 'dp')
- down_grad: bfloat16 [4, 768, 4096], P('expert', 'dp')
Inputs may be any that keep to these rules, and one draw needn't show every extreme that they name: A row of routes names 8 different ids. In the tokens of one device (aligned blocks of 128 rows) each expert e < 4 is named by at most 48 rows. In every draw some expert is named by exactly 48 rows in every block of one data group of 4 blocks.
All inputs are finite; a program needn't handle non-finite values.
Results may differ from a plain program's by a relative error of at most 0.006.
Values may be sent and summed in bfloat16 or wider, within the bound.
No kernel may reach another device: no remote copies, remote signals or barrier semaphores. Data moves between devices by JAX's collectives and lax.ppermute only.
A program may use at most 192 MiB of HBM per device.

v0:
```python
import functools

import jax
import jax.numpy as jnp
from jax import lax
from jax.experimental import pallas as pl
from jax.experimental.pallas import tpu as pltpu
from jax.sharding import Mesh, PartitionSpec as P

CAP = 48
BF = jnp.bfloat16
F32 = jnp.float32
AXES = ("w", "x", "y", "v", "c")
VMEM = pl.BlockSpec(memory_space=pltpu.VMEM)
SMEM = pl.BlockSpec(memory_space=pltpu.SMEM)
LIMIT = 48 * 1024 * 1024


def swap_expert(a, k):
    return lax.ppermute(a, ("v", "c"), [(i, i ^ k) for i in range(4)])


def shift(a, axis, j):
    if j == 0:
        return a
    return lax.ppermute(a, axis, [(i, (i + j) % 4) for i in range(4)])


def swap_w(a):
    return lax.ppermute(a, "w", [(0, 1), (1, 0)])


def rows_dot(a, b):
    return lax.dot_general(a, b, (((0,), (0,)), ((), ())), preferred_element_type=F32)


def wide_dot(a, b):
    return lax.dot_general(a, b, (((1,), (1,)), ((), ())), preferred_element_type=F32)


def shape(rows, cols, dtype=BF):
    return jax.ShapeDtypeStruct((rows, cols), dtype)


def call(body, outs, ins, scratch=(), flops=0, moved=0, scalars=1):
    return pl.pallas_call(
        body,
        out_shape=outs,
        in_specs=[SMEM] * scalars + [VMEM] * (ins - scalars),
        out_specs=[VMEM] * len(outs),
        scratch_shapes=list(scratch),
        compiler_params=pltpu.CompilerParams(vmem_limit_bytes=LIMIT),
        cost_estimate=pl.CostEstimate(flops=flops, bytes_accessed=moved, transcendentals=0),
    )


def aligned(i, size):
    return pl.ds(pl.multiple_of(i * size, size), size)


def pack_x(at, x0, x1, x2, x3, *outs):
    x, y = at[1], at[2]
    whole, alongx, alongy = outs[0], outs[1:5], outs[5:9]
    for k, piece in enumerate((x0, x1, x2, x3)):
        rows = pl.ds(k * CAP, CAP)
        whole[rows, :] = piece[...]
        for j in range(4):
            for b in range(2):
                tx = b * 4 + lax.rem(x + j, 4)
                alongx[j][rows, b * 512 : b * 512 + 512] = piece[:, aligned(tx, 512)]
            for b in range(8):
                ty = b * 4 + lax.rem(y + j, 4)
                alongy[j][rows, b * 128 : b * 128 + 128] = piece[:, aligned(ty, 128)]


def pack_g(at, g0, g1, g2, g3, hidden, *outs):
    for j in range(4):
        cols = aligned(lax.rem(at[2] + j, 4), 1024)
        for k, piece in enumerate((g0, g1, g2, g3)):
            outs[j][k * CAP : k * CAP + CAP, :1024] = piece[:, cols]
        outs[j][:, 1024:] = hidden[...]


def act_step(x, wg, wu, hidden, slope, silu):
    gpart = jnp.dot(x[...], wg[...], preferred_element_type=F32)
    upart = jnp.dot(x[...], wu[...], preferred_element_type=F32)
    sig = jax.nn.sigmoid(gpart)
    soft = gpart * sig
    hidden[...] = (soft * upart).astype(BF)
    slope[...] = upart * (sig * (1.0 + gpart * (1.0 - sig)))
    silu[...] = soft


def act_call(X, gate_up, inner):
    rows, width = X.shape
    step = 256
    n = inner // step
    out = pl.BlockSpec((rows, step), lambda i: (0, i))
    return pl.pallas_call(
        act_step,
        grid=(n,),
        in_specs=[
            pl.BlockSpec((rows, width), lambda i: (0, 0)),
            pl.BlockSpec((width, step), lambda i: (0, i)),
            pl.BlockSpec((width, step), lambda i: (0, i + n)),
        ],
        out_specs=[out, out, out],
        out_shape=[shape(rows, inner), shape(rows, inner, F32), shape(rows, inner, F32)],
        compiler_params=pltpu.CompilerParams(vmem_limit_bytes=LIMIT),
        cost_estimate=pl.CostEstimate(
            flops=4 * rows * width * inner, bytes_accessed=4 * width * inner, transcendentals=0
        ),
    )(X, gate_up, gate_up)


def dh_step(g0, g1, g2, g3, wd, slope, silu, dact_g, dact_u, whole):
    @pl.when(pl.program_id(0) == 0)
    def _():
        for k, piece in enumerate((g0, g1, g2, g3)):
            whole[k * CAP : k * CAP + CAP, :] = piece[...]

    dh = wide_dot(whole[...], wd[...])
    dact_g[...] = (dh * slope[...]).astype(BF)
    dact_u[...] = (dh * silu[...]).astype(BF)


def dh_call(gs, down_proj, slope, silu):
    inner, width = down_proj.shape
    rows = slope.shape[0]
    step = 256
    part = pl.BlockSpec((rows, step), lambda i: (0, i))
    return pl.pallas_call(
        dh_step,
        grid=(inner // step,),
        in_specs=[pl.BlockSpec((CAP, width), lambda i: (0, 0))] * 4
        + [pl.BlockSpec((step, width), lambda i: (i, 0)), part, part],
        out_specs=[part, part],
        out_shape=[shape(rows, inner)] * 2,
        scratch_shapes=[pltpu.VMEM((rows, width), BF)],
        compiler_params=pltpu.CompilerParams(vmem_limit_bytes=LIMIT),
        cost_estimate=pl.CostEstimate(
            flops=2 * rows * width * inner, bytes_accessed=2 * width * inner, transcendentals=0
        ),
    )(*gs, down_proj, slope, silu)


def back_step(dg, du, wt, b0, b1, b2, b3):
    inner = dg.shape[1]
    got = wide_dot(dg[...], wt[:, :inner]) + wide_dot(du[...], wt[:, inner:])
    for k, out in enumerate((b0, b1, b2, b3)):
        out[...] = got[k * CAP : k * CAP + CAP].astype(BF)


def back_call(dg, du, gate_up):
    rows, inner = dg.shape
    width = gate_up.shape[0]
    step = 512
    return pl.pallas_call(
        back_step,
        grid=(width // step,),
        in_specs=[pl.BlockSpec((rows, inner), lambda i: (0, 0))] * 2
        + [pl.BlockSpec((step, 2 * inner), lambda i: (i, 0))],
        out_specs=[pl.BlockSpec((CAP, step), lambda i: (0, i))] * 4,
        out_shape=[shape(CAP, width)] * 4,
        compiler_params=pltpu.CompilerParams(vmem_limit_bytes=LIMIT),
        cost_estimate=pl.CostEstimate(
            flops=4 * rows * width * inner, bytes_accessed=4 * width * inner, transcendentals=0
        ),
    )(dg, du, gate_up)


def tok_step(mask, a0, a1, a2, a3, out, whole):
    for k, piece in enumerate((a0, a1, a2, a3)):
        whole[k * CAP : k * CAP + CAP, :] = piece[...]
    out[...] = jnp.dot(mask[...], whole[...], preferred_element_type=F32).astype(BF)


def tile_step(axis, at, *refs):
    xs, ds, outs, xall, dall = refs[:4], refs[4:8], refs[8:12], refs[12], refs[13]
    rows = xs[0].shape[0]
    for p in range(4):
        xall[p * rows : p * rows + rows, :] = xs[p][...]
        dall[p * rows : p * rows + rows, :] = ds[p][...]
    for j in (1, 2, 3, 0):
        other = lax.rem(at[axis] + j, 4)
        for b in range(2):
            got = rows_dot(xall[:, aligned(b * 4 + other, 128)], dall[...])
            outs[j][b * 128 : b * 128 + 128, :] = got.astype(outs[j].dtype)


def tile_call(axis, at, xs, ds):
    rows, part = xs[0].shape
    inner = ds[0].shape[1]
    return call(
        functools.partial(tile_step, axis),
        [shape(256, inner, F32)] + [shape(256, inner)] * 3,
        9,
        [pltpu.VMEM((4 * rows, part), BF), pltpu.VMEM((4 * rows, inner), BF)],
        flops=8 * rows * part * inner,
        moved=8 * rows * (part + inner),
    )(at, *xs, *ds)


def down_step(at, *refs):
    gh, outs, gall, hall, total = refs[:4], refs[4:8], refs[8], refs[9], refs[10]
    rows = gh[0].shape[0]
    for p in range(4):
        gall[p * rows : p * rows + rows, :] = gh[p][:, :1024]
        hall[p * rows : p * rows + rows, :] = gh[p][:, 1024:]
    for b in range(6):
        cols = slice(b * 128, b * 128 + 128)
        total[cols, :] = rows_dot(hall[:, cols], gall[...])
    for j in (1, 2, 3, 0):
        other = lax.rem(at[1] + j, 4)
        for b in range(2):
            outs[j][b * 96 : b * 96 + 96, :] = total[aligned(b * 4 + other, 96), :].astype(outs[j].dtype)


def down_call(at, gh):
    rows, wide = gh[0].shape
    inner = wide - 1024
    return call(
        down_step,
        [shape(192, 1024, F32)] + [shape(192, 1024)] * 3,
        5,
        [
            pltpu.VMEM((4 * rows, 1024), BF),
            pltpu.VMEM((4 * rows, inner), BF),
            pltpu.VMEM((inner, 1024), F32),
        ],
        flops=8 * rows * 1024 * inner,
        moved=8 * rows * wide,
    )(at, *gh)


def sum_step(at, own, r1, r2, r3, keep, send):
    half = keep.shape[0]
    w = at[0]

    def part(i):
        rows = aligned(i, half)
        return own[rows, :] + r1[rows, :].astype(F32) + r2[rows, :].astype(F32) + r3[rows, :].astype(F32)

    send[...] = part(1 - w).astype(BF)
    keep[...] = part(w)


def sum_call(at, own, got):
    rows, cols = own.shape
    return call(
        sum_step, [shape(rows // 2, cols, F32), shape(rows // 2, cols)], 5, moved=10 * rows * cols
    )(at, own, *got)


def shards(tokens, cotangent, routes, gates, gate_up, down_proj):
    gate_up, down_proj = gate_up[0], down_proj[0]
    w, x, y = lax.axis_index("w"), lax.axis_index("x"), lax.axis_index("y")
    at = jnp.stack([w, x, y]).astype(jnp.int32)
    me = lax.axis_index(("v", "c"))
    toks, width = tokens.shape
    inner = down_proj.shape[0]
    experts = jnp.bitwise_xor(me, jnp.arange(4, dtype=jnp.int32))
    matches = routes[:, :, None] == experts[None, None, :]
    member = jnp.any(matches, axis=1)
    weight = jnp.sum(jnp.where(matches, gates[:, :, None], F32(0.0)), axis=1)
    position = jnp.cumsum(member.astype(jnp.int32), axis=0) - 1
    select = member[:, :, None] & (
        position[:, :, None] == jnp.arange(CAP, dtype=jnp.int32)[None, None, :]
    )
    mask = select.astype(BF).reshape(toks, 4 * CAP)
    slot_gate = jnp.sum(jnp.where(select, weight[:, :, None], F32(0.0)), axis=0).reshape(4 * CAP, 1)
    send_x = rows_dot(mask, tokens).astype(BF).reshape(4, CAP, width)
    send_g = (rows_dot(mask, cotangent) * slot_gate).astype(BF).reshape(4, CAP, width)
    xs = [send_x[0]] + [swap_expert(send_x[k], k) for k in (1, 2, 3)]
    gs = [send_g[0]] + [swap_expert(send_g[k], k) for k in (1, 2, 3)]
    rows = 4 * CAP

    part = shape(rows, width // 4)
    packed = call(pack_x, [shape(rows, width)] + [part] * 8, 5, moved=8 * rows * width)(at, *xs)
    X = packed[0]
    xa = [shift(packed[1 + j], "x", j) for j in range(4)]
    xb = [shift(packed[5 + j], "y", j) for j in range(4)]
    hidden, slope, silu = act_call(X, gate_up, inner)
    dact_g, dact_u = dh_call(gs, down_proj, slope, silu)
    da = [shift(dact_g, "x", j) for j in range(4)]
    db = [shift(dact_u, "y", j) for j in range(4)]

    gh = call(pack_g, [shape(rows, width // 4 + inner)] * 4, 6, moved=8 * rows * width // 2)(
        at, *gs, hidden
    )
    gh = [shift(gh[j], "y", j) for j in range(4)]

    back = back_call(dact_g, dact_u, gate_up)
    arrived = [back[0]] + [swap_expert(back[k], k) for k in (1, 2, 3)]
    token_grad = call(
        tok_step,
        [shape(toks, width)],
        5,
        [pltpu.VMEM((rows, width), BF)],
        flops=2 * toks * rows * width,
        moved=2 * (rows + toks) * width,
        scalars=0,
    )(mask, *arrived)[0]

    def half(axis, name, xs, ds):
        parts = tile_call(axis, at, xs, ds)
        keep, send = sum_call(at, parts[0], [shift(parts[j], name, j) for j in (1, 2, 3)])
        return (keep + swap_w(send).astype(F32)).astype(BF)

    parts = down_call(at, gh)
    keep, send = sum_call(at, parts[0], [shift(parts[j], "x", j) for j in (1, 2, 3)])
    down = (keep + swap_w(send).astype(F32)).astype(BF).reshape(4, 24, width // 4)
    cols = [
        shift(lax.dynamic_index_in_dim(down, (y + j) % 4, 0, False), "y", j) for j in range(4)
    ]
    turned = jnp.concatenate(cols[::-1] + cols[::-1], axis=1)
    down_grad = lax.dynamic_slice_in_dim(turned, (3 - y) * (width // 4), width, 1)

    gate_grad = half(2, "y", xa, da)
    up_grad = half(1, "x", xb, db)
    return token_grad, jnp.concatenate([gate_grad, up_grad], axis=1)[None], down_grad[None]


def solution(mesh):
    fine = Mesh(mesh.devices.reshape(2, 4, 4, 2, 2), AXES)
    rows, expert, dp = P(AXES, None), ("v", "c"), ("w", "x", "y")
    in_specs = (rows, rows, rows, rows, P(expert, None, None), P(expert, None, None))
    out_specs = (rows, P(expert, dp, None), P(expert, dp, None))
    return jax.shard_map(
        shards, mesh=fine, in_specs=in_specs, out_specs=out_specs, check_vma=False
    )
```

profile of v0, /device:TPU:0, one launch (start us, length us, event | category | flops | bytes accessed | tf_op | source)
XLA Modules:
  0.0 197.4 jit_solution(15817766487270483120)
XLA Ops:
  4.0 3.4 %collective-permute-start.5 = (bf16[48,4096]{1,0:T(8,128)(2,1)S(1)}, bf16[48,4096]{1,0:T(8,128)(2,1)S(1)}, u32[]{:S(2)}, u32[]{:S(2)}) collective-permute-start(bf16[48,4096]{1,0:T(8,128)(2,1)S(1)} %get-tuple-element.85), channel_id=1, source_target_pairs={{0,3},{1,2},{2,1},{3,0},{4,7},{5,6},{6,5},{7,4},{8,11},{9,10},{10,... | collective-permute-start | bytes 1179656 | tf_op jit(solution)/shard_map/ppermute | solution.py:20
  10.0 3.0 %collective-permute-start.2 = (bf16[48,4096]{1,0:T(8,128)(2,1)}, bf16[48,4096]{1,0:T(8,128)(2,1)S(1)}, u32[]{:S(2)}, u32[]{:S(2)}) collective-permute-start(bf16[48,4096]{1,0:T(8,128)(2,1)} %get-tuple-element.89), channel_id=1, source_target_pairs={{0,3},{1,2},{2,1},{3,0},{4,7},{5,6},{6,5},{7,4},{8,11},{9,10},{10,... | collective-permute-start | bytes 1179656 | tf_op jit(solution)/shard_map/ppermute | solution.py:20
  13.6 3.3 %collective-permute-done.5.x3 = bf16[48,4096]{1,0:T(8,128)(2,1)S(1)} collective-permute-done((bf16[48,4096]{1,0:T(8,128)(2,1)S(1)}, bf16[48,4096]{1,0:T(8,128)(2,1)S(1)}, u32[]{:S(2)}, u32[]{:S(2)}) %collective-permute-start.5) | collective-permute-done | bytes 393248 | tf_op jit(solution)/shard_map/ppermute | solution.py:20
  17.8 8.6 %collective-permute-done.4.x2 = bf16[48,4096]{1,0:T(8,128)(2,1)} collective-permute-done((bf16[48,4096]{1,0:T(8,128)(2,1)}, bf16[48,4096]{1,0:T(8,128)(2,1)}, u32[]{:S(2)}, u32[]{:S(2)}) %collective-permute-start.4) | collective-permute-done | bytes 393248 | tf_op jit(solution)/shard_map/ppermute | solution.py:20
  26.4 3.0 %shard_map.85 = (bf16[192,4096]{1,0:T(8,128)(2,1)}, bf16[192,1024]{1,0:T(8,128)(2,1)S(1)}, bf16[192,1024]{1,0:T(8,128)(2,1)S(1)}, bf16[192,1024]{1,0:T(8,128)(2,...) custom-call(s32[3]{0:T(128)S(1)} %pad_add_fusion.at, ...), custom_call_target="tpu_custom_call" | custom-call | bytes 6291456 | tf_op jit(solution)/shard_map/pallas_call | solution.py:279
  30.8 6.7 %shard_map.86 = (bf16[192,768]{1,0:T(8,128)(2,1)S(1)}, f32[192,768]{1,0:T(8,128)S(1)}, f32[192,768]{1,0:T(8,128)S(1)}) custom-call(bf16[192,4096]{1,0:T(8,128)(2,1)S(1)} %copy-done.1, bf16[4096,1536]{1,0:T(8,128)(2,1)} %bitcast.25, bf16[4096,1536]{1,0:T(8,128)(2,1)} %bitcast.26), custom_call_target="tpu_custom_call" | custom-call | flops 2415919104 | bytes 12582912 | tf_op jit(solution)/shard_map/pallas_call | solution.py:99
  37.5 4.8 %collective-permute-done.1.g2 = bf16[48,4096]{1,0:T(8,128)(2,1)S(1)} collective-permute-done((bf16[48,4096]{1,0:T(8,128)(2,1)}, bf16[48,4096]{1,0:T(8,128)(2,1)S(1)}, u32[]{:S(2)}, u32[]{:S(2)}) %collective-permute-start.1) | collective-permute-done | bytes 393248 | tf_op jit(solution)/shard_map/ppermute | solution.py:20
  42.3 5.1 %shard_map.87 = (bf16[192,768]{1,0:T(8,128)(2,1)S(1)}, bf16[192,768]{1,0:T(8,128)(2,1)S(1)}) custom-call(bf16[48,4096]{1,0:T(8,128)(2,1)S(1)} %get-tuple-element.92.g0, bf16[48,4096]{1,0:T(8,128)(2,1)S(1)} %collective-permute-done.g1, bf16[48,4096]{1,0:T(8,128)(2,1)S(1)} %collective-permute-done.1.g2, bf16[48,4096]{1,0:T(8,128)(2,1)S(1)} %collective-permute-done.2.g3, ...), custom_call_target="tpu_custom_call" | custom-call | flops 1207959552 | bytes 6291456 | tf_op jit(solution)/shard_map/pallas_call | solution.py:132
  47.4 2.8 %collective-permute-start.14 = (bf16[192,768]{1,0:T(8,128)(2,1)S(1)}, bf16[192,768]{1,0:T(8,128)(2,1)S(1)}, u32[]{:S(2)}, u32[]{:S(2)}) collective-permute-start(bf16[192,768]{1,0:T(8,128)(2,1)S(1)} %get-tuple-element.46.dg.refs_4_), channel_id=1, source_target_pairs={{0,48},{16,0},{32,16},{48,32},{1,49},{17,1},{33,17},{49,33},{2,50}... | collective-permute-start | bytes 884744 | tf_op jit(solution)/shard_map/ppermute | solution.py:26
  51.9 3.0 %collective-permute-start.24 = (bf16[192,768]{1,0:T(8,128)(2,1)S(1)}, bf16[192,768]{1,0:T(8,128)(2,1)S(1)}, u32[]{:S(2)}, u32[]{:S(2)}) collective-permute-start(bf16[192,768]{1,0:T(8,128)(2,1)S(1)} %get-tuple-element.47.du.refs_4_), channel_id=1, source_target_pairs={{0,12},{4,0},{8,4},{12,8},{1,13},{5,1},{9,5},{13,9},{2,14},{6,2},{... | collective-permute-start | bytes 884744 | tf_op jit(solution)/shard_map/ppermute | solution.py:26
  55.6 7.5 %collective-permute-done.14.refs_7_ = bf16[192,768]{1,0:T(8,128)(2,1)S(1)} collective-permute-done((bf16[192,768]{1,0:T(8,128)(2,1)S(1)}, bf16[192,768]{1,0:T(8,128)(2,1)S(1)}, u32[]{:S(2)}, u32[]{:S(2)}) %collective-permute-start.14) | collective-permute-done | bytes 294944 | tf_op jit(solution)/shard_map/ppermute | solution.py:26
  63.8 5.1 %collective-permute-start.10 = (bf16[192,1024]{1,0:T(8,128)(2,1)S(1)}, bf16[192,1024]{1,0:T(8,128)(2,1)S(1)}, u32[]{:S(2)}, u32[]{:S(2)}) collective-permute-start(bf16[192,1024]{1,0:T(8,128)(2,1)S(1)} %get-tuple-element.54), channel_id=1, source_target_pairs={{0,32},{16,48},{32,0},{48,16},{1,33},{17,49},{33,1},{49,17},{2,34}... | collective-permute-start | bytes 1179656 | tf_op jit(solution)/shard_map/ppermute | solution.py:26
  72.1 7.9 %collective-permute-done.22.refs_5_ = bf16[192,768]{1,0:T(8,128)(2,1)S(1)} collective-permute-done((bf16[192,768]{1,0:T(8,128)(2,1)S(1)}, bf16[192,768]{1,0:T(8,128)(2,1)S(1)}, u32[]{:S(2)}, u32[]{:S(2)}) %collective-permute-start.22) | collective-permute-done | bytes 294944 | tf_op jit(solution)/shard_map/ppermute | solution.py:26
  80.0 2.0 %collective-permute-start.20 = (bf16[192,1024]{1,0:T(8,128)(2,1)S(1)}, bf16[192,1024]{1,0:T(8,128)(2,1)S(1)}, u32[]{:S(2)}, u32[]{:S(2)}) collective-permute-start(bf16[192,1024]{1,0:T(8,128)(2,1)S(1)} %get-tuple-element.64), channel_id=1, source_target_pairs={{0,8},{4,12},{8,0},{12,4},{1,9},{5,13},{9,1},{13,5},{2,10},{6,14},... | collective-permute-start | bytes 1179656 | tf_op jit(solution)/shard_map/ppermute | solution.py:26
  87.0 9.4 %shard_map.88 = (bf16[48,4096]{1,0:T(8,128)(2,1)S(1)}, bf16[48,4096]{1,0:T(8,128)(2,1)S(1)}, bf16[48,4096]{1,0:T(8,128)(2,1)S(1)}, bf16[48,4096]{1,0:T(8,128)(2,1)S(1)}) custom-call(bf16[192,768]{1,0:T(8,128)(2,1)S(1)} %get-tuple-element.46.dg.refs_4_, bf16[192,768]{1,0:T(8,128)(2,1)S(1)} %get-tuple-element.47.du.refs_4_, bf16[4096,1536]{1,0:T(8,128)(2,1)} %bitcast.27), custom_call_target="tpu_custom_call" | custom-call | flops 2415919104 | bytes 12582912 | tf_op jit(solution)/shard_map/pallas_call | solution.py:158
  98.0 4.0 %collective-permute-start.7 = (bf16[48,4096]{1,0:T(8,128)(2,1)S(1)}, bf16[48,4096]{1,0:T(8,128)(2,1)S(1)}, u32[]{:S(2)}, u32[]{:S(2)}) collective-permute-start(bf16[48,4096]{1,0:T(8,128)(2,1)S(1)} %get-tuple-element.50), channel_id=1, source_target_pairs={{0,2},{1,3},{2,0},{3,1},{4,6},{5,7},{6,4},{7,5},{8,10},{9,11},{10,... | collective-permute-start | bytes 1179656 | tf_op jit(solution)/shard_map/ppermute | solution.py:20
  102.0 2.9 %collective-permute-start.30 = (bf16[192,1792]{1,0:T(8,128)(2,1)S(1)}, bf16[192,1792]{1,0:T(8,128)(2,1)S(1)}, u32[]{:S(2)}, u32[]{:S(2)}) collective-permute-start(bf16[192,1792]{1,0:T(8,128)(2,1)S(1)} %get-tuple-element.75), channel_id=1, source_target_pairs={{0,8},{4,12},{8,0},{12,4},{1,9},{5,13},{9,1},{13,5},{2,10},{6,14},... | collective-permute-start | bytes 2064392 | tf_op jit(solution)/shard_map/ppermute | solution.py:26
  108.2 2.2 %shard_map.90 = (f32[256,768]{1,0:T(8,128)S(1)}, bf16[256,768]{1,0:T(8,128)(2,1)S(1)}, bf16[256,768]{1,0:T(8,128)(2,1)S(1)}, bf16[256,768]{1,0:T(8,128)(2,1)S(1)}) custom-call(s32[3]{0:T(128)S(1)} %pad_add_fusion.at, bf16[192,1024]{1,0:T(8,128)(2,1)S(1)} %get-tuple-element.52.refs_0_, bf16[192,1024]{1,0:T(8,128)(2,1)S(1)} %collective-permute-done.9.refs_1_, ...), custom_call_target="tpu_custom_call" | custom-call | flops 1207959552 | bytes 2752512 | tf_op jit(solution)/shard_map/pallas_call | solution.py:194
  112.5 2.9 %collective-permute-start.16 = (bf16[256,768]{1,0:T(8,128)(2,1)S(1)}, bf16[256,768]{1,0:T(8,128)(2,1)S(1)}, u32[]{:S(2)}, u32[]{:S(2)}) collective-permute-start(bf16[256,768]{1,0:T(8,128)(2,1)S(1)} %get-tuple-element.58), channel_id=1, source_target_pairs={{0,8},{4,12},{8,0},{12,4},{1,9},{5,13},{9,1},{13,5},{2,10},{6,14},... | collective-permute-start | bytes 1179656 | tf_op jit(solution)/shard_map/ppermute | solution.py:26
  116.7 2.8 %shard_map.92 = (f32[256,768]{1,0:T(8,128)S(1)}, bf16[256,768]{1,0:T(8,128)(2,1)S(1)}, bf16[256,768]{1,0:T(8,128)(2,1)S(1)}, bf16[256,768]{1,0:T(8,128)(2,1)}) custom-call(s32[3]{0:T(128)S(1)} %pad_add_fusion.at, bf16[192,1024]{1,0:T(8,128)(2,1)S(1)} %get-tuple-element.62.refs_0_, bf16[192,1024]{1,0:T(8,128)(2,1)S(1)} %collective-permute-done.19.refs_1_, ...), custom_call_target="tpu_custom_call" | custom-call | flops 1207959552 | bytes 2752512 | tf_op jit(solution)/shard_map/pallas_call | solution.py:194
  119.5 8.2 %collective-permute-done.30.refs_2_ = bf16[192,1792]{1,0:T(8,128)(2,1)S(1)} collective-permute-done((bf16[192,1792]{1,0:T(8,128)(2,1)S(1)}, bf16[192,1792]{1,0:T(8,128)(2,1)S(1)}, u32[]{:S(2)}, u32[]{:S(2)}) %collective-permute-start.30) | collective-permute-done | bytes 688160 | tf_op jit(solution)/shard_map/ppermute | solution.py:26
  127.7 8.3 %collective-permute-done.15.r1 = bf16[256,768]{1,0:T(8,128)(2,1)S(1)} collective-permute-done((bf16[256,768]{1,0:T(8,128)(2,1)S(1)}, bf16[256,768]{1,0:T(8,128)(2,1)S(1)}, u32[]{:S(2)}, u32[]{:S(2)}) %collective-permute-start.15) | collective-permute-done | bytes 393248 | tf_op jit(solution)/shard_map/ppermute | solution.py:26
  136.1 6.1 %collective-permute-done.16.r2 = bf16[256,768]{1,0:T(8,128)(2,1)S(1)} collective-permute-done((bf16[256,768]{1,0:T(8,128)(2,1)S(1)}, bf16[256,768]{1,0:T(8,128)(2,1)S(1)}, u32[]{:S(2)}, u32[]{:S(2)}) %collective-permute-start.16) | collective-permute-done | bytes 393248 | tf_op jit(solution)/shard_map/ppermute | solution.py:26
  142.5 9.2 %collective-permute-done.17.r3 = bf16[256,768]{1,0:T(8,128)(2,1)S(1)} collective-permute-done((bf16[256,768]{1,0:T(8,128)(2,1)S(1)}, bf16[256,768]{1,0:T(8,128)(2,1)S(1)}, u32[]{:S(2)}, u32[]{:S(2)}) %collective-permute-start.17) | collective-permute-done | bytes 393248 | tf_op jit(solution)/shard_map/ppermute | solution.py:26
  154.0 3.3 %shard_map.95 = (f32[192,1024]{1,0:T(8,128)S(1)}, bf16[192,1024]{1,0:T(8,128)(2,1)}, bf16[192,1024]{1,0:T(8,128)(2,1)}, bf16[192,1024]{1,0:T(8,128)(2,1)}) custom-call(s32[3]{0:T(128)S(1)} %pad_add_fusion.at, bf16[192,1792]{1,0:T(8,128)(2,1)S(1)} %get-tuple-element.73.refs_0_, bf16[192,1792]{1,0:T(8,128)(2,1)S(1)} %collective-permute-done.29.refs_1_, ...), custom_call_target="tpu_custom_call" | custom-call | flops 1207959552 | bytes 2752512 | tf_op jit(solution)/shard_map/pallas_call | solution.py:222
  158.1 2.0 %collective-permute-start.32 = (bf16[192,1024]{1,0:T(8,128)(2,1)}, bf16[192,1024]{1,0:T(8,128)(2,1)}, u32[]{:S(2)}, u32[]{:S(2)}) collective-permute-start(bf16[192,1024]{1,0:T(8,128)(2,1)} %get-tuple-element.78), channel_id=1, source_target_pairs={{0,16},{16,32},{32,48},{48,0},{1,17},{17,33},{33,49},{49,1},{2,18}... | collective-permute-start | bytes 1179656 | tf_op jit(solution)/shard_map/ppermute | solution.py:26
  160.9 2.7 %collective-permute-start.34 = (bf16[192,1024]{1,0:T(8,128)(2,1)}, bf16[192,1024]{1,0:T(8,128)(2,1)}, u32[]{:S(2)}, u32[]{:S(2)}) collective-permute-start(bf16[192,1024]{1,0:T(8,128)(2,1)} %get-tuple-element.80), channel_id=1, source_target_pairs={{0,48},{16,0},{32,16},{48,32},{1,49},{17,1},{33,17},{49,33},{2,50}... | collective-permute-start | bytes 1179656 | tf_op jit(solution)/shard_map/ppermute | solution.py:26
  172.3 5.9 %collective-permute-done.32.r1 = bf16[192,1024]{1,0:T(8,128)(2,1)} collective-permute-done((bf16[192,1024]{1,0:T(8,128)(2,1)}, bf16[192,1024]{1,0:T(8,128)(2,1)}, u32[]{:S(2)}, u32[]{:S(2)}) %collective-permute-start.32) | collective-permute-done | bytes 393248 | tf_op jit(solution)/shard_map/ppermute | solution.py:26
  181.9 4.7 %collective-permute-done.35 = bf16[96,1024]{1,0:T(8,128)(2,1)S(1)} collective-permute-done((bf16[96,1024]{1,0:T(8,128)(2,1)S(1)}, bf16[96,1024]{1,0:T(8,128)(2,1)S(1)}, u32[]{:S(2)}, u32[]{:S(2)}) %collective-permute-start.35) | collective-permute-done | bytes 196640 | tf_op jit(solution)/shard_map/ppermute | solution.py:30
  186.7 3.4 %collective-permute-start.36 = (bf16[24,1024]{1,0:T(8,128)(2,1)S(1)}, bf16[24,1024]{1,0:T(8,128)(2,1)S(1)}, u32[]{:S(2)}, u32[]{:S(2)}) collective-permute-start(bf16[24,1024]{1,0:T(8,128)(2,1)S(1)} %get-tuple-element.95), channel_id=1, source_target_pairs={{0,12},{4,0},{8,4},{12,8},{1,13},{5,1},{9,5},{13,9},{2,14},{6,2},{... | collective-permute-start | bytes 147464 | tf_op jit(solution)/shard_map/ppermute | solution.py:26
  190.8 1.9 collective-permute-start.37
  192.7 3.8 %collective-permute-done.37 = bf16[24,1024]{1,0:T(8,128)(2,1)S(1)} collective-permute-done((bf16[24,1024]{1,0:T(8,128)(2,1)S(1)}, bf16[24,1024]{1,0:T(8,128)(2,1)S(1)}, u32[]{:S(2)}, u32[]{:S(2)}) %collective-permute-start.37) | collective-permute-done | bytes 49184 | tf_op jit(solution)/shard_map/ppermute | solution.py:26
  (140 shorter events, 46.5 us)
Async XLA Ops:
  4.0 12.9 %collective-permute-start.5 = (bf16[48,4096]{1,0:T(8,128)(2,1)S(1)}, bf16[48,4096]{1,0:T(8,128)(2,1)S(1)}, u32[]{:S(2)}, u32[]{:S(2)}) collective-permute-start(bf16[48,4096]{1,0:T(8,128)(2,1)S(1)} %get-tuple-element.85), channel_id=1, source_target_pairs={{0,3},{1,2},{2,1},{3,0},{4,7},{5,6},{6,5},{7,4},{8,11},{9,10},{10,... | collective-permute-start | bytes 1179656 | tf_op jit(solution)/shard_map/ppermute | solution.py:20
  7.4 19.0 %collective-permute-start.4 = (bf16[48,4096]{1,0:T(8,128)(2,1)}, bf16[48,4096]{1,0:T(8,128)(2,1)}, u32[]{:S(2)}, u32[]{:S(2)}) collective-permute-start(bf16[48,4096]{1,0:T(8,128)(2,1)} %get-tuple-element.86), channel_id=1, source_target_pairs={{0,2},{1,3},{2,0},{3,1},{4,6},{5,7},{6,4},{7,5},{8,10},{9,11},{10,... | collective-permute-start | bytes 1179656 | tf_op jit(solution)/shard_map/ppermute | solution.py:20
  8.0 18.4 %collective-permute-start.3 = (bf16[48,4096]{1,0:T(8,128)(2,1)}, bf16[48,4096]{1,0:T(8,128)(2,1)}, u32[]{:S(2)}, u32[]{:S(2)}) collective-permute-start(bf16[48,4096]{1,0:T(8,128)(2,1)} %get-tuple-element.87), channel_id=1, source_target_pairs={{0,1},{1,0},{2,3},{3,2},{4,5},{5,4},{6,7},{7,6},{8,9},{9,8},{10,11... | collective-permute-start | bytes 1179656 | tf_op jit(solution)/shard_map/ppermute | solution.py:20
  10.0 27.5 %collective-permute-start.2 = (bf16[48,4096]{1,0:T(8,128)(2,1)}, bf16[48,4096]{1,0:T(8,128)(2,1)S(1)}, u32[]{:S(2)}, u32[]{:S(2)}) collective-permute-start(bf16[48,4096]{1,0:T(8,128)(2,1)} %get-tuple-element.89), channel_id=1, source_target_pairs={{0,3},{1,2},{2,1},{3,0},{4,7},{5,6},{6,5},{7,4},{8,11},{9,10},{10,... | collective-permute-start | bytes 1179656 | tf_op jit(solution)/shard_map/ppermute | solution.py:20
  13.0 29.4 %collective-permute-start.1 = (bf16[48,4096]{1,0:T(8,128)(2,1)}, bf16[48,4096]{1,0:T(8,128)(2,1)S(1)}, u32[]{:S(2)}, u32[]{:S(2)}) collective-permute-start(bf16[48,4096]{1,0:T(8,128)(2,1)} %get-tuple-element.90), channel_id=1, source_target_pairs={{0,2},{1,3},{2,0},{3,1},{4,6},{5,7},{6,4},{7,5},{8,10},{9,11},{10,... | collective-permute-start | bytes 1179656 | tf_op jit(solution)/shard_map/ppermute | solution.py:20
  16.9 25.4 %collective-permute-start = (bf16[48,4096]{1,0:T(8,128)(2,1)}, bf16[48,4096]{1,0:T(8,128)(2,1)S(1)}, u32[]{:S(2)}, u32[]{:S(2)}) collective-permute-start(bf16[48,4096]{1,0:T(8,128)(2,1)} %get-tuple-element.91), channel_id=1, source_target_pairs={{0,1},{1,0},{2,3},{3,2},{4,5},{5,4},{6,7},{7,6},{8,9},{9,8},{10,11... | collective-permute-start | bytes 1179656 | tf_op jit(solution)/shard_map/ppermute | solution.py:20
  47.4 15.6 %collective-permute-start.14 = (bf16[192,768]{1,0:T(8,128)(2,1)S(1)}, bf16[192,768]{1,0:T(8,128)(2,1)S(1)}, u32[]{:S(2)}, u32[]{:S(2)}) collective-permute-start(bf16[192,768]{1,0:T(8,128)(2,1)S(1)} %get-tuple-element.46.dg.refs_4_), channel_id=1, source_target_pairs={{0,48},{16,0},{32,16},{48,32},{1,49},{17,1},{33,17},{49,33},{2,50}... | collective-permute-start | bytes 884744 | tf_op jit(solution)/shard_map/ppermute | solution.py:26
  50.2 13.5 %collective-permute-start.13 = (bf16[192,768]{1,0:T(8,128)(2,1)S(1)}, bf16[192,768]{1,0:T(8,128)(2,1)S(1)}, u32[]{:S(2)}, u32[]{:S(2)}) collective-permute-start(bf16[192,768]{1,0:T(8,128)(2,1)S(1)} %get-tuple-element.46.dg.refs_4_), channel_id=1, source_target_pairs={{0,32},{16,48},{32,0},{48,16},{1,33},{17,49},{33,1},{49,17},{2,34}... | collective-permute-start | bytes 884744 | tf_op jit(solution)/shard_map/ppermute | solution.py:26
  51.0 17.8 %collective-permute-start.12 = (bf16[192,768]{1,0:T(8,128)(2,1)S(1)}, bf16[192,768]{1,0:T(8,128)(2,1)S(1)}, u32[]{:S(2)}, u32[]{:S(2)}) collective-permute-start(bf16[192,768]{1,0:T(8,128)(2,1)S(1)} %get-tuple-element.46.dg.refs_4_), channel_id=1, source_target_pairs={{0,16},{16,32},{32,48},{48,0},{1,17},{17,33},{33,49},{49,1},{2,18}... | collective-permute-start | bytes 884744 | tf_op jit(solution)/shard_map/ppermute | solution.py:26
  51.9 18.5 %collective-permute-start.24 = (bf16[192,768]{1,0:T(8,128)(2,1)S(1)}, bf16[192,768]{1,0:T(8,128)(2,1)S(1)}, u32[]{:S(2)}, u32[]{:S(2)}) collective-permute-start(bf16[192,768]{1,0:T(8,128)(2,1)S(1)} %get-tuple-element.47.du.refs_4_), channel_id=1, source_target_pairs={{0,12},{4,0},{8,4},{12,8},{1,13},{5,1},{9,5},{13,9},{2,14},{6,2},{... | collective-permute-start | bytes 884744 | tf_op jit(solution)/shard_map/ppermute | solution.py:26
  54.9 15.5 %collective-permute-start.23 = (bf16[192,768]{1,0:T(8,128)(2,1)S(1)}, bf16[192,768]{1,0:T(8,128)(2,1)S(1)}, u32[]{:S(2)}, u32[]{:S(2)}) collective-permute-start(bf16[192,768]{1,0:T(8,128)(2,1)S(1)} %get-tuple-element.47.du.refs_4_), channel_id=1, source_target_pairs={{0,8},{4,12},{8,0},{12,4},{1,9},{5,13},{9,1},{13,5},{2,10},{6,14},... | collective-permute-start | bytes 884744 | tf_op jit(solution)/shard_map/ppermute | solution.py:26
  63.7 19.0 %collective-permute-start.9 = (bf16[192,1024]{1,0:T(8,128)(2,1)S(1)}, bf16[192,1024]{1,0:T(8,128)(2,1)S(1)}, u32[]{:S(2)}, u32[]{:S(2)}) collective-permute-start(bf16[192,1024]{1,0:T(8,128)(2,1)S(1)} %get-tuple-element.53), channel_id=1, source_target_pairs={{0,16},{16,32},{32,48},{48,0},{1,17},{17,33},{33,49},{49,1},{2,18}... | collective-permute-start | bytes 1179656 | tf_op jit(solution)/shard_map/ppermute | solution.py:26
  63.8 21.7 %collective-permute-start.10 = (bf16[192,1024]{1,0:T(8,128)(2,1)S(1)}, bf16[192,1024]{1,0:T(8,128)(2,1)S(1)}, u32[]{:S(2)}, u32[]{:S(2)}) collective-permute-start(bf16[192,1024]{1,0:T(8,128)(2,1)S(1)} %get-tuple-element.54), channel_id=1, source_target_pairs={{0,32},{16,48},{32,0},{48,16},{1,33},{17,49},{33,1},{49,17},{2,34}... | collective-permute-start | bytes 1179656 | tf_op jit(solution)/shard_map/ppermute | solution.py:26
  70.5 26.8 %collective-permute-start.11 = (bf16[192,1024]{1,0:T(8,128)(2,1)S(1)}, bf16[192,1024]{1,0:T(8,128)(2,1)S(1)}, u32[]{:S(2)}, u32[]{:S(2)}) collective-permute-start(bf16[192,1024]{1,0:T(8,128)(2,1)S(1)} %get-tuple-element.55), channel_id=1, source_target_pairs={{0,48},{16,0},{32,16},{48,32},{1,49},{17,1},{33,17},{49,33},{2,50}... | collective-permute-start | bytes 1179656 | tf_op jit(solution)/shard_map/ppermute | solution.py:26
  70.5 27.5 %collective-permute-start.19 = (bf16[192,1024]{1,0:T(8,128)(2,1)S(1)}, bf16[192,1024]{1,0:T(8,128)(2,1)S(1)}, u32[]{:S(2)}, u32[]{:S(2)}) collective-permute-start(bf16[192,1024]{1,0:T(8,128)(2,1)S(1)} %get-tuple-element.63), channel_id=1, source_target_pairs={{0,4},{4,8},{8,12},{12,0},{1,5},{5,9},{9,13},{13,1},{2,6},{6,10},{... | collective-permute-start | bytes 1179656 | tf_op jit(solution)/shard_map/ppermute | solution.py:26
  80.0 21.9 %collective-permute-start.20 = (bf16[192,1024]{1,0:T(8,128)(2,1)S(1)}, bf16[192,1024]{1,0:T(8,128)(2,1)S(1)}, u32[]{:S(2)}, u32[]{:S(2)}) collective-permute-start(bf16[192,1024]{1,0:T(8,128)(2,1)S(1)} %get-tuple-element.64), channel_id=1, source_target_pairs={{0,8},{4,12},{8,0},{12,4},{1,9},{5,13},{9,1},{13,5},{2,10},{6,14},... | collective-permute-start | bytes 1179656 | tf_op jit(solution)/shard_map/ppermute | solution.py:26
  82.8 22.1 %collective-permute-start.21 = (bf16[192,1024]{1,0:T(8,128)(2,1)S(1)}, bf16[192,1024]{1,0:T(8,128)(2,1)S(1)}, u32[]{:S(2)}, u32[]{:S(2)}) collective-permute-start(bf16[192,1024]{1,0:T(8,128)(2,1)S(1)} %get-tuple-element.65), channel_id=1, source_target_pairs={{0,12},{4,0},{8,4},{12,8},{1,13},{5,1},{9,5},{13,9},{2,14},{6,2},{... | collective-permute-start | bytes 1179656 | tf_op jit(solution)/shard_map/ppermute | solution.py:26
  85.5 29.9 %collective-permute-start.29 = (bf16[192,1792]{1,0:T(8,128)(2,1)S(1)}, bf16[192,1792]{1,0:T(8,128)(2,1)S(1)}, u32[]{:S(2)}, u32[]{:S(2)}) collective-permute-start(bf16[192,1792]{1,0:T(8,128)(2,1)S(1)} %get-tuple-element.74), channel_id=1, source_target_pairs={{0,4},{4,8},{8,12},{12,0},{1,5},{5,9},{9,13},{13,1},{2,6},{6,10},{... | collective-permute-start | bytes 2064392 | tf_op jit(solution)/shard_map/ppermute | solution.py:26
  98.0 13.8 %collective-permute-start.7 = (bf16[48,4096]{1,0:T(8,128)(2,1)S(1)}, bf16[48,4096]{1,0:T(8,128)(2,1)S(1)}, u32[]{:S(2)}, u32[]{:S(2)}) collective-permute-start(bf16[48,4096]{1,0:T(8,128)(2,1)S(1)} %get-tuple-element.50), channel_id=1, source_target_pairs={{0,2},{1,3},{2,0},{3,1},{4,6},{5,7},{6,4},{7,5},{8,10},{9,11},{10,... | collective-permute-start | bytes 1179656 | tf_op jit(solution)/shard_map/ppermute | solution.py:20
  102.0 25.8 %collective-permute-start.30 = (bf16[192,1792]{1,0:T(8,128)(2,1)S(1)}, bf16[192,1792]{1,0:T(8,128)(2,1)S(1)}, u32[]{:S(2)}, u32[]{:S(2)}) collective-permute-start(bf16[192,1792]{1,0:T(8,128)(2,1)S(1)} %get-tuple-element.75), channel_id=1, source_target_pairs={{0,8},{4,12},{8,0},{12,4},{1,9},{5,13},{9,1},{13,5},{2,10},{6,14},... | collective-permute-start | bytes 2064392 | tf_op jit(solution)/shard_map/ppermute | solution.py:26
  104.9 48.2 %collective-permute-start.31 = (bf16[192,1792]{1,0:T(8,128)(2,1)S(1)}, bf16[192,1792]{1,0:T(8,128)(2,1)S(1)}, u32[]{:S(2)}, u32[]{:S(2)}) collective-permute-start(bf16[192,1792]{1,0:T(8,128)(2,1)S(1)} %get-tuple-element.76), channel_id=1, source_target_pairs={{0,12},{4,0},{8,4},{12,8},{1,13},{5,1},{9,5},{13,9},{2,14},{6,2},{... | collective-permute-start | bytes 2064392 | tf_op jit(solution)/shard_map/ppermute | solution.py:26
  110.4 25.6 %collective-permute-start.15 = (bf16[256,768]{1,0:T(8,128)(2,1)S(1)}, bf16[256,768]{1,0:T(8,128)(2,1)S(1)}, u32[]{:S(2)}, u32[]{:S(2)}) collective-permute-start(bf16[256,768]{1,0:T(8,128)(2,1)S(1)} %get-tuple-element.57), channel_id=1, source_target_pairs={{0,4},{4,8},{8,12},{12,0},{1,5},{5,9},{9,13},{13,1},{2,6},{6,10},{... | collective-permute-start | bytes 1179656 | tf_op jit(solution)/shard_map/ppermute | solution.py:26
  112.5 29.7 %collective-permute-start.16 = (bf16[256,768]{1,0:T(8,128)(2,1)S(1)}, bf16[256,768]{1,0:T(8,128)(2,1)S(1)}, u32[]{:S(2)}, u32[]{:S(2)}) collective-permute-start(bf16[256,768]{1,0:T(8,128)(2,1)S(1)} %get-tuple-element.58), channel_id=1, source_target_pairs={{0,8},{4,12},{8,0},{12,4},{1,9},{5,13},{9,1},{13,5},{2,10},{6,14},... | collective-permute-start | bytes 1179656 | tf_op jit(solution)/shard_map/ppermute | solution.py:26
  115.4 36.3 %collective-permute-start.17 = (bf16[256,768]{1,0:T(8,128)(2,1)S(1)}, bf16[256,768]{1,0:T(8,128)(2,1)S(1)}, u32[]{:S(2)}, u32[]{:S(2)}) collective-permute-start(bf16[256,768]{1,0:T(8,128)(2,1)S(1)} %get-tuple-element.59), channel_id=1, source_target_pairs={{0,12},{4,0},{8,4},{12,8},{1,13},{5,1},{9,5},{13,9},{2,14},{6,2},{... | collective-permute-start | bytes 1179656 | tf_op jit(solution)/shard_map/ppermute | solution.py:26
  127.7 29.6 %collective-permute-start.8 = (bf16[48,4096]{1,0:T(8,128)(2,1)S(1)}, bf16[48,4096]{1,0:T(8,128)(2,1)S(1)}, u32[]{:S(2)}, u32[]{:S(2)}) collective-permute-start(bf16[48,4096]{1,0:T(8,128)(2,1)S(1)} %get-tuple-element.51), channel_id=1, source_target_pairs={{0,3},{1,2},{2,1},{3,0},{4,7},{5,6},{6,5},{7,4},{8,11},{9,10},{10,... | collective-permute-start | bytes 1179656 | tf_op jit(solution)/shard_map/ppermute | solution.py:20
  136.0 24.1 %collective-permute-start.25 = (bf16[256,768]{1,0:T(8,128)(2,1)S(1)}, bf16[256,768]{1,0:T(8,128)(2,1)S(1)}, u32[]{:S(2)}, u32[]{:S(2)}) collective-permute-start(bf16[256,768]{1,0:T(8,128)(2,1)S(1)} %get-tuple-element.67), channel_id=1, source_target_pairs={{0,16},{16,32},{32,48},{48,0},{1,17},{17,33},{33,49},{49,1},{2,18}... | collective-permute-start | bytes 1179656 | tf_op jit(solution)/shard_map/ppermute | solution.py:26
  142.1 18.0 %collective-permute-start.26 = (bf16[256,768]{1,0:T(8,128)(2,1)S(1)}, bf16[256,768]{1,0:T(8,128)(2,1)S(1)}, u32[]{:S(2)}, u32[]{:S(2)}) collective-permute-start(bf16[256,768]{1,0:T(8,128)(2,1)S(1)} %get-tuple-element.68), channel_id=1, source_target_pairs={{0,32},{16,48},{32,0},{48,16},{1,33},{17,49},{33,1},{49,17},{2,34}... | collective-permute-start | bytes 1179656 | tf_op jit(solution)/shard_map/ppermute | solution.py:26
  151.7 17.3 %collective-permute-start.27 = (bf16[256,768]{1,0:T(8,128)(2,1)}, bf16[256,768]{1,0:T(8,128)(2,1)}, u32[]{:S(2)}, u32[]{:S(2)}) collective-permute-start(bf16[256,768]{1,0:T(8,128)(2,1)} %get-tuple-element.69), channel_id=1, source_target_pairs={{0,48},{16,0},{32,16},{48,32},{1,49},{17,1},{33,17},{49,33},{2,50}... | collective-permute-start | bytes 1179656 | tf_op jit(solution)/shard_map/ppermute | solution.py:26
  153.0 18.3 %collective-permute-start.18 = (bf16[128,768]{1,0:T(8,128)(2,1)}, bf16[128,768]{1,0:T(8,128)(2,1)}, u32[]{:S(2)}, u32[]{:S(2)}) collective-permute-start(bf16[128,768]{1,0:T(8,128)(2,1)} %get-tuple-element.61), channel_id=1, source_target_pairs={{0,64},{64,0},{1,65},{65,1},{2,66},{66,2},{3,67},{67,3},{4,68},{68... | collective-permute-start | bytes 589832 | tf_op jit(solution)/shard_map/ppermute | solution.py:30
  158.1 20.1 %collective-permute-start.32 = (bf16[192,1024]{1,0:T(8,128)(2,1)}, bf16[192,1024]{1,0:T(8,128)(2,1)}, u32[]{:S(2)}, u32[]{:S(2)}) collective-permute-start(bf16[192,1024]{1,0:T(8,128)(2,1)} %get-tuple-element.78), channel_id=1, source_target_pairs={{0,16},{16,32},{32,48},{48,0},{1,17},{17,33},{33,49},{49,1},{2,18}... | collective-permute-start | bytes 1179656 | tf_op jit(solution)/shard_map/ppermute | solution.py:26
  160.2 18.0 %collective-permute-start.33 = (bf16[192,1024]{1,0:T(8,128)(2,1)}, bf16[192,1024]{1,0:T(8,128)(2,1)}, u32[]{:S(2)}, u32[]{:S(2)}) collective-permute-start(bf16[192,1024]{1,0:T(8,128)(2,1)} %get-tuple-element.79), channel_id=1, source_target_pairs={{0,32},{16,48},{32,0},{48,16},{1,33},{17,49},{33,1},{49,17},{2,34}... | collective-permute-start | bytes 1179656 | tf_op jit(solution)/shard_map/ppermute | solution.py:26
  160.9 18.4 %collective-permute-start.34 = (bf16[192,1024]{1,0:T(8,128)(2,1)}, bf16[192,1024]{1,0:T(8,128)(2,1)}, u32[]{:S(2)}, u32[]{:S(2)}) collective-permute-start(bf16[192,1024]{1,0:T(8,128)(2,1)} %get-tuple-element.80), channel_id=1, source_target_pairs={{0,48},{16,0},{32,16},{48,32},{1,49},{17,1},{33,17},{49,33},{2,50}... | collective-permute-start | bytes 1179656 | tf_op jit(solution)/shard_map/ppermute | solution.py:26
  (30 other events, 179.6 us)
where the time goes:
time: 199 us; the launch traced here: 197 us
  waiting for transfers between devices  81.8 us (41%)
  starting transfers between devices  56.4 us (28%)
  Pallas kernels  38.5 us (19%)
  local copies, waits for them, and re-layouts  15.3 us (8%)
  other arithmetic  3.17 us (2%)
    ppermute x27, waiting for transfers between devices, shift(): return lax.ppermute(a, axis, [(i, (i + j) % 4) for i in range(4)])  59.8 us
    ppermute x27, starting transfers between devices, shift(): return lax.ppermute(a, axis, [(i, (i + j) % 4) for i in range(4)])  40.8 us
    ppermute x9, waiting for transfers between devices, swap_expert(): return lax.ppermute(a, ('v', 'c'), [(i, i ^ k) for i in range(4)])  17.4 us
    ppermute x9, starting transfers between devices, swap_expert(): return lax.ppermute(a, ('v', 'c'), [(i, i ^ k) for i in range(4)])  12.5 us
    unnamed x53, local copies, waits for them, and re-layouts  11.9 us
    pallas_call x1, Pallas kernels, back_call(): pl.pallas_call(back_step, grid=(width // step,), in_specs=[pl.BlockSpec((...  9.41 us
    pallas_call x1, Pallas kernels, act_call(): pl.pallas_call(act_step, grid=(n,), in_specs=[pl.BlockSpec((rows, width),...  6.69 us
    pallas_call x1, Pallas kernels, dh_call(): pl.pallas_call(dh_step, grid=(inner // step,), in_specs=[pl.BlockSpec((CA...  5.05 us
  transfers between devices with their start and end apart: 39, of which 16 were waited for; matrix products, arithmetic and copies ran while one was open for 2% of the time, Pallas kernels for 17%

commit v1 on v0

v1 whole, which is shorter than its diff:
```python
import functools

import jax
import jax.numpy as jnp
from jax import lax
from jax.experimental import pallas as pl
from jax.experimental.pallas import tpu as pltpu
from jax.sharding import Mesh, PartitionSpec as P

CAP = 48
BF = jnp.bfloat16
F32 = jnp.float32
AXES = ("w", "x", "y", "v", "c")
VMEM = pl.BlockSpec(memory_space=pltpu.VMEM)
SMEM = pl.BlockSpec(memory_space=pltpu.SMEM)
MB = 1024 * 1024


def swap_expert(a):
    return lax.all_to_all(a, ("v", "c"), split_axis=0, concat_axis=0, tiled=True)


def shift(a, axis, j):
    if j == 0:
        return a
    return lax.ppermute(a, axis, [(i, (i + j) % 4) for i in range(4)])


def swap_w(a):
    return lax.ppermute(a, "w", [(0, 1), (1, 0)])


def rows_dot(a, b):
    return lax.dot_general(a, b, (((0,), (0,)), ((), ())), preferred_element_type=F32)


def wide_dot(a, b):
    return lax.dot_general(a, b, (((1,), (1,)), ((), ())), preferred_element_type=F32)


def shape(rows, cols, dtype=BF):
    return jax.ShapeDtypeStruct((rows, cols), dtype)


def call(body, outs, ins, scratch=(), flops=0, moved=0, scalars=1, after=0, limit=8):
    return pl.pallas_call(
        body,
        out_shape=outs,
        in_specs=[SMEM] * scalars + [VMEM] * (ins - scalars) + [pl.BlockSpec(memory_space=pl.ANY)] * after,
        out_specs=[VMEM] * len(outs),
        scratch_shapes=list(scratch),
        compiler_params=pltpu.CompilerParams(vmem_limit_bytes=limit * MB),
        cost_estimate=pl.CostEstimate(flops=flops, bytes_accessed=moved, transcendentals=0),
    )


def aligned(i, size):
    return pl.ds(pl.multiple_of(i * size, size), size)


def pack_x(at, whole, *outs):
    for j in range(4):
        for b in range(2):
            cols = aligned(b * 4 + lax.rem(at[1] + j, 4), 512)
            outs[j][:, b * 512 : b * 512 + 512] = whole[:, cols]


def pack_g(whole, hidden, *rest):
    out, part = rest[-1], whole.shape[1] // 4
    for i in range(4):
        out[i, :, :part] = whole[:, i * part : i * part + part]
        out[i, :, part:] = hidden[...]


def act_step(x, wg, wu, hidden, slope, silu):
    gpart = jnp.dot(x[...], wg[...], preferred_element_type=F32)
    upart = jnp.dot(x[...], wu[...], preferred_element_type=F32)
    sig = jax.nn.sigmoid(gpart)
    soft = gpart * sig
    hidden[...] = (soft * upart).astype(BF)
    slope[...] = upart * (sig * (1.0 + gpart * (1.0 - sig)))
    silu[...] = soft


def act_call(X, gate_up, inner):
    rows, width = X.shape
    step = 256
    n = inner // step
    out = pl.BlockSpec((rows, step), lambda i: (0, i))
    return pl.pallas_call(
        act_step,
        grid=(n,),
        in_specs=[
            pl.BlockSpec((rows, width), lambda i: (0, 0)),
            pl.BlockSpec((width, step), lambda i: (0, i)),
            pl.BlockSpec((width, step), lambda i: (0, i + n)),
        ],
        out_specs=[out, out, out],
        out_shape=[shape(rows, inner), shape(rows, inner, F32), shape(rows, inner, F32)],
        compiler_params=pltpu.CompilerParams(vmem_limit_bytes=16 * MB),
        cost_estimate=pl.CostEstimate(
            flops=4 * rows * width * inner, bytes_accessed=4 * width * inner, transcendentals=0
        ),
    )(X, gate_up, gate_up)


def dh_step(whole, wd, slope, silu, *rest):
    dact = rest[-1]
    dh = wide_dot(whole[...], wd[...])
    dact[0] = (dh * slope[...]).astype(BF)
    dact[1] = (dh * silu[...]).astype(BF)


def dh_call(G, down_proj, slope, silu, after):
    inner, width = down_proj.shape
    rows = slope.shape[0]
    step = 256
    part = pl.BlockSpec((rows, step), lambda i: (0, i))
    return pl.pallas_call(
        dh_step,
        grid=(inner // step,),
        in_specs=[
            pl.BlockSpec((rows, width), lambda i: (0, 0)),
            pl.BlockSpec((step, width), lambda i: (i, 0)),
            part,
            part,
        ]
        + [pl.BlockSpec(memory_space=pl.ANY)] * len(after),
        out_specs=pl.BlockSpec((2, rows, step), lambda i: (0, 0, i)),
        out_shape=jax.ShapeDtypeStruct((2, rows, inner), BF),
        compiler_params=pltpu.CompilerParams(vmem_limit_bytes=16 * MB),
        cost_estimate=pl.CostEstimate(
            flops=2 * rows * width * inner, bytes_accessed=2 * width * inner, transcendentals=0
        ),
    )(G, down_proj, slope, silu, *after)


def back_step(dact, wt, *rest):
    out, inner = rest[-1], dact.shape[2]
    out[...] = (wide_dot(dact[0], wt[:, :inner]) + wide_dot(dact[1], wt[:, inner:])).astype(BF)


def back_call(dact, gate_up, after):
    rows, inner = dact.shape[1:]
    width = gate_up.shape[0]
    step = 512
    return pl.pallas_call(
        back_step,
        grid=(width // step,),
        in_specs=[pl.BlockSpec((2, rows, inner), lambda i: (0, 0, 0))]
        + [pl.BlockSpec((step, 2 * inner), lambda i: (i, 0))]
        + [pl.BlockSpec(memory_space=pl.ANY)] * len(after),
        out_specs=pl.BlockSpec((rows, step), lambda i: (0, i)),
        out_shape=shape(rows, width),
        compiler_params=pltpu.CompilerParams(vmem_limit_bytes=16 * MB),
        cost_estimate=pl.CostEstimate(
            flops=4 * rows * width * inner, bytes_accessed=4 * width * inner, transcendentals=0
        ),
    )(dact, gate_up, *after)


def tok_step(mask, whole, out):
    out[...] = jnp.dot(mask[...], whole[...], preferred_element_type=F32).astype(BF)


def tile_step(at, *refs):
    xs, ds, outs, xall, dall = refs[:4], refs[4:8], refs[-6:-2], refs[-2], refs[-1]
    rows, inner = ds[0].shape[1:]
    for p in range(4):
        part = slice(p * rows, p * rows + rows)
        xall[part, :] = xs[p][...]
        for h in range(2):
            dall[part, h * inner : h * inner + inner] = ds[p][h]
    for j in (1, 2, 3, 0):
        other = lax.rem(at[2] + j, 4)
        for b in range(2):
            got = rows_dot(xall[:, aligned(b * 4 + other, 128)], dall[...])
            outs[j][b * 128 : b * 128 + 128, :] = got.astype(outs[j].dtype)


def tile_call(at, xs, ds, after):
    rows, part = xs[0].shape
    wide = 2 * ds[0].shape[2]
    return call(
        tile_step,
        [shape(256, wide, F32)] + [shape(256, wide)] * 3,
        9,
        [pltpu.VMEM((4 * rows, part), BF), pltpu.VMEM((4 * rows, wide), BF)],
        flops=8 * rows * part * wide,
        moved=8 * rows * (part + wide),
        after=len(after),
        limit=12,
    )(at, *xs, *ds, *after)


def down_step(at, both, *rest):
    outs, gall, hall, total = rest[-7:-3], rest[-3], rest[-2], rest[-1]
    rows, part, inner = both.shape[1], gall.shape[1], hall.shape[1]
    for i in range(4):
        gall[i * rows : i * rows + rows, :] = both[i, :, :part]
        hall[i * rows : i * rows + rows, :] = both[i, :, part:]
    for b in range(inner // 128):
        cols = slice(b * 128, b * 128 + 128)
        total[cols, :] = rows_dot(hall[:, cols], gall[...])
    for j in (1, 2, 3, 0):
        other = lax.rem(at[1] + j, 4)
        for b in range(2):
            outs[j][b * 96 : b * 96 + 96, :] = total[aligned(b * 4 + other, 96), :].astype(outs[j].dtype)


def down_call(at, both, part, after):
    rows, inner = both.shape[1], both.shape[2] - part
    return call(
        down_step,
        [shape(192, part, F32)] + [shape(192, part)] * 3,
        2,
        [
            pltpu.VMEM((4 * rows, part), BF),
            pltpu.VMEM((4 * rows, inner), BF),
            pltpu.VMEM((inner, part), F32),
        ],
        flops=8 * rows * part * inner,
        moved=8 * rows * (part + inner),
        after=len(after),
        limit=16,
    )(at, both, *after)


def sum_step(at, *refs):
    parts, keep, send = refs[:4], refs[-2], refs[-1]
    half = keep.shape[0]

    def part(i):
        rows = aligned(i, half)
        return sum((r[rows, :].astype(F32) for r in parts[1:]), parts[0][rows, :])

    send[...] = part(1 - at[0]).astype(BF)
    keep[...] = part(at[0])


def sum_call(at, parts, after):
    rows, cols = parts[0].shape
    outs = [shape(rows // 2, cols, F32), shape(rows // 2, cols)]
    return call(sum_step, outs, 5, moved=10 * rows * cols, after=len(after))(at, *parts, *after)


def shards(tokens, cotangent, routes, gates, gate_up, down_proj):
    gate_up, down_proj = gate_up[0], down_proj[0]
    w, x, y = lax.axis_index("w"), lax.axis_index("x"), lax.axis_index("y")
    at = jnp.stack([w, x, y]).astype(jnp.int32)
    toks, width = tokens.shape
    inner = down_proj.shape[0]
    experts = jnp.arange(4, dtype=jnp.int32)
    matches = routes[:, :, None] == experts[None, None, :]
    member = jnp.any(matches, axis=1)
    weight = jnp.sum(jnp.where(matches, gates[:, :, None], F32(0.0)), axis=1)
    position = jnp.cumsum(member.astype(jnp.int32), axis=0) - 1
    select = member[:, :, None] & (
        position[:, :, None] == jnp.arange(CAP, dtype=jnp.int32)[None, None, :]
    )
    mask = select.astype(BF).reshape(toks, 4 * CAP)
    slot_gate = jnp.sum(jnp.where(select, weight[:, :, None], F32(0.0)), axis=0).reshape(4 * CAP, 1)
    send_x = rows_dot(mask, tokens).astype(BF).reshape(4, CAP, width)
    send_g = (rows_dot(mask, cotangent) * slot_gate).astype(BF).reshape(4, CAP, width)
    rows = 4 * CAP
    X = swap_expert(send_x).reshape(rows, width)
    G = swap_expert(send_g).reshape(rows, width)

    part = width // 4
    packed = call(pack_x, [shape(rows, part)] * 4, 2, moved=4 * rows * width)(at, X)
    xa = [shift(packed[j], "x", j) for j in range(4)]
    hidden, slope, silu = act_call(X, gate_up, inner)
    sent = call(
        pack_g,
        [jax.ShapeDtypeStruct((4, rows, part + inner), BF)],
        2,
        moved=4 * rows * width,
        scalars=0,
        after=3,
    )(G, hidden, *xa[1:])[0]
    both = lax.all_to_all(sent, "y", split_axis=0, concat_axis=0, tiled=True)
    dact = dh_call(G, down_proj, slope, silu, [sent])
    da = [shift(dact, "x", j) for j in range(4)]
    parts = tile_call(at, xa, da, [])
    gate = [parts[0]] + [shift(parts[j], "y", j) for j in (1, 2, 3)]
    back = back_call(dact, gate_up, [da[2]])
    arrived = swap_expert(back.reshape(4, CAP, width)).reshape(rows, width)
    token_grad = call(
        tok_step,
        [shape(toks, width)],
        2,
        flops=2 * toks * rows * width,
        moved=2 * (rows + toks) * width,
        scalars=0,
    )(mask, arrived)[0]
    parts = down_call(at, both, part, [])
    down = [parts[0]] + [shift(parts[j], "x", j) for j in (1, 2, 3)]

    keep, send = sum_call(at, down, [])
    down_grad = (keep + swap_w(send).astype(F32)).astype(BF).reshape(4, 24, part)
    down_grad = lax.all_to_all(down_grad, "y", split_axis=0, concat_axis=0, tiled=True)
    down_grad = jnp.concatenate([down_grad[i] for i in range(4)], axis=1)

    keep, send = sum_call(at, gate, [token_grad])
    gate_up_grad = (keep + swap_w(send).astype(F32)).astype(BF)
    return token_grad, gate_up_grad[None], down_grad[None]


def solution(mesh):
    fine = Mesh(mesh.devices.reshape(2, 4, 4, 2, 2), AXES)
    rows, expert, dp = P(AXES, None), ("v", "c"), ("w", "x", "y")
    in_specs = (rows, rows, rows, rows, P(expert, None, None), P(expert, None, None))
    out_specs = (rows, P(expert, dp, None), P(expert, dp, None))
    return jax.shard_map(
        shards, mesh=fine, in_specs=in_specs, out_specs=out_specs, check_vma=False
    )
```

time: 199 us -> 179 us (0.90)
  waiting for transfers between devices: 81.8 us -> 67.5 us
  starting transfers between devices: 56.4 us -> 46.8 us
  local copies, waits for them, and re-layouts: 15.3 us -> 23 us
  Pallas kernels: 38.5 us -> 31 us
  matrix products: 1.24 us -> 4.81 us
    all_to_all x0 -> x5, starting transfers between devices: none -> 22.8 us  [the longest x3 14.2 us: swap_expert(): lax.all_to_all(a, ('v', 'c'), split_axis=0, concat_axis=0, tiled=True)]
    all_to_all x0 -> x5, waiting for transfers between devices: none -> 22.5 us  [the longest x3 20.8 us: swap_expert(): lax.all_to_all(a, ('v', 'c'), split_axis=0, concat_axis=0, tiled=True)]
    ppermute x27 -> x12, starting transfers between devices: 40.8 us -> 21.8 us  [shift(): return lax.ppermute(a, axis, [(i, (i + j) % 4) for i in range(4)])]
    ppermute x27 -> x12, waiting for transfers between devices: 59.8 us -> 41.2 us  [shift(): return lax.ppermute(a, axis, [(i, (i + j) % 4) for i in range(4)])]
    ppermute x9 -> x0, waiting for transfers between devices: 17.4 us -> none  [swap_expert(): return lax.ppermute(a, ('v', 'c'), [(i, i ^ k) for i in range(4)])]
    ppermute x9 -> x0, starting transfers between devices: 12.5 us -> none  [swap_expert(): return lax.ppermute(a, ('v', 'c'), [(i, i ^ k) for i in range(4)])]
    unnamed x53 -> x54, local copies, waits for them, and re-layouts: 11.9 us -> 22.4 us
    dot_general x2, matrix products: 1.24 us -> 4.81 us  [rows_dot(): lax.dot_general(a, b, (((0,), (0,)), ((), ())), preferred_element_type=F32)]
  transfers between devices with their start and end apart: 39 -> 19, of which waited for: 16 -> 9; matrix products, arithmetic and copies ran while one was open for 2% -> 3% of each run, Pallas kernels for 17% -> 16%
where the time goes in v1:
time: 179 us; the launch traced here: 178 us
  waiting for transfers between devices  67.5 us (38%)
  starting transfers between devices  46.8 us (26%)
  Pallas kernels  31 us (17%)
  local copies, waits for them, and re-layouts  23 us (13%)
  matrix products  4.81 us (3%)
  other arithmetic  4.37 us (2%)
    ppermute x12, waiting for transfers between devices, shift(): return lax.ppermute(a, axis, [(i, (i + j) % 4) for i in range(4)])  41.2 us
    unnamed x54, local copies, waits for them, and re-layouts  22.4 us
    ppermute x12, starting transfers between devices, shift(): return lax.ppermute(a, axis, [(i, (i + j) % 4) for i in range(4)])  21.8 us
    all_to_all x3, waiting for transfers between devices, swap_expert(): lax.all_to_all(a, ('v', 'c'), split_axis=0, concat_axis=0, tiled=True)  20.8 us
    all_to_all x3, starting transfers between devices, swap_expert(): lax.all_to_all(a, ('v', 'c'), split_axis=0, concat_axis=0, tiled=True)  14.2 us
    pallas_call x1, Pallas kernels, back_call(): pl.pallas_call(back_step, grid=(width // step,), in_specs=[pl.BlockSpec((...  6.16 us
    pallas_call x1, Pallas kernels, tile_call(): call(tile_step, [shape(256, wide, F32)] + [shape(256, wide)] * 3, 9, [plt...  5.2 us
    dot_general x2, matrix products, rows_dot(): lax.dot_general(a, b, (((0,), (0,)), ((), ())), preferred_element_type=F32)  4.81 us
  transfers between devices with their start and end apart: 19, of which 9 were waited for; matrix products, arithmetic and copies ran while one was open for 3% of the time, Pallas kernels for 16%

profile of v1, /device:TPU:0, one launch (start us, length us, event | category | flops | bytes accessed | tf_op | source)
XLA Modules:
  0.0 178.3 jit_solution(15779514956393239304)
XLA Ops:
  2.2 1.8 convolution_convert_fusion
  4.0 5.4 %all-to-all-start.1 = ((bf16[4,48,4096]{2,1,0:T(8,128)(2,1)}), bf16[4,48,4096]{2,1,0:T(8,128)(2,1)S(1)}, u32[]{:S(2)}, u32[]{:S(2)}) async-start(bf16[4,48,4096]{2,1,0:T(8,128)(2,1)} %bitcast.38), calls=%async_computation.1 | async-start | bytes 3145728 | tf_op jit(solution)/shard_map/all_to_all | solution.py:20
  9.6 3.0 %fusion = bf16[192,4096]{1,0:T(8,128)(2,1)} fusion(pred[128,192]{1,0:T(32,128)(4,1)S(1)} %get-tuple-element.42, bf16[128,4096]{1,0:T(8,128)(2,1)} %param.7, f32[192]{0:T(256)S(1)} %mul.10), kind=kOutput, calls=%fused_computation.1 | convolution fusion | flops 202899456 | bytes 2646784 | tf_op jit(solution)/shard_map/dot_general | solution.py:34
  12.6 18.3 %all-to-all-done.1 = bf16[4,48,4096]{2,1,0:T(8,128)(2,1)S(1)} async-done(((bf16[4,48,4096]{2,1,0:T(8,128)(2,1)}), bf16[4,48,4096]{2,1,0:T(8,128)(2,1)S(1)}, u32[]{:S(2)}, u32[]{:S(2)}) %all-to-all-start.1) | async-done | bytes 1572896 | tf_op jit(solution)/shard_map/all_to_all | solution.py:20
  30.9 4.4 %all-to-all-start = ((bf16[4,48,4096]{2,1,0:T(8,128)(2,1)}), bf16[4,48,4096]{2,1,0:T(8,128)(2,1)}, u32[]{:S(2)}, u32[]{:S(2)}) async-start(bf16[4,48,4096]{2,1,0:T(8,128)(2,1)} %bitcast.37), calls=%async_computation | async-start | bytes 3145728 | tf_op jit(solution)/shard_map/all_to_all | solution.py:20
  35.4 1.7 shard_map.86
  39.3 2.7 %collective-permute-start.1 = (bf16[192,1024]{1,0:T(8,128)(2,1)}, bf16[192,1024]{1,0:T(8,128)(2,1)S(1)}, u32[]{:S(2)}, u32[]{:S(2)}) collective-permute-start(bf16[192,1024]{1,0:T(8,128)(2,1)} %get-tuple-element.26), channel_id=1, source_target_pairs={{0,32},{16,48},{32,0},{48,16},{1,33},{17,49},{33,1},{49,17},{2,34}... | collective-permute-start | bytes 1179656 | tf_op jit(solution)/shard_map/ppermute | solution.py:26
  43.5 4.6 %copy-done.1 = bf16[1,4096,1536]{2,1,0:T(8,128)(2,1)S(1)} copy-done((bf16[1,4096,1536]{2,1,0:T(8,128)(2,1)S(1)}, bf16[1,4096,1536]{2,1,0:T(8,128)(2,1)}, u32[]{:S(2)}) %copy-start.1) | copy-done | bytes 12582936
  48.1 4.1 %shard_map.85 = (bf16[192,768]{1,0:T(8,128)(2,1)S(1)}, f32[192,768]{1,0:T(8,128)S(1)}, f32[192,768]{1,0:T(8,128)S(1)}) custom-call(bf16[192,4096]{1,0:T(8,128)(2,1)S(1)} %bitcast.34, bf16[4096,1536]{1,0:T(8,128)(2,1)S(1)} %bitcast.30, bf16[4096,1536]{1,0:T(8,128)(2,1)S(1)} %bitcast.31), custom_call_target="tpu_custom_call" | custom-call | flops 2415919104 | bytes 12582912 | tf_op jit(solution)/shard_map/pallas_call | solution.py:90
  54.6 2.4 %all-to-all-done = bf16[4,48,4096]{2,1,0:T(8,128)(2,1)} async-done(((bf16[4,48,4096]{2,1,0:T(8,128)(2,1)}), bf16[4,48,4096]{2,1,0:T(8,128)(2,1)}, u32[]{:S(2)}, u32[]{:S(2)}) %all-to-all-start) | async-done | bytes 1572896 | tf_op jit(solution)/shard_map/all_to_all | solution.py:20
  57.0 3.2 %collective-permute-done.1.rest_1_.refs_2_ = bf16[192,1024]{1,0:T(8,128)(2,1)S(1)} collective-permute-done((bf16[192,1024]{1,0:T(8,128)(2,1)}, bf16[192,1024]{1,0:T(8,128)(2,1)S(1)}, u32[]{:S(2)}, u32[]{:S(2)}) %collective-permute-start.1) | collective-permute-done | bytes 393248 | tf_op jit(solution)/shard_map/ppermute | solution.py:26
  64.4 4.7 %all-to-all-start.3 = ((bf16[4,192,1792]{2,1,0:T(8,128)(2,1)}), bf16[4,192,1792]{2,1,0:T(8,128)(2,1)}, u32[]{:S(2)}, u32[]{:S(2)}) async-start(bf16[4,192,1792]{2,1,0:T(8,128)(2,1)} %copy-done.3), calls=%async_computation.3 | async-start | bytes 5505024 | tf_op jit(solution)/shard_map/all_to_all | solution.py:281
  69.2 1.8 %copy-done.4 = bf16[4,192,1792]{2,1,0:T(8,128)(2,1)S(1)} copy-done((bf16[4,192,1792]{2,1,0:T(8,128)(2,1)S(1)}, bf16[4,192,1792]{2,1,0:T(8,128)(2,1)}, u32[]{:S(2)}) %copy-start.4) | copy-done | bytes 2752536
  71.0 2.8 %copy-done.5 = bf16[1,768,4096]{2,1,0:T(8,128)(2,1)S(1)} copy-done((bf16[1,768,4096]{2,1,0:T(8,128)(2,1)S(1)}, bf16[1,768,4096]{2,1,0:T(8,128)(2,1)}, u32[]{:S(2)}) %copy-start.5) | copy-done | bytes 6291480
  73.8 4.1 %shard_map.88.dact.refs_4_ = bf16[2,192,768]{2,1,0:T(8,128)(2,1)S(1)} custom-call(bf16[192,4096]{1,0:T(8,128)(2,1)} %bitcast.3.whole, bf16[768,4096]{1,0:T(8,128)(2,1)S(1)} %bitcast.35, f32[192,768]{1,0:T(8,128)S(1)} %copy-done.10, f32[192,768]{1,0:T(8,128)S(1)} %copy-done.12, bf16[4,192,1792]{2,1,0:T(8,128)(2,1)S(1)} %copy-done.4), custom_call_target="tpu_custom_call" | custom-call | flops 1207959552 | bytes 6291456 | tf_op jit(solution)/shard_map/pallas_call | solution.py:119
  77.9 2.7 %collective-permute-start.3 = (bf16[2,192,768]{2,1,0:T(8,128)(2,1)S(1)}, bf16[2,192,768]{2,1,0:T(8,128)(2,1)S(1)}, u32[]{:S(2)}, u32[]{:S(2)}) collective-permute-start(bf16[2,192,768]{2,1,0:T(8,128)(2,1)S(1)} %shard_map.88.dact.refs_4_), channel_id=1, source_target_pairs={{0,32},{16,48},{32,0},{48,16},{1,33},{17,49},{33,1},{49,17},{2,34}... | collective-permute-start | bytes 1769480 | tf_op jit(solution)/shard_map/ppermute | solution.py:26
  82.6 13.1 %collective-permute-done.3.rest_0_.refs_6_ = bf16[2,192,768]{2,1,0:T(8,128)(2,1)S(1)} collective-permute-done((bf16[2,192,768]{2,1,0:T(8,128)(2,1)S(1)}, bf16[2,192,768]{2,1,0:T(8,128)(2,1)S(1)}, u32[]{:S(2)}, u32[]{:S(2)}) %collective-permute-start.3) | collective-permute-done | bytes 589856 | tf_op jit(solution)/shard_map/ppermute | solution.py:26
  95.8 4.6 %copy-done.2 = bf16[1,4096,1536]{2,1,0:T(8,128)(2,1)S(1)} copy-done((bf16[1,4096,1536]{2,1,0:T(8,128)(2,1)S(1)}, bf16[1,4096,1536]{2,1,0:T(8,128)(2,1)}, u32[]{:S(2)}) %copy-start.2) | copy-done | bytes 12582936
  100.3 6.2 %shard_map.89 = bf16[192,4096]{1,0:T(8,128)(2,1)} custom-call(bf16[2,192,768]{2,1,0:T(8,128)(2,1)S(1)} %shard_map.88.dact.refs_4_, bf16[4096,1536]{1,0:T(8,128)(2,1)S(1)} %bitcast.32, bf16[2,192,768]{2,1,0:T(8,128)(2,1)S(1)} %collective-permute-done.3.rest_0_.refs_6_), custom_call_target="tpu_custom_call" | custom-call | flops 2415919104 | bytes 12582912 | tf_op jit(solution)/shard_map/pallas_call | solution.py:147
  107.3 4.5 %all-to-all-start.2 = ((bf16[4,48,4096]{2,1,0:T(8,128)(2,1)}), bf16[4,48,4096]{2,1,0:T(8,128)(2,1)S(1)}, u32[]{:S(2)}, u32[]{:S(2)}) async-start(bf16[4,48,4096]{2,1,0:T(8,128)(2,1)} %bitcast.11), calls=%async_computation.2 | async-start | bytes 3145728 | tf_op jit(solution)/shard_map/all_to_all | solution.py:20
  111.8 3.7 %shard_map.93 = (f32[192,1024]{1,0:T(8,128)S(1)}, bf16[192,1024]{1,0:T(8,128)(2,1)S(1)}, bf16[192,1024]{1,0:T(8,128)(2,1)S(1)}, bf16[192,1024]{1,0:T(8,128)(2,1)S(1)}) custom-call(s32[3]{0:T(128)S(1)} %pad_add_fusion.at, bf16[4,192,1792]{2,1,0:T(8,128)(2,1)} %all-to-all-done.3.both), custom_call_target="tpu_custom_call" | custom-call | flops 1207959552 | bytes 2752512 | tf_op jit(solution)/shard_map/pallas_call | solution.py:213
  116.9 5.2 %shard_map.91 = (f32[256,1536]{1,0:T(8,128)S(1)}, bf16[256,1536]{1,0:T(8,128)(2,1)}, bf16[256,1536]{1,0:T(8,128)(2,1)}, bf16[256,1536]{1,0:T(8,128)(2,1)}) custom-call(s32[3]{0:T(128)S(1)} %pad_add_fusion.at, bf16[192,1024]{1,0:T(8,128)(2,1)S(1)} %copy-done.24, bf16[192,1024]{1,0:T(8,128)(2,1)S(1)} %copy-done.16, bf16[192,1024]{1,0:T(8,128)(2,1)S(1)} %copy-done.18, ...), custom_call_target="tpu_custom_call" | custom-call | flops 2415919104 | bytes 3932160 | tf_op jit(solution)/shard_map/pallas_call | solution.py:184
  122.1 2.0 %collective-permute-start.6 = (bf16[256,1536]{1,0:T(8,128)(2,1)}, bf16[256,1536]{1,0:T(8,128)(2,1)S(1)}, u32[]{:S(2)}, u32[]{:S(2)}) collective-permute-start(bf16[256,1536]{1,0:T(8,128)(2,1)} %get-tuple-element.30), channel_id=1, source_target_pairs={{0,4},{4,8},{8,12},{12,0},{1,5},{5,9},{9,13},{13,1},{2,6},{6,10},{... | collective-permute-start | bytes 2359304 | tf_op jit(solution)/shard_map/ppermute | solution.py:26
  124.0 2.7 %collective-permute-start.7 = (bf16[256,1536]{1,0:T(8,128)(2,1)}, bf16[256,1536]{1,0:T(8,128)(2,1)}, u32[]{:S(2)}, u32[]{:S(2)}) collective-permute-start(bf16[256,1536]{1,0:T(8,128)(2,1)} %get-tuple-element.31), channel_id=1, source_target_pairs={{0,8},{4,12},{8,0},{12,4},{1,9},{5,13},{9,1},{13,5},{2,10},{6,14},... | collective-permute-start | bytes 2359304 | tf_op jit(solution)/shard_map/ppermute | solution.py:26
  128.2 2.4 %collective-permute-start.11 = (bf16[192,1024]{1,0:T(8,128)(2,1)S(1)}, bf16[192,1024]{1,0:T(8,128)(2,1)S(1)}, u32[]{:S(2)}, u32[]{:S(2)}) collective-permute-start(bf16[192,1024]{1,0:T(8,128)(2,1)S(1)} %get-tuple-element.37), channel_id=1, source_target_pairs={{0,32},{16,48},{32,0},{48,16},{1,33},{17,49},{33,1},{49,17},{2,34}... | collective-permute-start | bytes 1179656 | tf_op jit(solution)/shard_map/ppermute | solution.py:26
  132.1 7.9 %collective-permute-done.11.refs_2_ = bf16[192,1024]{1,0:T(8,128)(2,1)S(1)} collective-permute-done((bf16[192,1024]{1,0:T(8,128)(2,1)S(1)}, bf16[192,1024]{1,0:T(8,128)(2,1)S(1)}, u32[]{:S(2)}, u32[]{:S(2)}) %collective-permute-start.11) | collective-permute-done | bytes 393248 | tf_op jit(solution)/shard_map/ppermute | solution.py:26
  140.1 7.7 %collective-permute-done.12.refs_3_ = bf16[192,1024]{1,0:T(8,128)(2,1)S(1)} collective-permute-done((bf16[192,1024]{1,0:T(8,128)(2,1)S(1)}, bf16[192,1024]{1,0:T(8,128)(2,1)S(1)}, u32[]{:S(2)}, u32[]{:S(2)}) %collective-permute-start.12) | collective-permute-done | bytes 393248 | tf_op jit(solution)/shard_map/ppermute | solution.py:26
  152.3 9.2 %collective-permute-done.7.refs_2_ = bf16[256,1536]{1,0:T(8,128)(2,1)} collective-permute-done((bf16[256,1536]{1,0:T(8,128)(2,1)}, bf16[256,1536]{1,0:T(8,128)(2,1)}, u32[]{:S(2)}, u32[]{:S(2)}) %collective-permute-start.7) | collective-permute-done | bytes 786464 | tf_op jit(solution)/shard_map/ppermute | solution.py:26
  162.8 1.8 shard_map.92
  167.3 3.9 %all-to-all-start.4 = ((bf16[4,24,1024]{2,1,0:T(8,128)(2,1)}), bf16[4,24,1024]{2,1,0:T(8,128)(2,1)S(1)}, u32[]{:S(2)}, u32[]{:S(2)}) async-start(bf16[4,24,1024]{2,1,0:T(8,128)(2,1)} %bitcast.14), calls=%async_computation.4 | async-start | bytes 393216 | tf_op jit(solution)/shard_map/all_to_all | solution.py:301
  171.2 3.8 %collective-permute-done.9 = bf16[128,1536]{1,0:T(8,128)(2,1)S(1)} collective-permute-done((bf16[128,1536]{1,0:T(8,128)(2,1)S(1)}, bf16[128,1536]{1,0:T(8,128)(2,1)S(1)}, u32[]{:S(2)}, u32[]{:S(2)}) %collective-permute-start.9) | collective-permute-done | bytes 393248 | tf_op jit(solution)/shard_map/ppermute | solution.py:30
  175.8 1.7 all-to-all-done.4
  (93 shorter events, 29.5 us)
Async XLA Ops:
  4.0 5.4 %copy-start.25 = (s32[128,8]{0,1:T(8,128)S(1)}, s32[128,8]{0,1:T(8,128)}, u32[]{:S(2)}) copy-start(s32[128,8]{0,1:T(8,128)} %param.8) | copy-start | bytes 12292
  4.0 5.4 %copy-start.26 = (f32[128,8]{0,1:T(8,128)S(1)}, f32[128,8]{0,1:T(8,128)}, u32[]{:S(2)}) copy-start(f32[128,8]{0,1:T(8,128)} %param.9) | copy-start | bytes 12292
  4.0 26.9 %all-to-all-start.1 = ((bf16[4,48,4096]{2,1,0:T(8,128)(2,1)}), bf16[4,48,4096]{2,1,0:T(8,128)(2,1)S(1)}, u32[]{:S(2)}, u32[]{:S(2)}) async-start(bf16[4,48,4096]{2,1,0:T(8,128)(2,1)} %bitcast.38), calls=%async_computation.1 | async-start | bytes 3145728 | tf_op jit(solution)/shard_map/all_to_all | solution.py:20
  30.9 26.0 %all-to-all-start = ((bf16[4,48,4096]{2,1,0:T(8,128)(2,1)}), bf16[4,48,4096]{2,1,0:T(8,128)(2,1)}, u32[]{:S(2)}, u32[]{:S(2)}) async-start(bf16[4,48,4096]{2,1,0:T(8,128)(2,1)} %bitcast.37), calls=%async_computation | async-start | bytes 3145728 | tf_op jit(solution)/shard_map/all_to_all | solution.py:20
  37.9 19.1 %collective-permute-start = (bf16[192,1024]{1,0:T(8,128)(2,1)}, bf16[192,1024]{1,0:T(8,128)(2,1)S(1)}, u32[]{:S(2)}, u32[]{:S(2)}) collective-permute-start(bf16[192,1024]{1,0:T(8,128)(2,1)} %get-tuple-element.25), channel_id=1, source_target_pairs={{0,16},{16,32},{32,48},{48,0},{1,17},{17,33},{33,49},{49,1},{2,18}... | collective-permute-start | bytes 1179656 | tf_op jit(solution)/shard_map/ppermute | solution.py:26
  39.3 20.8 %collective-permute-start.1 = (bf16[192,1024]{1,0:T(8,128)(2,1)}, bf16[192,1024]{1,0:T(8,128)(2,1)S(1)}, u32[]{:S(2)}, u32[]{:S(2)}) collective-permute-start(bf16[192,1024]{1,0:T(8,128)(2,1)} %get-tuple-element.26), channel_id=1, source_target_pairs={{0,32},{16,48},{32,0},{48,16},{1,33},{17,49},{33,1},{49,17},{2,34}... | collective-permute-start | bytes 1179656 | tf_op jit(solution)/shard_map/ppermute | solution.py:26
  42.1 18.1 %collective-permute-start.2 = (bf16[192,1024]{1,0:T(8,128)(2,1)}, bf16[192,1024]{1,0:T(8,128)(2,1)}, u32[]{:S(2)}, u32[]{:S(2)}) collective-permute-start(bf16[192,1024]{1,0:T(8,128)(2,1)} %get-tuple-element.27), channel_id=1, source_target_pairs={{0,48},{16,0},{32,16},{48,32},{1,49},{17,1},{33,17},{49,33},{2,50}... | collective-permute-start | bytes 1179656 | tf_op jit(solution)/shard_map/ppermute | solution.py:26
  43.5 4.6 %copy-start.1 = (bf16[1,4096,1536]{2,1,0:T(8,128)(2,1)S(1)}, bf16[1,4096,1536]{2,1,0:T(8,128)(2,1)}, u32[]{:S(2)}) copy-start(bf16[1,4096,1536]{2,1,0:T(8,128)(2,1)} %param.10) | copy-start | bytes 37748740
  57.0 5.9 %copy-start.15 = (bf16[192,1024]{1,0:T(8,128)(2,1)}, bf16[192,1024]{1,0:T(8,128)(2,1)S(1)}, u32[]{:S(2)}) copy-start(bf16[192,1024]{1,0:T(8,128)(2,1)S(1)} %collective-permute-done.rest_0_.refs_1_) | copy-start | bytes 1179652
  64.4 4.7 %copy-start.10 = (f32[192,768]{1,0:T(8,128)S(1)}, f32[192,768]{1,0:T(8,128)}, u32[]{:S(2)}) copy-start(f32[192,768]{1,0:T(8,128)} %copy-done.9) | copy-start | bytes 1769476
  64.4 4.7 %copy-start.12 = (f32[192,768]{1,0:T(8,128)S(1)}, f32[192,768]{1,0:T(8,128)}, u32[]{:S(2)}) copy-start(f32[192,768]{1,0:T(8,128)} %copy-done.11) | copy-start | bytes 1769476
  64.4 42.9 %all-to-all-start.3 = ((bf16[4,192,1792]{2,1,0:T(8,128)(2,1)}), bf16[4,192,1792]{2,1,0:T(8,128)(2,1)}, u32[]{:S(2)}, u32[]{:S(2)}) async-start(bf16[4,192,1792]{2,1,0:T(8,128)(2,1)} %copy-done.3), calls=%async_computation.3 | async-start | bytes 5505024 | tf_op jit(solution)/shard_map/all_to_all | solution.py:281
  77.9 17.9 %collective-permute-start.3 = (bf16[2,192,768]{2,1,0:T(8,128)(2,1)S(1)}, bf16[2,192,768]{2,1,0:T(8,128)(2,1)S(1)}, u32[]{:S(2)}, u32[]{:S(2)}) collective-permute-start(bf16[2,192,768]{2,1,0:T(8,128)(2,1)S(1)} %shard_map.88.dact.refs_4_), channel_id=1, source_target_pairs={{0,32},{16,48},{32,0},{48,16},{1,33},{17,49},{33,1},{49,17},{2,34}... | collective-permute-start | bytes 1769480 | tf_op jit(solution)/shard_map/ppermute | solution.py:26
  80.6 36.2 %collective-permute-start.5 = (bf16[2,192,768]{2,1,0:T(8,128)(2,1)S(1)}, bf16[2,192,768]{2,1,0:T(8,128)(2,1)}, u32[]{:S(2)}, u32[]{:S(2)}) collective-permute-start(bf16[2,192,768]{2,1,0:T(8,128)(2,1)S(1)} %shard_map.88.dact.refs_4_), channel_id=1, source_target_pairs={{0,48},{16,0},{32,16},{48,32},{1,49},{17,1},{33,17},{49,33},{2,50}... | collective-permute-start | bytes 1769480 | tf_op jit(solution)/shard_map/ppermute | solution.py:26
  81.9 34.9 %collective-permute-start.4 = (bf16[2,192,768]{2,1,0:T(8,128)(2,1)S(1)}, bf16[2,192,768]{2,1,0:T(8,128)(2,1)}, u32[]{:S(2)}, u32[]{:S(2)}) collective-permute-start(bf16[2,192,768]{2,1,0:T(8,128)(2,1)S(1)} %shard_map.88.dact.refs_4_), channel_id=1, source_target_pairs={{0,16},{16,32},{32,48},{48,0},{1,17},{17,33},{33,49},{49,1},{2,18}... | collective-permute-start | bytes 1769480 | tf_op jit(solution)/shard_map/ppermute | solution.py:26
  95.8 4.6 %copy-start.2 = (bf16[1,4096,1536]{2,1,0:T(8,128)(2,1)S(1)}, bf16[1,4096,1536]{2,1,0:T(8,128)(2,1)}, u32[]{:S(2)}) copy-start(bf16[1,4096,1536]{2,1,0:T(8,128)(2,1)} %param.10) | copy-start | bytes 37748740
  107.3 43.6 %all-to-all-start.2 = ((bf16[4,48,4096]{2,1,0:T(8,128)(2,1)}), bf16[4,48,4096]{2,1,0:T(8,128)(2,1)S(1)}, u32[]{:S(2)}, u32[]{:S(2)}) async-start(bf16[4,48,4096]{2,1,0:T(8,128)(2,1)} %bitcast.11), calls=%async_computation.2 | async-start | bytes 3145728 | tf_op jit(solution)/shard_map/all_to_all | solution.py:20
  111.8 5.1 %copy-start.14 = (bf16[2,192,768]{2,1,0:T(8,128)(2,1)S(1)}, bf16[2,192,768]{2,1,0:T(8,128)(2,1)}, u32[]{:S(2)}) copy-start(bf16[2,192,768]{2,1,0:T(8,128)(2,1)} %copy-done.13) | copy-start | bytes 1769476
  111.8 5.1 %copy-start.16 = (bf16[192,1024]{1,0:T(8,128)(2,1)S(1)}, bf16[192,1024]{1,0:T(8,128)(2,1)}, u32[]{:S(2)}) copy-start(bf16[192,1024]{1,0:T(8,128)(2,1)} %copy-done.15) | copy-start | bytes 1179652
  111.8 5.1 %copy-start.18 = (bf16[192,1024]{1,0:T(8,128)(2,1)S(1)}, bf16[192,1024]{1,0:T(8,128)(2,1)}, u32[]{:S(2)}) copy-start(bf16[192,1024]{1,0:T(8,128)(2,1)} %copy-done.17) | copy-start | bytes 1179652
  111.8 5.1 %copy-start.24 = (bf16[192,1024]{1,0:T(8,128)(2,1)S(1)}, bf16[192,1024]{1,0:T(8,128)(2,1)}, u32[]{:S(2)}) copy-start(bf16[192,1024]{1,0:T(8,128)(2,1)} %copy-done.23) | copy-start | bytes 1179652
  115.5 15.1 %collective-permute-start.10 = (bf16[192,1024]{1,0:T(8,128)(2,1)S(1)}, bf16[192,1024]{1,0:T(8,128)(2,1)S(1)}, u32[]{:S(2)}, u32[]{:S(2)}) collective-permute-start(bf16[192,1024]{1,0:T(8,128)(2,1)S(1)} %get-tuple-element.36), channel_id=1, source_target_pairs={{0,16},{16,32},{32,48},{48,0},{1,17},{17,33},{33,49},{49,1},{2,18}... | collective-permute-start | bytes 1179656 | tf_op jit(solution)/shard_map/ppermute | solution.py:26
  122.1 27.8 %copy-start.7 = (f32[256,1536]{1,0:T(8,128)}, f32[256,1536]{1,0:T(8,128)S(1)}, u32[]{:S(2)}) copy-start(f32[256,1536]{1,0:T(8,128)S(1)} %get-tuple-element.29.refs_0_) | copy-start | bytes 4718596
  122.1 30.3 %collective-permute-start.6 = (bf16[256,1536]{1,0:T(8,128)(2,1)}, bf16[256,1536]{1,0:T(8,128)(2,1)S(1)}, u32[]{:S(2)}, u32[]{:S(2)}) collective-permute-start(bf16[256,1536]{1,0:T(8,128)(2,1)} %get-tuple-element.30), channel_id=1, source_target_pairs={{0,4},{4,8},{8,12},{12,0},{1,5},{5,9},{9,13},{13,1},{2,6},{6,10},{... | collective-permute-start | bytes 2359304 | tf_op jit(solution)/shard_map/ppermute | solution.py:26
  124.0 37.5 %collective-permute-start.7 = (bf16[256,1536]{1,0:T(8,128)(2,1)}, bf16[256,1536]{1,0:T(8,128)(2,1)}, u32[]{:S(2)}, u32[]{:S(2)}) collective-permute-start(bf16[256,1536]{1,0:T(8,128)(2,1)} %get-tuple-element.31), channel_id=1, source_target_pairs={{0,8},{4,12},{8,0},{12,4},{1,9},{5,13},{9,1},{13,5},{2,10},{6,14},... | collective-permute-start | bytes 2359304 | tf_op jit(solution)/shard_map/ppermute | solution.py:26
  126.7 34.8 %collective-permute-start.8 = (bf16[256,1536]{1,0:T(8,128)(2,1)}, bf16[256,1536]{1,0:T(8,128)(2,1)}, u32[]{:S(2)}, u32[]{:S(2)}) collective-permute-start(bf16[256,1536]{1,0:T(8,128)(2,1)} %get-tuple-element.32), channel_id=1, source_target_pairs={{0,12},{4,0},{8,4},{12,8},{1,13},{5,1},{9,5},{13,9},{2,14},{6,2},{... | collective-permute-start | bytes 2359304 | tf_op jit(solution)/shard_map/ppermute | solution.py:26
  128.2 11.9 %collective-permute-start.11 = (bf16[192,1024]{1,0:T(8,128)(2,1)S(1)}, bf16[192,1024]{1,0:T(8,128)(2,1)S(1)}, u32[]{:S(2)}, u32[]{:S(2)}) collective-permute-start(bf16[192,1024]{1,0:T(8,128)(2,1)S(1)} %get-tuple-element.37), channel_id=1, source_target_pairs={{0,32},{16,48},{32,0},{48,16},{1,33},{17,49},{33,1},{49,17},{2,34}... | collective-permute-start | bytes 1179656 | tf_op jit(solution)/shard_map/ppermute | solution.py:26
  130.5 17.3 %collective-permute-start.12 = (bf16[192,1024]{1,0:T(8,128)(2,1)S(1)}, bf16[192,1024]{1,0:T(8,128)(2,1)S(1)}, u32[]{:S(2)}, u32[]{:S(2)}) collective-permute-start(bf16[192,1024]{1,0:T(8,128)(2,1)S(1)} %get-tuple-element.38), channel_id=1, source_target_pairs={{0,48},{16,0},{32,16},{48,32},{1,49},{17,1},{33,17},{49,33},{2,50}... | collective-permute-start | bytes 1179656 | tf_op jit(solution)/shard_map/ppermute | solution.py:26
  149.9 15.8 %collective-permute-start.13 = (bf16[96,1024]{1,0:T(8,128)(2,1)}, bf16[96,1024]{1,0:T(8,128)(2,1)}, u32[]{:S(2)}, u32[]{:S(2)}) collective-permute-start(bf16[96,1024]{1,0:T(8,128)(2,1)} %get-tuple-element.40), channel_id=1, source_target_pairs={{0,64},{64,0},{1,65},{65,1},{2,66},{66,2},{3,67},{67,3},{4,68},{68... | collective-permute-start | bytes 589832 | tf_op jit(solution)/shard_map/ppermute | solution.py:30
  150.9 10.6 %copy-start.8 = (f32[256,1536]{1,0:T(8,128)S(1)}, f32[256,1536]{1,0:T(8,128)}, u32[]{:S(2)}) copy-start(f32[256,1536]{1,0:T(8,128)} %copy-done.7) | copy-start | bytes 4718596
  164.5 10.5 %collective-permute-start.9 = (bf16[128,1536]{1,0:T(8,128)(2,1)S(1)}, bf16[128,1536]{1,0:T(8,128)(2,1)S(1)}, u32[]{:S(2)}, u32[]{:S(2)}) collective-permute-start(bf16[128,1536]{1,0:T(8,128)(2,1)S(1)} %get-tuple-element.34), channel_id=1, source_target_pairs={{0,64},{64,0},{1,65},{65,1},{2,66},{66,2},{3,67},{67,3},{4,68},{68... | collective-permute-start | bytes 1179656 | tf_op jit(solution)/shard_map/ppermute | solution.py:30
  167.3 10.3 %all-to-all-start.4 = ((bf16[4,24,1024]{2,1,0:T(8,128)(2,1)}), bf16[4,24,1024]{2,1,0:T(8,128)(2,1)S(1)}, u32[]{:S(2)}, u32[]{:S(2)}) async-start(bf16[4,24,1024]{2,1,0:T(8,128)(2,1)} %bitcast.14), calls=%async_computation.4 | async-start | bytes 393216 | tf_op jit(solution)/shard_map/all_to_all | solution.py:301
  (14 other events, 20.4 us)

commit v2 on v1

--- a/solution.py
+++ b/solution.py
@@ -16,8 +16,8 @@
 MB = 1024 * 1024
 
 
-def swap_expert(a):
-    return lax.all_to_all(a, ("v", "c"), split_axis=0, concat_axis=0, tiled=True)
+def swap_expert(a, k):
+    return lax.ppermute(a, ("v", "c"), [(i, i ^ k) for i in range(4)])
 
 
 def shift(a, axis, j):
@@ -58,17 +58,22 @@
     return pl.ds(pl.multiple_of(i * size, size), size)
 
 
-def pack_x(at, whole, *outs):
-    for j in range(4):
-        for b in range(2):
-            cols = aligned(b * 4 + lax.rem(at[1] + j, 4), 512)
-            outs[j][:, b * 512 : b * 512 + 512] = whole[:, cols]
-
-
-def pack_g(whole, hidden, *rest):
-    out, part = rest[-1], whole.shape[1] // 4
+def pack_x(at, x0, x1, x2, x3, *outs):
+    whole = outs[4]
+    for k, piece in enumerate((x0, x1, x2, x3)):
+        rows = slice(k * CAP, k * CAP + CAP)
+        whole[rows, :] = piece[...]
+        for j in range(4):
+            for b in range(2):
+                cols = aligned(b * 4 + lax.rem(at[1] + j, 4), 512)
+                outs[j][rows, b * 512 : b * 512 + 512] = piece[:, cols]
+
+
+def pack_g(g0, g1, g2, g3, hidden, *rest):
+    out, part = rest[-1], g0.shape[1] // 4
     for i in range(4):
-        out[i, :, :part] = whole[:, i * part : i * part + part]
+        for k, piece in enumerate((g0, g1, g2, g3)):
+            out[i, k * CAP : k * CAP + CAP, :part] = piece[:, i * part : i * part + part]
         out[i, :, part:] = hidden[...]
 
 
@@ -97,21 +102,27 @@
         ],
         out_specs=[out, out, out],
         out_shape=[shape(rows, inner), shape(rows, inner, F32), shape(rows, inner, F32)],
-        compiler_params=pltpu.CompilerParams(vmem_limit_bytes=16 * MB),
+        compiler_params=pltpu.CompilerParams(vmem_limit_bytes=48 * MB),
         cost_estimate=pl.CostEstimate(
             flops=4 * rows * width * inner, bytes_accessed=4 * width * inner, transcendentals=0
         ),
     )(X, gate_up, gate_up)
 
 
-def dh_step(whole, wd, slope, silu, *rest):
-    dact = rest[-1]
+def dh_step(g0, g1, g2, g3, wd, slope, silu, *rest):
+    dact, whole = rest[-2:]
+
+    @pl.when(pl.program_id(0) == 0)
+    def _():
+        for k, piece in enumerate((g0, g1, g2, g3)):
+            whole[k * CAP : k * CAP + CAP, :] = piece[...]
+
     dh = wide_dot(whole[...], wd[...])
     dact[0] = (dh * slope[...]).astype(BF)
     dact[1] = (dh * silu[...]).astype(BF)
 
 
-def dh_call(G, down_proj, slope, silu, after):
+def dh_call(gs, down_proj, slope, silu, after):
     inner, width = down_proj.shape
     rows = slope.shape[0]
     step = 256
@@ -119,47 +130,48 @@
     return pl.pallas_call(
         dh_step,
         grid=(inner // step,),
-        in_specs=[
-            pl.BlockSpec((rows, width), lambda i: (0, 0)),
-            pl.BlockSpec((step, width), lambda i: (i, 0)),
-            part,
-            part,
-        ]
+        in_specs=[pl.BlockSpec((CAP, width), lambda i: (0, 0))] * 4
+        + [pl.BlockSpec((step, width), lambda i: (i, 0)), part, part]
         + [pl.BlockSpec(memory_space=pl.ANY)] * len(after),
         out_specs=pl.BlockSpec((2, rows, step), lambda i: (0, 0, i)),
         out_shape=jax.ShapeDtypeStruct((2, rows, inner), BF),
-        compiler_params=pltpu.CompilerParams(vmem_limit_bytes=16 * MB),
+        scratch_shapes=[pltpu.VMEM((rows, width), BF)],
+        compiler_params=pltpu.CompilerParams(vmem_limit_bytes=48 * MB),
         cost_estimate=pl.CostEstimate(
             flops=2 * rows * width * inner, bytes_accessed=2 * width * inner, transcendentals=0
         ),
-    )(G, down_proj, slope, silu, *after)
-
-
-def back_step(dact, wt, *rest):
+    )(*gs, down_proj, slope, silu, *after)
+
+
+def back_step(at, dact, wt, *rest):
     out, inner = rest[-1], dact.shape[2]
-    out[...] = (wide_dot(dact[0], wt[:, :inner]) + wide_dot(dact[1], wt[:, inner:])).astype(BF)
-
-
-def back_call(dact, gate_up, after):
+    got = wide_dot(dact[0], wt[:, :inner]) + wide_dot(dact[1], wt[:, inner:])
+    for k in range(4):
+        out[jnp.bitwise_xor(at[3], k)] = got[k * CAP : k * CAP + CAP].astype(BF)
+
+
+def back_call(at, dact, gate_up, after):
     rows, inner = dact.shape[1:]
     width = gate_up.shape[0]
     step = 512
     return pl.pallas_call(
         back_step,
         grid=(width // step,),
-        in_specs=[pl.BlockSpec((2, rows, inner), lambda i: (0, 0, 0))]
+        in_specs=[SMEM, pl.BlockSpec((2, rows, inner), lambda i: (0, 0, 0))]
         + [pl.BlockSpec((step, 2 * inner), lambda i: (i, 0))]
         + [pl.BlockSpec(memory_space=pl.ANY)] * len(after),
-        out_specs=pl.BlockSpec((rows, step), lambda i: (0, i)),
-        out_shape=shape(rows, width),
-        compiler_params=pltpu.CompilerParams(vmem_limit_bytes=16 * MB),
+        out_specs=pl.BlockSpec((4, CAP, step), lambda i: (0, 0, i)),
+        out_shape=jax.ShapeDtypeStruct((4, CAP, width), BF),
+        compiler_params=pltpu.CompilerParams(vmem_limit_bytes=48 * MB),
         cost_estimate=pl.CostEstimate(
             flops=4 * rows * width * inner, bytes_accessed=4 * width * inner, transcendentals=0
         ),
-    )(dact, gate_up, *after)
-
-
-def tok_step(mask, whole, out):
+    )(at, dact, gate_up, *after)
+
+
+def tok_step(at, mask, arrived, out, whole):
+    for k in range(4):
+        whole[k * CAP : k * CAP + CAP, :] = arrived[jnp.bitwise_xor(at[3], k)]
     out[...] = jnp.dot(mask[...], whole[...], preferred_element_type=F32).astype(BF)
 
 
@@ -247,10 +259,11 @@
 def shards(tokens, cotangent, routes, gates, gate_up, down_proj):
     gate_up, down_proj = gate_up[0], down_proj[0]
     w, x, y = lax.axis_index("w"), lax.axis_index("x"), lax.axis_index("y")
-    at = jnp.stack([w, x, y]).astype(jnp.int32)
+    me = lax.axis_index(("v", "c"))
+    at = jnp.stack([w, x, y, me]).astype(jnp.int32)
     toks, width = tokens.shape
     inner = down_proj.shape[0]
-    experts = jnp.arange(4, dtype=jnp.int32)
+    experts = jnp.bitwise_xor(me, jnp.arange(4, dtype=jnp.int32))
     matches = routes[:, :, None] == experts[None, None, :]
     member = jnp.any(matches, axis=1)
     weight = jnp.sum(jnp.where(matches, gates[:, :, None], F32(0.0)), axis=1)
@@ -263,36 +276,38 @@
     send_x = rows_dot(mask, tokens).astype(BF).reshape(4, CAP, width)
     send_g = (rows_dot(mask, cotangent) * slot_gate).astype(BF).reshape(4, CAP, width)
     rows = 4 * CAP
-    X = swap_expert(send_x).reshape(rows, width)
-    G = swap_expert(send_g).reshape(rows, width)
+    xs = [send_x[0]] + [swap_expert(send_x[k], k) for k in (1, 2, 3)]
+    gs = [send_g[0]] + [swap_expert(send_g[k], k) for k in (1, 2, 3)]
 
     part = width // 4
-    packed = call(pack_x, [shape(rows, part)] * 4, 2, moved=4 * rows * width)(at, X)
+    packed = call(
+        pack_x, [shape(rows, part)] * 4 + [shape(rows, width)], 5, moved=4 * rows * width
+    )(at, *xs)
     xa = [shift(packed[j], "x", j) for j in range(4)]
-    hidden, slope, silu = act_call(X, gate_up, inner)
+    hidden, slope, silu = act_call(packed[4], gate_up, inner)
+    dact = dh_call(gs, down_proj, slope, silu, xa[1:])
+    da = [shift(dact, "x", j) for j in range(4)]
     sent = call(
         pack_g,
         [jax.ShapeDtypeStruct((4, rows, part + inner), BF)],
-        2,
+        5,
         moved=4 * rows * width,
         scalars=0,
-        after=3,
-    )(G, hidden, *xa[1:])[0]
+        after=1,
+    )(*gs, hidden, dact)[0]
     both = lax.all_to_all(sent, "y", split_axis=0, concat_axis=0, tiled=True)
-    dact = dh_call(G, down_proj, slope, silu, [sent])
-    da = [shift(dact, "x", j) for j in range(4)]
     parts = tile_call(at, xa, da, [])
     gate = [parts[0]] + [shift(parts[j], "y", j) for j in (1, 2, 3)]
-    back = back_call(dact, gate_up, [da[2]])
-    arrived = swap_expert(back.reshape(4, CAP, width)).reshape(rows, width)
+    back = back_call(at, dact, gate_up, [da[1], sent])
+    arrived = lax.all_to_all(back, ("v", "c"), split_axis=0, concat_axis=0, tiled=True)
     token_grad = call(
         tok_step,
         [shape(toks, width)],
-        2,
+        3,
+        [pltpu.VMEM((rows, width), BF)],
         flops=2 * toks * rows * width,
         moved=2 * (rows + toks) * width,
-        scalars=0,
-    )(mask, arrived)[0]
+    )(at, mask, arrived)[0]
     parts = down_call(at, both, part, [])
     down = [parts[0]] + [shift(parts[j], "x", j) for j in (1, 2, 3)]
 

time: 179 us -> 166 us (0.927)
  local copies, waits for them, and re-layouts: 23 us -> 10.8 us
  Pallas kernels: 31 us -> 36.5 us
  starting transfers between devices: 46.8 us -> 43.1 us
  matrix products: 4.81 us -> 2.45 us
    all_to_all x3 -> x1, waiting for transfers between devices: 20.8 us -> 0.01 us  [shards(): lax.all_to_all(back, ('v', 'c'), split_axis=0, concat_axis=0, tiled=True)]
    unnamed x54 -> x42, local copies, waits for them, and re-layouts: 22.4 us -> 8.11 us
    ppermute x0 -> x6, waiting for transfers between devices: none -> 13.8 us  [swap_expert(): return lax.ppermute(a, ('v', 'c'), [(i, i ^ k) for i in range(4)])]
    all_to_all x3 -> x1, starting transfers between devices: 14.2 us -> 5.18 us  [shards(): lax.all_to_all(back, ('v', 'c'), split_axis=0, concat_axis=0, tiled=True)]
    ppermute x0 -> x6, starting transfers between devices: none -> 7.65 us  [swap_expert(): return lax.ppermute(a, ('v', 'c'), [(i, i ^ k) for i in range(4)])]
    all_to_all x1, waiting for transfers between devices: 0.01 us -> 4.11 us  [shards(): both = lax.all_to_all(sent, 'y', split_axis=0, concat_axis=0, tiled=True)]
    pallas_call x5, Pallas kernels: 15 us -> 18.1 us  [the longest x1 9.47 us: back_call(): pl.pallas_call(back_step, grid=(width // step,), in_specs=[SMEM, pl.Block...]
    pallas_call x1, Pallas kernels: 4.06 us -> 6.64 us  [act_call(): pl.pallas_call(act_step, grid=(n,), in_specs=[pl.BlockSpec((rows, width),...]
  transfers between devices with their start and end apart: 19 -> 23, of which waited for: 9 -> 13; matrix products, arithmetic and copies ran while one was open for 3% -> 3% of each run, Pallas kernels for 16% -> 19%
where the time goes in v2:
time: 166 us; the launch traced here: 165 us
  waiting for transfers between devices  66.9 us (40%)
  starting transfers between devices  43.1 us (26%)
  Pallas kernels  36.5 us (22%)
  local copies, waits for them, and re-layouts  10.8 us (7%)
  other arithmetic  4.5 us (3%)
  matrix products  2.45 us (1%)
    ppermute x12, waiting for transfers between devices, shift(): return lax.ppermute(a, axis, [(i, (i + j) % 4) for i in range(4)])  43.4 us
    ppermute x12, starting transfers between devices, shift(): return lax.ppermute(a, axis, [(i, (i + j) % 4) for i in range(4)])  19.8 us
    ppermute x6, waiting for transfers between devices, swap_expert(): return lax.ppermute(a, ('v', 'c'), [(i, i ^ k) for i in range(4)])  13.8 us
    pallas_call x1, Pallas kernels, back_call(): pl.pallas_call(back_step, grid=(width // step,), in_specs=[SMEM, pl.Block...  9.47 us
    unnamed x42, local copies, waits for them, and re-layouts  8.11 us
    ppermute x6, starting transfers between devices, swap_expert(): return lax.ppermute(a, ('v', 'c'), [(i, i ^ k) for i in range(4)])  7.65 us
    pallas_call x1, Pallas kernels, act_call(): pl.pallas_call(act_step, grid=(n,), in_specs=[pl.BlockSpec((rows, width),...  6.64 us
    pallas_call x1, Pallas kernels, dh_call(): pl.pallas_call(dh_step, grid=(inner // step,), in_specs=[pl.BlockSpec((CA...  5.33 us
  transfers between devices with their start and end apart: 23, of which 13 were waited for; matrix products, arithmetic and copies ran while one was open for 3% of the time, Pallas kernels for 19%

profile of v2, /device:TPU:0, one launch (start us, length us, event | category | flops | bytes accessed | tf_op | source)
XLA Modules:
  0.0 165.2 jit_solution(17869505438749400266)
XLA Ops:
  4.0 4.0 %collective-permute-start.4 = (bf16[48,4096]{1,0:T(8,128)(2,1)}, bf16[48,4096]{1,0:T(8,128)(2,1)S(1)}, u32[]{:S(2)}, u32[]{:S(2)}) collective-permute-start(bf16[48,4096]{1,0:T(8,128)(2,1)} %get-tuple-element.46), channel_id=1, source_target_pairs={{0,2},{1,3},{2,0},{3,1},{4,6},{5,7},{6,4},{7,5},{8,10},{9,11},{10,... | collective-permute-start | bytes 1179656 | tf_op jit(solution)/shard_map/ppermute | solution.py:20
  8.4 1.8 %fusion = bf16[192,4096]{1,0:T(8,128)(2,1)S(1)} fusion(pred[128,192]{1,0:T(32,128)(4,1)S(1)} %get-tuple-element.44, bf16[128,4096]{1,0:T(8,128)(2,1)} %param.7, f32[192]{0:T(256)S(1)} %mul.14), kind=kOutput, calls=%fused_computation.1 | convolution fusion | flops 202899456 | bytes 2646784 | tf_op jit(solution)/shard_map/dot_general | solution.py:34
  11.4 3.4 %collective-permute-start.1 = (bf16[48,4096]{1,0:T(8,128)(2,1)}, bf16[48,4096]{1,0:T(8,128)(2,1)S(1)}, u32[]{:S(2)}, u32[]{:S(2)}) collective-permute-start(bf16[48,4096]{1,0:T(8,128)(2,1)} %get-tuple-element.50), channel_id=1, source_target_pairs={{0,2},{1,3},{2,0},{3,1},{4,6},{5,7},{6,4},{7,5},{8,10},{9,11},{10,... | collective-permute-start | bytes 1179656 | tf_op jit(solution)/shard_map/ppermute | solution.py:20
  14.9 3.2 %collective-permute-done.4.x2 = bf16[48,4096]{1,0:T(8,128)(2,1)S(1)} collective-permute-done((bf16[48,4096]{1,0:T(8,128)(2,1)}, bf16[48,4096]{1,0:T(8,128)(2,1)S(1)}, u32[]{:S(2)}, u32[]{:S(2)}) %collective-permute-start.4) | collective-permute-done | bytes 393248 | tf_op jit(solution)/shard_map/ppermute | solution.py:20
  18.2 8.2 %collective-permute-done.5.x3 = bf16[48,4096]{1,0:T(8,128)(2,1)} collective-permute-done((bf16[48,4096]{1,0:T(8,128)(2,1)}, bf16[48,4096]{1,0:T(8,128)(2,1)}, u32[]{:S(2)}, u32[]{:S(2)}) %collective-permute-start.5) | collective-permute-done | bytes 393248 | tf_op jit(solution)/shard_map/ppermute | solution.py:20
  29.8 2.7 %collective-permute-start.7 = (bf16[192,1024]{1,0:T(8,128)(2,1)S(1)}, bf16[192,1024]{1,0:T(8,128)(2,1)S(1)}, u32[]{:S(2)}, u32[]{:S(2)}) collective-permute-start(bf16[192,1024]{1,0:T(8,128)(2,1)S(1)} %get-tuple-element.27), channel_id=1, source_target_pairs={{0,32},{16,48},{32,0},{48,16},{1,33},{17,49},{33,1},{49,17},{2,34}... | collective-permute-start | bytes 1179656 | tf_op jit(solution)/shard_map/ppermute | solution.py:26
  34.0 6.6 %shard_map.86 = (bf16[192,768]{1,0:T(8,128)(2,1)S(1)}, f32[192,768]{1,0:T(8,128)S(1)}, f32[192,768]{1,0:T(8,128)S(1)}) custom-call(bf16[192,4096]{1,0:T(8,128)(2,1)S(1)} %get-tuple-element.23.x, bf16[4096,1536]{1,0:T(8,128)(2,1)} %bitcast.25, bf16[4096,1536]{1,0:T(8,128)(2,1)} %bitcast.26), custom_call_target="tpu_custom_call" | custom-call | flops 2415919104 | bytes 12582912 | tf_op jit(solution)/shard_map/pallas_call | solution.py:95
  40.7 2.4 %collective-permute-done.2.g3 = bf16[48,4096]{1,0:T(8,128)(2,1)S(1)} collective-permute-done((bf16[48,4096]{1,0:T(8,128)(2,1)}, bf16[48,4096]{1,0:T(8,128)(2,1)S(1)}, u32[]{:S(2)}, u32[]{:S(2)}) %collective-permute-start.2) | collective-permute-done | bytes 393248 | tf_op jit(solution)/shard_map/ppermute | solution.py:20
  43.1 7.1 %collective-permute-done.7.rest_1_.refs_2_ = bf16[192,1024]{1,0:T(8,128)(2,1)S(1)} collective-permute-done((bf16[192,1024]{1,0:T(8,128)(2,1)S(1)}, bf16[192,1024]{1,0:T(8,128)(2,1)S(1)}, u32[]{:S(2)}, u32[]{:S(2)}) %collective-permute-start.7) | collective-permute-done | bytes 393248 | tf_op jit(solution)/shard_map/ppermute | solution.py:26
  50.2 5.3 %shard_map.87.rest_0_.dact.refs_4_ = bf16[2,192,768]{2,1,0:T(8,128)(2,1)S(1)} custom-call(bf16[48,4096]{1,0:T(8,128)(2,1)S(1)} %get-tuple-element.52.g0, bf16[48,4096]{1,0:T(8,128)(2,1)S(1)} %collective-permute-done.g1, bf16[48,4096]{1,0:T(8,128)(2,1)S(1)} %collective-permute-done.1.g2, bf16[48,4096]{1,0:T(8,128)(2,1)S(1)} %collective-permute-done.2.g3, ...), custom_call_target="tpu_custom_call" | custom-call | flops 1207959552 | bytes 6291456 | tf_op jit(solution)/shard_map/pallas_call | solution.py:130
  55.7 1.5 copy-done.1
  57.3 4.6 %all-to-all-start.1 = ((bf16[4,192,1792]{2,1,0:T(8,128)(2,1)}), bf16[4,192,1792]{2,1,0:T(8,128)(2,1)}, u32[]{:S(2)}, u32[]{:S(2)}) async-start(bf16[4,192,1792]{2,1,0:T(8,128)(2,1)} %copy-done.1), calls=%async_computation.1 | async-start | bytes 5505024 | tf_op jit(solution)/shard_map/all_to_all | solution.py:298
  63.1 2.4 %collective-permute-start.10 = (bf16[2,192,768]{2,1,0:T(8,128)(2,1)S(1)}, bf16[2,192,768]{2,1,0:T(8,128)(2,1)}, u32[]{:S(2)}, u32[]{:S(2)}) collective-permute-start(bf16[2,192,768]{2,1,0:T(8,128)(2,1)S(1)} %shard_map.87.rest_0_.dact.refs_4_), channel_id=1, source_target_pairs={{0,32},{16,48},{32,0},{48,16},{1,33},{17,49},{33,1},{49,17},{2,34}... | collective-permute-start | bytes 1769480 | tf_op jit(solution)/shard_map/ppermute | solution.py:26
  65.5 1.6 collective-permute-start.11
  67.1 10.7 %collective-permute-done.9.rest_0_.refs_5_ = bf16[2,192,768]{2,1,0:T(8,128)(2,1)S(1)} collective-permute-done((bf16[2,192,768]{2,1,0:T(8,128)(2,1)S(1)}, bf16[2,192,768]{2,1,0:T(8,128)(2,1)S(1)}, u32[]{:S(2)}, u32[]{:S(2)}) %collective-permute-start.9) | collective-permute-done | bytes 589856 | tf_op jit(solution)/shard_map/ppermute | solution.py:26
  77.7 1.8 %copy-done.2 = bf16[4,192,1792]{2,1,0:T(8,128)(2,1)S(1)} copy-done((bf16[4,192,1792]{2,1,0:T(8,128)(2,1)S(1)}, bf16[4,192,1792]{2,1,0:T(8,128)(2,1)}, u32[]{:S(2)}) %copy-start.2) | copy-done | bytes 2752536
  79.5 9.5 %shard_map.89 = bf16[4,48,4096]{2,1,0:T(8,128)(2,1)S(1)} custom-call(s32[4]{0:T(128)S(1)} %pad_add_fusion.at, bf16[2,192,768]{2,1,0:T(8,128)(2,1)S(1)} %shard_map.87.rest_0_.dact.refs_4_, bf16[4096,1536]{1,0:T(8,128)(2,1)} %bitcast.27, bf16[2,192,768]{2,1,0:T(8,128)(2,1)S(1)} %collective-permute-done.9.rest_0_.refs_5_, bf16[4,192,1792]{2,1,0:T(8,128)(2,1)S(1)} %copy-done.2), custom_call_target="tpu_custom_call" | custom-call | flops 2415919104 | bytes 12582912 | tf_op jit(solution)/shard_map/pallas_call | solution.py:157
  91.0 4.1 %all-to-all-done.1.both = bf16[4,192,1792]{2,1,0:T(8,128)(2,1)} async-done(((bf16[4,192,1792]{2,1,0:T(8,128)(2,1)}), bf16[4,192,1792]{2,1,0:T(8,128)(2,1)}, u32[]{:S(2)}, u32[]{:S(2)}) %all-to-all-start.1) | async-done | bytes 2752544 | tf_op jit(solution)/shard_map/all_to_all | solution.py:298
  95.1 5.2 %all-to-all-start = ((bf16[4,48,4096]{2,1,0:T(8,128)(2,1)}), bf16[4,48,4096]{2,1,0:T(8,128)(2,1)S(1)}, u32[]{:S(2)}, u32[]{:S(2)}) async-start(bf16[4,48,4096]{2,1,0:T(8,128)(2,1)} %copy-done.3), calls=%async_computation | async-start | bytes 3145728 | tf_op jit(solution)/shard_map/all_to_all | solution.py:302
  100.3 3.7 %shard_map.93 = (f32[192,1024]{1,0:T(8,128)S(1)}, bf16[192,1024]{1,0:T(8,128)(2,1)S(1)}, bf16[192,1024]{1,0:T(8,128)(2,1)S(1)}, bf16[192,1024]{1,0:T(8,128)(2,1)S(1)}) custom-call(s32[4]{0:T(128)S(1)} %pad_add_fusion.at, bf16[4,192,1792]{2,1,0:T(8,128)(2,1)} %all-to-all-done.1.both), custom_call_target="tpu_custom_call" | custom-call | flops 1207959552 | bytes 2752512 | tf_op jit(solution)/shard_map/pallas_call | solution.py:225
  105.0 4.8 %shard_map.91 = (f32[256,1536]{1,0:T(8,128)S(1)}, bf16[256,1536]{1,0:T(8,128)(2,1)}, bf16[256,1536]{1,0:T(8,128)(2,1)}, bf16[256,1536]{1,0:T(8,128)(2,1)}) custom-call(s32[4]{0:T(128)S(1)} %pad_add_fusion.at, bf16[192,1024]{1,0:T(8,128)(2,1)S(1)} %copy-done.18, bf16[192,1024]{1,0:T(8,128)(2,1)S(1)} %copy-done.12, bf16[192,1024]{1,0:T(8,128)(2,1)S(1)} %copy-done.14, ...), custom_call_target="tpu_custom_call" | custom-call | flops 2415919104 | bytes 3932160 | tf_op jit(solution)/shard_map/pallas_call | solution.py:196
  110.5 2.0 %collective-permute-start.13 = (bf16[256,1536]{1,0:T(8,128)(2,1)}, bf16[256,1536]{1,0:T(8,128)(2,1)}, u32[]{:S(2)}, u32[]{:S(2)}) collective-permute-start(bf16[256,1536]{1,0:T(8,128)(2,1)} %get-tuple-element.33), channel_id=1, source_target_pairs={{0,8},{4,12},{8,0},{12,4},{1,9},{5,13},{9,1},{13,5},{2,10},{6,14},... | collective-permute-start | bytes 2359304 | tf_op jit(solution)/shard_map/ppermute | solution.py:26
  113.3 3.0 %collective-permute-start.17 = (bf16[192,1024]{1,0:T(8,128)(2,1)S(1)}, bf16[192,1024]{1,0:T(8,128)(2,1)S(1)}, u32[]{:S(2)}, u32[]{:S(2)}) collective-permute-start(bf16[192,1024]{1,0:T(8,128)(2,1)S(1)} %get-tuple-element.39), channel_id=1, source_target_pairs={{0,32},{16,48},{32,0},{48,16},{1,33},{17,49},{33,1},{49,17},{2,34}... | collective-permute-start | bytes 1179656 | tf_op jit(solution)/shard_map/ppermute | solution.py:26
  118.5 7.5 %collective-permute-done.17.refs_2_ = bf16[192,1024]{1,0:T(8,128)(2,1)S(1)} collective-permute-done((bf16[192,1024]{1,0:T(8,128)(2,1)S(1)}, bf16[192,1024]{1,0:T(8,128)(2,1)S(1)}, u32[]{:S(2)}, u32[]{:S(2)}) %collective-permute-start.17) | collective-permute-done | bytes 393248 | tf_op jit(solution)/shard_map/ppermute | solution.py:26
  125.9 7.8 %collective-permute-done.18.refs_3_ = bf16[192,1024]{1,0:T(8,128)(2,1)S(1)} collective-permute-done((bf16[192,1024]{1,0:T(8,128)(2,1)S(1)}, bf16[192,1024]{1,0:T(8,128)(2,1)S(1)}, u32[]{:S(2)}, u32[]{:S(2)}) %collective-permute-start.18) | collective-permute-done | bytes 393248 | tf_op jit(solution)/shard_map/ppermute | solution.py:26
  136.9 1.9 %shard_map.90.refs_4_ = bf16[128,4096]{1,0:T(8,128)(2,1)} custom-call(s32[4]{0:T(128)S(1)} %pad_add_fusion.at, bf16[128,192]{1,0:T(8,128)(2,1)S(1)} %get-tuple-element.43.mask, bf16[4,48,4096]{2,1,0:T(8,128)(2,1)S(1)} %all-to-all-done.arrived), custom_call_target="tpu_custom_call" | custom-call | flops 201326592 | bytes 2621440 | tf_op jit(solution)/shard_map/pallas_call | solution.py:303
  138.8 9.0 %collective-permute-done.12.refs_1_ = bf16[256,1536]{1,0:T(8,128)(2,1)S(1)} collective-permute-done((bf16[256,1536]{1,0:T(8,128)(2,1)}, bf16[256,1536]{1,0:T(8,128)(2,1)S(1)}, u32[]{:S(2)}, u32[]{:S(2)}) %collective-permute-start.12) | collective-permute-done | bytes 786464 | tf_op jit(solution)/shard_map/ppermute | solution.py:26
  149.8 1.8 %shard_map.92 = (f32[128,1536]{1,0:T(8,128)S(1)}, bf16[128,1536]{1,0:T(8,128)(2,1)S(1)}) custom-call(s32[4]{0:T(128)S(1)} %pad_add_fusion.at, f32[256,1536]{1,0:T(8,128)S(1)} %copy-done.6, bf16[256,1536]{1,0:T(8,128)(2,1)S(1)} %collective-permute-done.12.refs_1_, bf16[256,1536]{1,0:T(8,128)(2,1)} %collective-permute-done.13.refs_2_, ...), custom_call_target="tpu_custom_call" | custom-call | bytes 3932160 | tf_op jit(solution)/shard_map/pallas_call | solution.py:256
  152.7 1.6 add_convert_fusion.1
  154.3 3.8 %all-to-all-start.2 = ((bf16[4,24,1024]{2,1,0:T(8,128)(2,1)}), bf16[4,24,1024]{2,1,0:T(8,128)(2,1)S(1)}, u32[]{:S(2)}, u32[]{:S(2)}) async-start(bf16[4,24,1024]{2,1,0:T(8,128)(2,1)} %bitcast.9), calls=%async_computation.2 | async-start | bytes 393216 | tf_op jit(solution)/shard_map/all_to_all | solution.py:316
  158.1 3.7 %collective-permute-done.15 = bf16[128,1536]{1,0:T(8,128)(2,1)S(1)} collective-permute-done((bf16[128,1536]{1,0:T(8,128)(2,1)S(1)}, bf16[128,1536]{1,0:T(8,128)(2,1)S(1)}, u32[]{:S(2)}, u32[]{:S(2)}) %collective-permute-start.15) | collective-permute-done | bytes 393248 | tf_op jit(solution)/shard_map/ppermute | solution.py:30
  162.6 1.8 %all-to-all-done.2 = bf16[4,24,1024]{2,1,0:T(8,128)(2,1)S(1)} async-done(((bf16[4,24,1024]{2,1,0:T(8,128)(2,1)}), bf16[4,24,1024]{2,1,0:T(8,128)(2,1)S(1)}, u32[]{:S(2)}, u32[]{:S(2)}) %all-to-all-start.2) | async-done | bytes 196640 | tf_op jit(solution)/shard_map/all_to_all | solution.py:316
  (92 shorter events, 25.6 us)
Async XLA Ops:
  2.9 5.2 %copy-start.19 = (s32[128,8]{0,1:T(8,128)S(1)}, s32[128,8]{0,1:T(8,128)}, u32[]{:S(2)}) copy-start(s32[128,8]{0,1:T(8,128)} %param.8) | copy-start | bytes 12292
  2.9 5.2 %copy-start.20 = (f32[128,8]{0,1:T(8,128)S(1)}, f32[128,8]{0,1:T(8,128)}, u32[]{:S(2)}) copy-start(f32[128,8]{0,1:T(8,128)} %param.9) | copy-start | bytes 12292
  4.0 10.9 %collective-permute-start.3 = (bf16[48,4096]{1,0:T(8,128)(2,1)}, bf16[48,4096]{1,0:T(8,128)(2,1)S(1)}, u32[]{:S(2)}, u32[]{:S(2)}) collective-permute-start(bf16[48,4096]{1,0:T(8,128)(2,1)} %get-tuple-element.47), channel_id=1, source_target_pairs={{0,1},{1,0},{2,3},{3,2},{4,5},{5,4},{6,7},{7,6},{8,9},{9,8},{10,11... | collective-permute-start | bytes 1179656 | tf_op jit(solution)/shard_map/ppermute | solution.py:20
  4.0 14.1 %collective-permute-start.4 = (bf16[48,4096]{1,0:T(8,128)(2,1)}, bf16[48,4096]{1,0:T(8,128)(2,1)S(1)}, u32[]{:S(2)}, u32[]{:S(2)}) collective-permute-start(bf16[48,4096]{1,0:T(8,128)(2,1)} %get-tuple-element.46), channel_id=1, source_target_pairs={{0,2},{1,3},{2,0},{3,1},{4,6},{5,7},{6,4},{7,5},{8,10},{9,11},{10,... | collective-permute-start | bytes 1179656 | tf_op jit(solution)/shard_map/ppermute | solution.py:20
  8.0 18.3 %collective-permute-start.5 = (bf16[48,4096]{1,0:T(8,128)(2,1)}, bf16[48,4096]{1,0:T(8,128)(2,1)}, u32[]{:S(2)}, u32[]{:S(2)}) collective-permute-start(bf16[48,4096]{1,0:T(8,128)(2,1)} %get-tuple-element.45), channel_id=1, source_target_pairs={{0,3},{1,2},{2,1},{3,0},{4,7},{5,6},{6,5},{7,4},{8,11},{9,10},{10,... | collective-permute-start | bytes 1179656 | tf_op jit(solution)/shard_map/ppermute | solution.py:20
  11.3 21.3 %collective-permute-start = (bf16[48,4096]{1,0:T(8,128)(2,1)}, bf16[48,4096]{1,0:T(8,128)(2,1)S(1)}, u32[]{:S(2)}, u32[]{:S(2)}) collective-permute-start(bf16[48,4096]{1,0:T(8,128)(2,1)} %get-tuple-element.51), channel_id=1, source_target_pairs={{0,1},{1,0},{2,3},{3,2},{4,5},{5,4},{6,7},{7,6},{8,9},{9,8},{10,11... | collective-permute-start | bytes 1179656 | tf_op jit(solution)/shard_map/ppermute | solution.py:20
  11.4 29.3 %collective-permute-start.1 = (bf16[48,4096]{1,0:T(8,128)(2,1)}, bf16[48,4096]{1,0:T(8,128)(2,1)S(1)}, u32[]{:S(2)}, u32[]{:S(2)}) collective-permute-start(bf16[48,4096]{1,0:T(8,128)(2,1)} %get-tuple-element.50), channel_id=1, source_target_pairs={{0,2},{1,3},{2,0},{3,1},{4,6},{5,7},{6,4},{7,5},{8,10},{9,11},{10,... | collective-permute-start | bytes 1179656 | tf_op jit(solution)/shard_map/ppermute | solution.py:20
  14.9 28.2 %collective-permute-start.2 = (bf16[48,4096]{1,0:T(8,128)(2,1)}, bf16[48,4096]{1,0:T(8,128)(2,1)S(1)}, u32[]{:S(2)}, u32[]{:S(2)}) collective-permute-start(bf16[48,4096]{1,0:T(8,128)(2,1)} %get-tuple-element.49), channel_id=1, source_target_pairs={{0,3},{1,2},{2,1},{3,0},{4,7},{5,6},{6,5},{7,4},{8,11},{9,10},{10,... | collective-permute-start | bytes 1179656 | tf_op jit(solution)/shard_map/ppermute | solution.py:20
  28.3 14.7 %collective-permute-start.6 = (bf16[192,1024]{1,0:T(8,128)(2,1)S(1)}, bf16[192,1024]{1,0:T(8,128)(2,1)S(1)}, u32[]{:S(2)}, u32[]{:S(2)}) collective-permute-start(bf16[192,1024]{1,0:T(8,128)(2,1)S(1)} %get-tuple-element.26), channel_id=1, source_target_pairs={{0,16},{16,32},{32,48},{48,0},{1,17},{17,33},{33,49},{49,1},{2,18}... | collective-permute-start | bytes 1179656 | tf_op jit(solution)/shard_map/ppermute | solution.py:26
  29.8 20.3 %collective-permute-start.7 = (bf16[192,1024]{1,0:T(8,128)(2,1)S(1)}, bf16[192,1024]{1,0:T(8,128)(2,1)S(1)}, u32[]{:S(2)}, u32[]{:S(2)}) collective-permute-start(bf16[192,1024]{1,0:T(8,128)(2,1)S(1)} %get-tuple-element.27), channel_id=1, source_target_pairs={{0,32},{16,48},{32,0},{48,16},{1,33},{17,49},{33,1},{49,17},{2,34}... | collective-permute-start | bytes 1179656 | tf_op jit(solution)/shard_map/ppermute | solution.py:26
  32.6 17.6 %collective-permute-start.8 = (bf16[192,1024]{1,0:T(8,128)(2,1)S(1)}, bf16[192,1024]{1,0:T(8,128)(2,1)S(1)}, u32[]{:S(2)}, u32[]{:S(2)}) collective-permute-start(bf16[192,1024]{1,0:T(8,128)(2,1)S(1)} %get-tuple-element.28), channel_id=1, source_target_pairs={{0,48},{16,0},{32,16},{48,32},{1,49},{17,1},{33,17},{49,33},{2,50}... | collective-permute-start | bytes 1179656 | tf_op jit(solution)/shard_map/ppermute | solution.py:26
  43.1 12.4 %copy-start.11 = (bf16[192,1024]{1,0:T(8,128)(2,1)}, bf16[192,1024]{1,0:T(8,128)(2,1)S(1)}, u32[]{:S(2)}) copy-start(bf16[192,1024]{1,0:T(8,128)(2,1)S(1)} %collective-permute-done.6.rest_0_.refs_1_) | copy-start | bytes 1179652
  50.2 5.4 %copy-start.13 = (bf16[192,1024]{1,0:T(8,128)(2,1)}, bf16[192,1024]{1,0:T(8,128)(2,1)S(1)}, u32[]{:S(2)}) copy-start(bf16[192,1024]{1,0:T(8,128)(2,1)S(1)} %collective-permute-done.7.rest_1_.refs_2_) | copy-start | bytes 1179652
  50.2 5.4 %copy-start.15 = (bf16[192,1024]{1,0:T(8,128)(2,1)}, bf16[192,1024]{1,0:T(8,128)(2,1)S(1)}, u32[]{:S(2)}) copy-start(bf16[192,1024]{1,0:T(8,128)(2,1)S(1)} %collective-permute-done.8.rest_2_.refs_3_) | copy-start | bytes 1179652
  57.3 37.8 %all-to-all-start.1 = ((bf16[4,192,1792]{2,1,0:T(8,128)(2,1)}), bf16[4,192,1792]{2,1,0:T(8,128)(2,1)}, u32[]{:S(2)}, u32[]{:S(2)}) async-start(bf16[4,192,1792]{2,1,0:T(8,128)(2,1)} %copy-done.1), calls=%async_computation.1 | async-start | bytes 5505024 | tf_op jit(solution)/shard_map/all_to_all | solution.py:298
  61.9 15.9 %collective-permute-start.9 = (bf16[2,192,768]{2,1,0:T(8,128)(2,1)S(1)}, bf16[2,192,768]{2,1,0:T(8,128)(2,1)S(1)}, u32[]{:S(2)}, u32[]{:S(2)}) collective-permute-start(bf16[2,192,768]{2,1,0:T(8,128)(2,1)S(1)} %shard_map.87.rest_0_.dact.refs_4_), channel_id=1, source_target_pairs={{0,16},{16,32},{32,48},{48,0},{1,17},{17,33},{33,49},{49,1},{2,18}... | collective-permute-start | bytes 1769480 | tf_op jit(solution)/shard_map/ppermute | solution.py:26
  63.1 41.8 %collective-permute-start.10 = (bf16[2,192,768]{2,1,0:T(8,128)(2,1)S(1)}, bf16[2,192,768]{2,1,0:T(8,128)(2,1)}, u32[]{:S(2)}, u32[]{:S(2)}) collective-permute-start(bf16[2,192,768]{2,1,0:T(8,128)(2,1)S(1)} %shard_map.87.rest_0_.dact.refs_4_), channel_id=1, source_target_pairs={{0,32},{16,48},{32,0},{48,16},{1,33},{17,49},{33,1},{49,17},{2,34}... | collective-permute-start | bytes 1769480 | tf_op jit(solution)/shard_map/ppermute | solution.py:26
  65.5 39.4 %collective-permute-start.11 = (bf16[2,192,768]{2,1,0:T(8,128)(2,1)S(1)}, bf16[2,192,768]{2,1,0:T(8,128)(2,1)}, u32[]{:S(2)}, u32[]{:S(2)}) collective-permute-start(bf16[2,192,768]{2,1,0:T(8,128)(2,1)S(1)} %shard_map.87.rest_0_.dact.refs_4_), channel_id=1, source_target_pairs={{0,48},{16,0},{32,16},{48,32},{1,49},{17,1},{33,17},{49,33},{2,50}... | collective-permute-start | bytes 1769480 | tf_op jit(solution)/shard_map/ppermute | solution.py:26
  95.1 41.8 %all-to-all-start = ((bf16[4,48,4096]{2,1,0:T(8,128)(2,1)}), bf16[4,48,4096]{2,1,0:T(8,128)(2,1)S(1)}, u32[]{:S(2)}, u32[]{:S(2)}) async-start(bf16[4,48,4096]{2,1,0:T(8,128)(2,1)} %copy-done.3), calls=%async_computation | async-start | bytes 3145728 | tf_op jit(solution)/shard_map/all_to_all | solution.py:302
  100.3 4.7 %copy-start.16 = (bf16[192,1024]{1,0:T(8,128)(2,1)S(1)}, bf16[192,1024]{1,0:T(8,128)(2,1)}, u32[]{:S(2)}) copy-start(bf16[192,1024]{1,0:T(8,128)(2,1)} %copy-done.15) | copy-start | bytes 1179652
  100.3 4.7 %copy-start.18 = (bf16[192,1024]{1,0:T(8,128)(2,1)S(1)}, bf16[192,1024]{1,0:T(8,128)(2,1)}, u32[]{:S(2)}) copy-start(bf16[192,1024]{1,0:T(8,128)(2,1)} %copy-done.17) | copy-start | bytes 1179652
  104.0 13.0 %collective-permute-start.16 = (bf16[192,1024]{1,0:T(8,128)(2,1)S(1)}, bf16[192,1024]{1,0:T(8,128)(2,1)S(1)}, u32[]{:S(2)}, u32[]{:S(2)}) collective-permute-start(bf16[192,1024]{1,0:T(8,128)(2,1)S(1)} %get-tuple-element.38), channel_id=1, source_target_pairs={{0,16},{16,32},{32,48},{48,0},{1,17},{17,33},{33,49},{49,1},{2,18}... | collective-permute-start | bytes 1179656 | tf_op jit(solution)/shard_map/ppermute | solution.py:26
  109.8 26.0 %copy-start.5 = (f32[256,1536]{1,0:T(8,128)}, f32[256,1536]{1,0:T(8,128)S(1)}, u32[]{:S(2)}) copy-start(f32[256,1536]{1,0:T(8,128)S(1)} %get-tuple-element.31.refs_0_) | copy-start | bytes 4718596
  109.9 37.9 %collective-permute-start.12 = (bf16[256,1536]{1,0:T(8,128)(2,1)}, bf16[256,1536]{1,0:T(8,128)(2,1)S(1)}, u32[]{:S(2)}, u32[]{:S(2)}) collective-permute-start(bf16[256,1536]{1,0:T(8,128)(2,1)} %get-tuple-element.32), channel_id=1, source_target_pairs={{0,4},{4,8},{8,12},{12,0},{1,5},{5,9},{9,13},{13,1},{2,6},{6,10},{... | collective-permute-start | bytes 2359304 | tf_op jit(solution)/shard_map/ppermute | solution.py:26
  110.5 37.3 %collective-permute-start.13 = (bf16[256,1536]{1,0:T(8,128)(2,1)}, bf16[256,1536]{1,0:T(8,128)(2,1)}, u32[]{:S(2)}, u32[]{:S(2)}) collective-permute-start(bf16[256,1536]{1,0:T(8,128)(2,1)} %get-tuple-element.33), channel_id=1, source_target_pairs={{0,8},{4,12},{8,0},{12,4},{1,9},{5,13},{9,1},{13,5},{2,10},{6,14},... | collective-permute-start | bytes 2359304 | tf_op jit(solution)/shard_map/ppermute | solution.py:26
  112.5 36.0 %collective-permute-start.14 = (bf16[256,1536]{1,0:T(8,128)(2,1)}, bf16[256,1536]{1,0:T(8,128)(2,1)}, u32[]{:S(2)}, u32[]{:S(2)}) collective-permute-start(bf16[256,1536]{1,0:T(8,128)(2,1)} %get-tuple-element.34), channel_id=1, source_target_pairs={{0,12},{4,0},{8,4},{12,8},{1,13},{5,1},{9,5},{13,9},{2,14},{6,2},{... | collective-permute-start | bytes 2359304 | tf_op jit(solution)/shard_map/ppermute | solution.py:26
  113.3 12.6 %collective-permute-start.17 = (bf16[192,1024]{1,0:T(8,128)(2,1)S(1)}, bf16[192,1024]{1,0:T(8,128)(2,1)S(1)}, u32[]{:S(2)}, u32[]{:S(2)}) collective-permute-start(bf16[192,1024]{1,0:T(8,128)(2,1)S(1)} %get-tuple-element.39), channel_id=1, source_target_pairs={{0,32},{16,48},{32,0},{48,16},{1,33},{17,49},{33,1},{49,17},{2,34}... | collective-permute-start | bytes 1179656 | tf_op jit(solution)/shard_map/ppermute | solution.py:26
  117.0 16.8 %collective-permute-start.18 = (bf16[192,1024]{1,0:T(8,128)(2,1)S(1)}, bf16[192,1024]{1,0:T(8,128)(2,1)S(1)}, u32[]{:S(2)}, u32[]{:S(2)}) collective-permute-start(bf16[192,1024]{1,0:T(8,128)(2,1)S(1)} %get-tuple-element.40), channel_id=1, source_target_pairs={{0,48},{16,0},{32,16},{48,32},{1,49},{17,1},{33,17},{49,33},{2,50}... | collective-permute-start | bytes 1179656 | tf_op jit(solution)/shard_map/ppermute | solution.py:26
  135.8 16.8 %collective-permute-start.19 = (bf16[96,1024]{1,0:T(8,128)(2,1)}, bf16[96,1024]{1,0:T(8,128)(2,1)}, u32[]{:S(2)}, u32[]{:S(2)}) collective-permute-start(bf16[96,1024]{1,0:T(8,128)(2,1)} %get-tuple-element.42), channel_id=1, source_target_pairs={{0,64},{64,0},{1,65},{65,1},{2,66},{66,2},{3,67},{67,3},{4,68},{68... | collective-permute-start | bytes 589832 | tf_op jit(solution)/shard_map/ppermute | solution.py:30
  136.9 11.7 %copy-start.6 = (f32[256,1536]{1,0:T(8,128)S(1)}, f32[256,1536]{1,0:T(8,128)}, u32[]{:S(2)}) copy-start(f32[256,1536]{1,0:T(8,128)} %copy-done.5) | copy-start | bytes 4718596
  151.6 10.2 %collective-permute-start.15 = (bf16[128,1536]{1,0:T(8,128)(2,1)S(1)}, bf16[128,1536]{1,0:T(8,128)(2,1)S(1)}, u32[]{:S(2)}, u32[]{:S(2)}) collective-permute-start(bf16[128,1536]{1,0:T(8,128)(2,1)S(1)} %get-tuple-element.36), channel_id=1, source_target_pairs={{0,64},{64,0},{1,65},{65,1},{2,66},{66,2},{3,67},{67,3},{4,68},{68... | collective-permute-start | bytes 1179656 | tf_op jit(solution)/shard_map/ppermute | solution.py:30
  154.3 10.1 %all-to-all-start.2 = ((bf16[4,24,1024]{2,1,0:T(8,128)(2,1)}), bf16[4,24,1024]{2,1,0:T(8,128)(2,1)S(1)}, u32[]{:S(2)}, u32[]{:S(2)}) async-start(bf16[4,24,1024]{2,1,0:T(8,128)(2,1)} %bitcast.9), calls=%async_computation.2 | async-start | bytes 393216 | tf_op jit(solution)/shard_map/all_to_all | solution.py:316
  (12 other events, 26.8 us)

commit v3 on v2

--- a/solution.py
+++ b/solution.py
@@ -110,7 +110,7 @@
 
 
 def dh_step(g0, g1, g2, g3, wd, slope, silu, *rest):
-    dact, whole = rest[-2:]
+    dact_g, dact_u, whole = rest[-3:]
 
     @pl.when(pl.program_id(0) == 0)
     def _():
@@ -118,8 +118,8 @@
             whole[k * CAP : k * CAP + CAP, :] = piece[...]
 
     dh = wide_dot(whole[...], wd[...])
-    dact[0] = (dh * slope[...]).astype(BF)
-    dact[1] = (dh * silu[...]).astype(BF)
+    dact_g[...] = (dh * slope[...]).astype(BF)
+    dact_u[...] = (dh * silu[...]).astype(BF)
 
 
 def dh_call(gs, down_proj, slope, silu, after):
@@ -133,8 +133,8 @@
         in_specs=[pl.BlockSpec((CAP, width), lambda i: (0, 0))] * 4
         + [pl.BlockSpec((step, width), lambda i: (i, 0)), part, part]
         + [pl.BlockSpec(memory_space=pl.ANY)] * len(after),
-        out_specs=pl.BlockSpec((2, rows, step), lambda i: (0, 0, i)),
-        out_shape=jax.ShapeDtypeStruct((2, rows, inner), BF),
+        out_specs=[part, part],
+        out_shape=[shape(rows, inner)] * 2,
         scratch_shapes=[pltpu.VMEM((rows, width), BF)],
         compiler_params=pltpu.CompilerParams(vmem_limit_bytes=48 * MB),
         cost_estimate=pl.CostEstimate(
@@ -143,21 +143,22 @@
     )(*gs, down_proj, slope, silu, *after)
 
 
-def back_step(at, dact, wt, *rest):
-    out, inner = rest[-1], dact.shape[2]
-    got = wide_dot(dact[0], wt[:, :inner]) + wide_dot(dact[1], wt[:, inner:])
+def back_step(at, dg, du, wt, *rest):
+    out, inner = rest[-1], dg.shape[1]
+    got = wide_dot(dg[...], wt[:, :inner]) + wide_dot(du[...], wt[:, inner:])
     for k in range(4):
         out[jnp.bitwise_xor(at[3], k)] = got[k * CAP : k * CAP + CAP].astype(BF)
 
 
-def back_call(at, dact, gate_up, after):
-    rows, inner = dact.shape[1:]
+def back_call(at, dg, du, gate_up, after):
+    rows, inner = dg.shape
     width = gate_up.shape[0]
     step = 512
     return pl.pallas_call(
         back_step,
         grid=(width // step,),
-        in_specs=[SMEM, pl.BlockSpec((2, rows, inner), lambda i: (0, 0, 0))]
+        in_specs=[SMEM]
+        + [pl.BlockSpec((rows, inner), lambda i: (0, 0))] * 2
         + [pl.BlockSpec((step, 2 * inner), lambda i: (i, 0))]
         + [pl.BlockSpec(memory_space=pl.ANY)] * len(after),
         out_specs=pl.BlockSpec((4, CAP, step), lambda i: (0, 0, i)),
@@ -166,7 +167,7 @@
         cost_estimate=pl.CostEstimate(
             flops=4 * rows * width * inner, bytes_accessed=4 * width * inner, transcendentals=0
         ),
-    )(at, dact, gate_up, *after)
+    )(at, dg, du, gate_up, *after)
 
 
 def tok_step(at, mask, arrived, out, whole):
@@ -177,12 +178,10 @@
 
 def tile_step(at, *refs):
     xs, ds, outs, xall, dall = refs[:4], refs[4:8], refs[-6:-2], refs[-2], refs[-1]
-    rows, inner = ds[0].shape[1:]
+    rows = xs[0].shape[0]
     for p in range(4):
-        part = slice(p * rows, p * rows + rows)
-        xall[part, :] = xs[p][...]
-        for h in range(2):
-            dall[part, h * inner : h * inner + inner] = ds[p][h]
+        xall[p * rows : p * rows + rows, :] = xs[p][...]
+        dall[p * rows : p * rows + rows, :] = ds[p][...]
     for j in (1, 2, 3, 0):
         other = lax.rem(at[2] + j, 4)
         for b in range(2):
@@ -192,14 +191,14 @@
 
 def tile_call(at, xs, ds, after):
     rows, part = xs[0].shape
-    wide = 2 * ds[0].shape[2]
+    inner = ds[0].shape[1]
     return call(
         tile_step,
-        [shape(256, wide, F32)] + [shape(256, wide)] * 3,
+        [shape(256, inner, F32)] + [shape(256, inner)] * 3,
         9,
-        [pltpu.VMEM((4 * rows, part), BF), pltpu.VMEM((4 * rows, wide), BF)],
-        flops=8 * rows * part * wide,
-        moved=8 * rows * (part + wide),
+        [pltpu.VMEM((4 * rows, part), BF), pltpu.VMEM((4 * rows, inner), BF)],
+        flops=8 * rows * part * inner,
+        moved=8 * rows * (part + inner),
         after=len(after),
         limit=12,
     )(at, *xs, *ds, *after)
@@ -285,20 +284,28 @@
     )(at, *xs)
     xa = [shift(packed[j], "x", j) for j in range(4)]
     hidden, slope, silu = act_call(packed[4], gate_up, inner)
-    dact = dh_call(gs, down_proj, slope, silu, xa[1:])
-    da = [shift(dact, "x", j) for j in range(4)]
     sent = call(
         pack_g,
         [jax.ShapeDtypeStruct((4, rows, part + inner), BF)],
         5,
         moved=4 * rows * width,
         scalars=0,
-        after=1,
-    )(*gs, hidden, dact)[0]
+        after=2,
+    )(*gs, hidden, xa[1], xa[3])[0]
+    dact_g, dact_u = dh_call(gs, down_proj, slope, silu, [sent])
+    da_g = [shift(dact_g, "x", j) for j in range(4)]
+    da_u = [shift(dact_u, "x", j) for j in range(4)]
     both = lax.all_to_all(sent, "y", split_axis=0, concat_axis=0, tiled=True)
-    parts = tile_call(at, xa, da, [])
-    gate = [parts[0]] + [shift(parts[j], "y", j) for j in (1, 2, 3)]
-    back = back_call(at, dact, gate_up, [da[1], sent])
+    def half(ds, after):
+        parts = tile_call(at, xa, ds, after)
+        return [parts[0]] + [shift(parts[j], "y", j) for j in (1, 2, 3)]
+
+    back = back_call(at, dact_g, dact_u, gate_up, [da_g[1]])
+    gate = half(da_g, [back])
+    up = half(da_u, [])
+    parts = down_call(at, both, part, [up[0]])
+    down = [parts[0]] + [shift(parts[j], "x", j) for j in (1, 2, 3)]
+
     arrived = lax.all_to_all(back, ("v", "c"), split_axis=0, concat_axis=0, tiled=True)
     token_grad = call(
         tok_step,
@@ -308,16 +315,20 @@
         flops=2 * toks * rows * width,
         moved=2 * (rows + toks) * width,
     )(at, mask, arrived)[0]
-    parts = down_call(at, both, part, [])
-    down = [parts[0]] + [shift(parts[j], "x", j) for j in (1, 2, 3)]
-
     keep, send = sum_call(at, down, [])
     down_grad = (keep + swap_w(send).astype(F32)).astype(BF).reshape(4, 24, part)
-    down_grad = lax.all_to_all(down_grad, "y", split_axis=0, concat_axis=0, tiled=True)
-    down_grad = jnp.concatenate([down_grad[i] for i in range(4)], axis=1)
-
-    keep, send = sum_call(at, gate, [token_grad])
-    gate_up_grad = (keep + swap_w(send).astype(F32)).astype(BF)
+    cols = [
+        shift(lax.dynamic_index_in_dim(down_grad, (y + j) % 4, 0, False), "y", j) for j in range(4)
+    ]
+    turned = jnp.stack(cols[::-1] + cols[::-1])
+    mine = lax.dynamic_slice_in_dim(turned, 3 - y, 4, 0)
+    down_grad = jnp.concatenate([mine[i] for i in range(4)], axis=1)
+
+    def last(parts, after):
+        keep, send = sum_call(at, parts, after)
+        return (keep + swap_w(send).astype(F32)).astype(BF)
+
+    gate_up_grad = jnp.concatenate([last(gate, []), last(up, [])], axis=1)
     return token_grad, gate_up_grad[None], down_grad[None]
 
 

time: 166 us -> 174 us (1.048)
  starting transfers between devices: 43.1 us -> 50.2 us
  local copies, waits for them, and re-layouts: 10.8 us -> 15.5 us
  waiting for transfers between devices: 66.9 us -> 62.4 us
  Pallas kernels: 36.5 us -> 38.9 us
    ppermute x12 -> x21, waiting for transfers between devices: 43.4 us -> 27.3 us  [shift(): return lax.ppermute(a, axis, [(i, (i + j) % 4) for i in range(4)])]
    ppermute x2 -> x3, waiting for transfers between devices: 3.7 us -> 18.6 us  [swap_w(): return lax.ppermute(a, 'w', [(0, 1), (1, 0)])]
    ppermute x12 -> x21, starting transfers between devices: 19.8 us -> 29.9 us  [shift(): return lax.ppermute(a, axis, [(i, (i + j) % 4) for i in range(4)])]
    unnamed x42 -> x53, local copies, waits for them, and re-layouts: 8.11 us -> 12.8 us
    all_to_all x1, waiting for transfers between devices: 4.11 us -> 0.01 us  [shards(): both = lax.all_to_all(sent, 'y', split_axis=0, concat_axis=0, tiled=True)]
    all_to_all x1 -> x0, starting transfers between devices: 3.79 us -> none  [shards(): lax.all_to_all(down_grad, 'y', split_axis=0, concat_axis=0, tiled=True)]
    ppermute x6, waiting for transfers between devices: 13.8 us -> 16.5 us  [swap_expert(): return lax.ppermute(a, ('v', 'c'), [(i, i ^ k) for i in range(4)])]
    all_to_all x1 -> x0, waiting for transfers between devices: 1.82 us -> none  [shards(): lax.all_to_all(down_grad, 'y', split_axis=0, concat_axis=0, tiled=True)]
  transfers between devices with their start and end apart: 23 -> 32, of which waited for: 13 -> 10; matrix products, arithmetic and copies ran while one was open for 3% -> 2% of each run, Pallas kernels for 19% -> 22%
where the time goes in v3:
time: 174 us; the launch traced here: 173 us
  waiting for transfers between devices  62.4 us (36%)
  starting transfers between devices  50.2 us (29%)
  Pallas kernels  38.9 us (22%)
  local copies, waits for them, and re-layouts  15.5 us (9%)
  other arithmetic  3.87 us (2%)
    ppermute x21, starting transfers between devices, shift(): return lax.ppermute(a, axis, [(i, (i + j) % 4) for i in range(4)])  29.9 us
    ppermute x21, waiting for transfers between devices, shift(): return lax.ppermute(a, axis, [(i, (i + j) % 4) for i in range(4)])  27.3 us
    ppermute x3, waiting for transfers between devices, swap_w(): return lax.ppermute(a, 'w', [(0, 1), (1, 0)])  18.6 us
    ppermute x6, waiting for transfers between devices, swap_expert(): return lax.ppermute(a, ('v', 'c'), [(i, i ^ k) for i in range(4)])  16.5 us
    unnamed x53, local copies, waits for them, and re-layouts  12.8 us
    pallas_call x1, Pallas kernels, back_call(): pl.pallas_call(back_step, grid=(width // step,), in_specs=[SMEM] + [pl.Bl...  10.3 us
    ppermute x6, starting transfers between devices, swap_expert(): return lax.ppermute(a, ('v', 'c'), [(i, i ^ k) for i in range(4)])  7.65 us
    pallas_call x1, Pallas kernels, act_call(): pl.pallas_call(act_step, grid=(n,), in_specs=[pl.BlockSpec((rows, width),...  6.65 us
  transfers between devices with their start and end apart: 32, of which 10 were waited for; matrix products, arithmetic and copies ran while one was open for 2% of the time, Pallas kernels for 22%

profile of v3, /device:TPU:0, one launch (start us, length us, event | category | flops | bytes accessed | tf_op | source)
XLA Modules:
  0.0 173.3 jit_solution(1707306871525557779)
XLA Ops:
  4.0 4.0 %collective-permute-start.4 = (bf16[48,4096]{1,0:T(8,128)(2,1)}, bf16[48,4096]{1,0:T(8,128)(2,1)}, u32[]{:S(2)}, u32[]{:S(2)}) collective-permute-start(bf16[48,4096]{1,0:T(8,128)(2,1)} %get-tuple-element.62), channel_id=1, source_target_pairs={{0,2},{1,3},{2,0},{3,1},{4,6},{5,7},{6,4},{7,5},{8,10},{9,11},{10,... | collective-permute-start | bytes 1179656 | tf_op jit(solution)/shard_map/ppermute | solution.py:20
  10.1 3.4 %collective-permute-start.1 = (bf16[48,4096]{1,0:T(8,128)(2,1)}, bf16[48,4096]{1,0:T(8,128)(2,1)S(1)}, u32[]{:S(2)}, u32[]{:S(2)}) collective-permute-start(bf16[48,4096]{1,0:T(8,128)(2,1)} %get-tuple-element.66), channel_id=1, source_target_pairs={{0,2},{1,3},{2,0},{3,1},{4,6},{5,7},{6,4},{7,5},{8,10},{9,11},{10,... | collective-permute-start | bytes 1179656 | tf_op jit(solution)/shard_map/ppermute | solution.py:20
  13.7 4.5 %collective-permute-done.4.x2 = bf16[48,4096]{1,0:T(8,128)(2,1)} collective-permute-done((bf16[48,4096]{1,0:T(8,128)(2,1)}, bf16[48,4096]{1,0:T(8,128)(2,1)}, u32[]{:S(2)}, u32[]{:S(2)}) %collective-permute-start.4) | collective-permute-done | bytes 393248 | tf_op jit(solution)/shard_map/ppermute | solution.py:20
  18.2 8.1 %collective-permute-done.5.x3 = bf16[48,4096]{1,0:T(8,128)(2,1)} collective-permute-done((bf16[48,4096]{1,0:T(8,128)(2,1)}, bf16[48,4096]{1,0:T(8,128)(2,1)}, u32[]{:S(2)}, u32[]{:S(2)}) %collective-permute-start.5) | collective-permute-done | bytes 393248 | tf_op jit(solution)/shard_map/ppermute | solution.py:20
  29.9 1.7 %collective-permute-start.7 = (bf16[192,1024]{1,0:T(8,128)(2,1)S(1)}, bf16[192,1024]{1,0:T(8,128)(2,1)S(1)}, u32[]{:S(2)}, u32[]{:S(2)}) collective-permute-start(bf16[192,1024]{1,0:T(8,128)(2,1)S(1)} %get-tuple-element.36), channel_id=1, source_target_pairs={{0,48},{16,0},{32,16},{48,32},{1,49},{17,1},{33,17},{49,33},{2,50}... | collective-permute-start | bytes 1179656 | tf_op jit(solution)/shard_map/ppermute | solution.py:26
  31.6 6.6 %shard_map.86 = (bf16[192,768]{1,0:T(8,128)(2,1)S(1)}, f32[192,768]{1,0:T(8,128)S(1)}, f32[192,768]{1,0:T(8,128)S(1)}) custom-call(bf16[192,4096]{1,0:T(8,128)(2,1)S(1)} %get-tuple-element.31.x, bf16[4096,1536]{1,0:T(8,128)(2,1)} %bitcast.40, bf16[4096,1536]{1,0:T(8,128)(2,1)} %bitcast.41), custom_call_target="tpu_custom_call" | custom-call | flops 2415919104 | bytes 12582912 | tf_op jit(solution)/shard_map/pallas_call | solution.py:95
  39.1 3.9 %collective-permute-done.2.g3 = bf16[48,4096]{1,0:T(8,128)(2,1)S(1)} collective-permute-done((bf16[48,4096]{1,0:T(8,128)(2,1)}, bf16[48,4096]{1,0:T(8,128)(2,1)S(1)}, u32[]{:S(2)}, u32[]{:S(2)}) %collective-permute-start.2) | collective-permute-done | bytes 393248 | tf_op jit(solution)/shard_map/ppermute | solution.py:20
  43.2 1.5 copy-done.1
  46.3 4.6 %all-to-all-start.1 = ((bf16[4,192,1792]{2,1,0:T(8,128)(2,1)}), bf16[4,192,1792]{2,1,0:T(8,128)(2,1)}, u32[]{:S(2)}, u32[]{:S(2)}) async-start(bf16[4,192,1792]{2,1,0:T(8,128)(2,1)} %copy-done.1), calls=%async_computation.1 | async-start | bytes 5505024 | tf_op jit(solution)/shard_map/all_to_all | solution.py:298
  50.9 3.1 %collective-permute-start.9 = (bf16[192,1024]{1,0:T(8,128)(2,1)}, bf16[192,1024]{1,0:T(8,128)(2,1)S(1)}, u32[]{:S(2)}, u32[]{:S(2)}) collective-permute-start(bf16[192,1024]{1,0:T(8,128)(2,1)} %copy-done.19), channel_id=1, source_target_pairs={{0,32},{16,48},{32,0},{48,16},{1,33},{17,49},{33,1},{49,17},{2,34}... | collective-permute-start | bytes 1179656 | tf_op jit(solution)/shard_map/ppermute | solution.py:26
  54.0 1.8 %copy-done.2 = bf16[4,192,1792]{2,1,0:T(8,128)(2,1)S(1)} copy-done((bf16[4,192,1792]{2,1,0:T(8,128)(2,1)S(1)}, bf16[4,192,1792]{2,1,0:T(8,128)(2,1)}, u32[]{:S(2)}) %copy-start.2) | copy-done | bytes 2752536
  56.8 5.1 %shard_map.88 = (bf16[192,768]{1,0:T(8,128)(2,1)S(1)}, bf16[192,768]{1,0:T(8,128)(2,1)S(1)}) custom-call(bf16[48,4096]{1,0:T(8,128)(2,1)S(1)} %get-tuple-element.68.g0, bf16[48,4096]{1,0:T(8,128)(2,1)S(1)} %collective-permute-done.g1, bf16[48,4096]{1,0:T(8,128)(2,1)S(1)} %collective-permute-done.1.g2, bf16[48,4096]{1,0:T(8,128)(2,1)S(1)} %collective-permute-done.2.g3, ...), custom_call_target="tpu_custom_call" | custom-call | flops 1207959552 | bytes 6291456 | tf_op jit(solution)/shard_map/pallas_call | solution.py:130
  62.5 2.0 %collective-permute-start.10 = (bf16[192,768]{1,0:T(8,128)(2,1)S(1)}, bf16[192,768]{1,0:T(8,128)(2,1)S(1)}, u32[]{:S(2)}, u32[]{:S(2)}) collective-permute-start(bf16[192,768]{1,0:T(8,128)(2,1)S(1)} %get-tuple-element.37.dg.refs_4_), channel_id=1, source_target_pairs={{0,32},{16,48},{32,0},{48,16},{1,33},{17,49},{33,1},{49,17},{2,34}... | collective-permute-start | bytes 884744 | tf_op jit(solution)/shard_map/ppermute | solution.py:26
  66.6 1.6 collective-permute-start.17
  68.2 11.2 %collective-permute-done.8.rest_0_.refs_5_ = bf16[192,768]{1,0:T(8,128)(2,1)S(1)} collective-permute-done((bf16[192,768]{1,0:T(8,128)(2,1)S(1)}, bf16[192,768]{1,0:T(8,128)(2,1)S(1)}, u32[]{:S(2)}, u32[]{:S(2)}) %collective-permute-start.8) | collective-permute-done | bytes 294944 | tf_op jit(solution)/shard_map/ppermute | solution.py:26
  79.4 10.3 %shard_map.89.refs_8_ = bf16[4,48,4096]{2,1,0:T(8,128)(2,1)} custom-call(s32[4]{0:T(128)S(1)} %pad_add_fusion.at, bf16[192,768]{1,0:T(8,128)(2,1)S(1)} %get-tuple-element.37.dg.refs_4_, bf16[192,768]{1,0:T(8,128)(2,1)S(1)} %get-tuple-element.38.du.refs_4_, bf16[4096,1536]{1,0:T(8,128)(2,1)} %bitcast.42, ...), custom_call_target="tpu_custom_call" | custom-call | flops 2415919104 | bytes 12582912 | tf_op jit(solution)/shard_map/pallas_call | solution.py:157
  89.7 2.2 %shard_map.91 = (f32[256,768]{1,0:T(8,128)S(1)}, bf16[256,768]{1,0:T(8,128)(2,1)S(1)}, bf16[256,768]{1,0:T(8,128)(2,1)S(1)}, bf16[256,768]{1,0:T(8,128)(2,1)S(1)}) custom-call(s32[4]{0:T(128)S(1)} %pad_add_fusion.at, bf16[192,1024]{1,0:T(8,128)(2,1)S(1)} %copy-done.18, bf16[192,1024]{1,0:T(8,128)(2,1)S(1)} %copy-done.14, ...), custom_call_target="tpu_custom_call" | custom-call | flops 1207959552 | bytes 2752512 | tf_op jit(solution)/shard_map/pallas_call | solution.py:195
  92.0 2.0 %collective-permute-start.12 = (bf16[256,768]{1,0:T(8,128)(2,1)S(1)}, bf16[256,768]{1,0:T(8,128)(2,1)S(1)}, u32[]{:S(2)}, u32[]{:S(2)}) collective-permute-start(bf16[256,768]{1,0:T(8,128)(2,1)S(1)} %get-tuple-element.42), channel_id=1, source_target_pairs={{0,4},{4,8},{8,12},{12,0},{1,5},{5,9},{9,13},{13,1},{2,6},{6,10},{... | collective-permute-start | bytes 1179656 | tf_op jit(solution)/shard_map/ppermute | solution.py:26
  94.0 2.7 %collective-permute-start.13 = (bf16[256,768]{1,0:T(8,128)(2,1)S(1)}, bf16[256,768]{1,0:T(8,128)(2,1)S(1)}, u32[]{:S(2)}, u32[]{:S(2)}) collective-permute-start(bf16[256,768]{1,0:T(8,128)(2,1)S(1)} %get-tuple-element.43), channel_id=1, source_target_pairs={{0,8},{4,12},{8,0},{12,4},{1,9},{5,13},{9,1},{13,5},{2,10},{6,14},... | collective-permute-start | bytes 1179656 | tf_op jit(solution)/shard_map/ppermute | solution.py:26
  98.1 2.7 %shard_map.93 = (f32[256,768]{1,0:T(8,128)S(1)}, bf16[256,768]{1,0:T(8,128)(2,1)}, bf16[256,768]{1,0:T(8,128)(2,1)}, bf16[256,768]{1,0:T(8,128)(2,1)}) custom-call(s32[4]{0:T(128)S(1)} %pad_add_fusion.at, bf16[192,1024]{1,0:T(8,128)(2,1)S(1)} %copy-done.18, bf16[192,1024]{1,0:T(8,128)(2,1)S(1)} %copy-done.14, ...), custom_call_target="tpu_custom_call" | custom-call | flops 1207959552 | bytes 2752512 | tf_op jit(solution)/shard_map/pallas_call | solution.py:195
  102.3 3.7 %collective-permute-done.12.refs_1_ = bf16[256,768]{1,0:T(8,128)(2,1)S(1)} collective-permute-done((bf16[256,768]{1,0:T(8,128)(2,1)S(1)}, bf16[256,768]{1,0:T(8,128)(2,1)S(1)}, u32[]{:S(2)}, u32[]{:S(2)}) %collective-permute-start.12) | collective-permute-done | bytes 393248 | tf_op jit(solution)/shard_map/ppermute | solution.py:26
  107.2 7.9 %collective-permute-done.13.refs_2_ = bf16[256,768]{1,0:T(8,128)(2,1)S(1)} collective-permute-done((bf16[256,768]{1,0:T(8,128)(2,1)S(1)}, bf16[256,768]{1,0:T(8,128)(2,1)S(1)}, u32[]{:S(2)}, u32[]{:S(2)}) %collective-permute-start.13) | collective-permute-done | bytes 393248 | tf_op jit(solution)/shard_map/ppermute | solution.py:26
  118.2 4.6 %shard_map.95 = (f32[192,1024]{1,0:T(8,128)S(1)}, bf16[192,1024]{1,0:T(8,128)(2,1)}, bf16[192,1024]{1,0:T(8,128)(2,1)}, bf16[192,1024]{1,0:T(8,128)(2,1)}) custom-call(s32[4]{0:T(128)S(1)} %pad_add_fusion.at, bf16[4,192,1792]{2,1,0:T(8,128)(2,1)} %all-to-all-done.1.both, f32[256,768]{1,0:T(8,128)S(1)} %get-tuple-element.47.refs_0_.rest_0_), custom_call_target="tpu_custom_call" | custom-call | flops 1207959552 | bytes 2752512 | tf_op jit(solution)/shard_map/pallas_call | solution.py:224
  123.7 1.8 %collective-permute-start.23 = (bf16[192,1024]{1,0:T(8,128)(2,1)}, bf16[192,1024]{1,0:T(8,128)(2,1)}, u32[]{:S(2)}, u32[]{:S(2)}) collective-permute-start(bf16[192,1024]{1,0:T(8,128)(2,1)} %get-tuple-element.54), channel_id=1, source_target_pairs={{0,16},{16,32},{32,48},{48,0},{1,17},{17,33},{33,49},{49,1},{2,18}... | collective-permute-start | bytes 1179656 | tf_op jit(solution)/shard_map/ppermute | solution.py:26
  127.0 2.7 %collective-permute-start.25 = (bf16[192,1024]{1,0:T(8,128)(2,1)}, bf16[192,1024]{1,0:T(8,128)(2,1)}, u32[]{:S(2)}, u32[]{:S(2)}) collective-permute-start(bf16[192,1024]{1,0:T(8,128)(2,1)} %get-tuple-element.56), channel_id=1, source_target_pairs={{0,48},{16,0},{32,16},{48,32},{1,49},{17,1},{33,17},{49,33},{2,50}... | collective-permute-start | bytes 1179656 | tf_op jit(solution)/shard_map/ppermute | solution.py:26
  129.7 4.9 %all-to-all-start = ((bf16[4,48,4096]{2,1,0:T(8,128)(2,1)}), bf16[4,48,4096]{2,1,0:T(8,128)(2,1)S(1)}, u32[]{:S(2)}, u32[]{:S(2)}) async-start(bf16[4,48,4096]{2,1,0:T(8,128)(2,1)} %shard_map.89.refs_8_), calls=%async_computation | async-start | bytes 3145728 | tf_op jit(solution)/shard_map/all_to_all | solution.py:309
  140.4 2.1 %collective-permute-start.26 = (bf16[96,1024]{1,0:T(8,128)(2,1)S(1)}, bf16[96,1024]{1,0:T(8,128)(2,1)S(1)}, u32[]{:S(2)}, u32[]{:S(2)}) collective-permute-start(bf16[96,1024]{1,0:T(8,128)(2,1)S(1)} %get-tuple-element.58), channel_id=1, source_target_pairs={{0,64},{64,0},{1,65},{65,1},{2,66},{66,2},{3,67},{67,3},{4,68},{68... | collective-permute-start | bytes 589832 | tf_op jit(solution)/shard_map/ppermute | solution.py:30
  142.5 14.7 %collective-permute-done.22 = bf16[128,768]{1,0:T(8,128)(2,1)S(1)} collective-permute-done((bf16[128,768]{1,0:T(8,128)(2,1)S(1)}, bf16[128,768]{1,0:T(8,128)(2,1)S(1)}, u32[]{:S(2)}, u32[]{:S(2)}) %collective-permute-start.22) | collective-permute-done | bytes 196640 | tf_op jit(solution)/shard_map/ppermute | solution.py:30
  157.2 4.0 %collective-permute-done.26 = bf16[96,1024]{1,0:T(8,128)(2,1)S(1)} collective-permute-done((bf16[96,1024]{1,0:T(8,128)(2,1)S(1)}, bf16[96,1024]{1,0:T(8,128)(2,1)S(1)}, u32[]{:S(2)}, u32[]{:S(2)}) %collective-permute-start.26) | collective-permute-done | bytes 196640 | tf_op jit(solution)/shard_map/ppermute | solution.py:30
  161.3 2.0 %collective-permute-start.27 = (bf16[24,1024]{1,0:T(8,128)(2,1)S(1)}, bf16[24,1024]{1,0:T(8,128)(2,1)S(1)}, u32[]{:S(2)}, u32[]{:S(2)}) collective-permute-start(bf16[24,1024]{1,0:T(8,128)(2,1)S(1)} %get-tuple-element.75), channel_id=1, source_target_pairs={{0,12},{4,0},{8,4},{12,8},{1,13},{5,1},{9,5},{13,9},{2,14},{6,2},{... | collective-permute-start | bytes 147464 | tf_op jit(solution)/shard_map/ppermute | solution.py:26
  164.1 1.9 %shard_map.90 = bf16[128,4096]{1,0:T(8,128)(2,1)} custom-call(s32[4]{0:T(128)S(1)} %pad_add_fusion.at, bf16[128,192]{1,0:T(8,128)(2,1)S(1)} %get-tuple-element.59.mask, bf16[4,48,4096]{2,1,0:T(8,128)(2,1)S(1)} %all-to-all-done.arrived), custom_call_target="tpu_custom_call" | custom-call | flops 201326592 | bytes 2621440 | tf_op jit(solution)/shard_map/pallas_call | solution.py:310
  167.9 3.7 %collective-permute-done.28 = bf16[24,1024]{1,0:T(8,128)(2,1)S(1)} collective-permute-done((bf16[24,1024]{1,0:T(8,128)(2,1)S(1)}, bf16[24,1024]{1,0:T(8,128)(2,1)S(1)}, u32[]{:S(2)}, u32[]{:S(2)}) %collective-permute-start.28) | collective-permute-done | bytes 49184 | tf_op jit(solution)/shard_map/ppermute | solution.py:26
  (127 shorter events, 35.3 us)
Async XLA Ops:
  4.0 9.7 %collective-permute-start.3 = (bf16[48,4096]{1,0:T(8,128)(2,1)S(1)}, bf16[48,4096]{1,0:T(8,128)(2,1)S(1)}, u32[]{:S(2)}, u32[]{:S(2)}) collective-permute-start(bf16[48,4096]{1,0:T(8,128)(2,1)S(1)} %get-tuple-element.63), channel_id=1, source_target_pairs={{0,1},{1,0},{2,3},{3,2},{4,5},{5,4},{6,7},{7,6},{8,9},{9,8},{10,11... | collective-permute-start | bytes 1179656 | tf_op jit(solution)/shard_map/ppermute | solution.py:20
  4.0 14.2 %collective-permute-start.4 = (bf16[48,4096]{1,0:T(8,128)(2,1)}, bf16[48,4096]{1,0:T(8,128)(2,1)}, u32[]{:S(2)}, u32[]{:S(2)}) collective-permute-start(bf16[48,4096]{1,0:T(8,128)(2,1)} %get-tuple-element.62), channel_id=1, source_target_pairs={{0,2},{1,3},{2,0},{3,1},{4,6},{5,7},{6,4},{7,5},{8,10},{9,11},{10,... | collective-permute-start | bytes 1179656 | tf_op jit(solution)/shard_map/ppermute | solution.py:20
  7.9 18.3 %collective-permute-start.5 = (bf16[48,4096]{1,0:T(8,128)(2,1)}, bf16[48,4096]{1,0:T(8,128)(2,1)}, u32[]{:S(2)}, u32[]{:S(2)}) collective-permute-start(bf16[48,4096]{1,0:T(8,128)(2,1)} %get-tuple-element.61), channel_id=1, source_target_pairs={{0,3},{1,2},{2,1},{3,0},{4,7},{5,6},{6,5},{7,4},{8,11},{9,10},{10,... | collective-permute-start | bytes 1179656 | tf_op jit(solution)/shard_map/ppermute | solution.py:20
  10.0 29.1 %collective-permute-start = (bf16[48,4096]{1,0:T(8,128)(2,1)}, bf16[48,4096]{1,0:T(8,128)(2,1)S(1)}, u32[]{:S(2)}, u32[]{:S(2)}) collective-permute-start(bf16[48,4096]{1,0:T(8,128)(2,1)} %get-tuple-element.67), channel_id=1, source_target_pairs={{0,1},{1,0},{2,3},{3,2},{4,5},{5,4},{6,7},{7,6},{8,9},{9,8},{10,11... | collective-permute-start | bytes 1179656 | tf_op jit(solution)/shard_map/ppermute | solution.py:20
  10.1 29.0 %collective-permute-start.1 = (bf16[48,4096]{1,0:T(8,128)(2,1)}, bf16[48,4096]{1,0:T(8,128)(2,1)S(1)}, u32[]{:S(2)}, u32[]{:S(2)}) collective-permute-start(bf16[48,4096]{1,0:T(8,128)(2,1)} %get-tuple-element.66), channel_id=1, source_target_pairs={{0,2},{1,3},{2,0},{3,1},{4,6},{5,7},{6,4},{7,5},{8,10},{9,11},{10,... | collective-permute-start | bytes 1179656 | tf_op jit(solution)/shard_map/ppermute | solution.py:20
  13.6 29.4 %collective-permute-start.2 = (bf16[48,4096]{1,0:T(8,128)(2,1)}, bf16[48,4096]{1,0:T(8,128)(2,1)S(1)}, u32[]{:S(2)}, u32[]{:S(2)}) collective-permute-start(bf16[48,4096]{1,0:T(8,128)(2,1)} %get-tuple-element.65), channel_id=1, source_target_pairs={{0,3},{1,2},{2,1},{3,0},{4,7},{5,6},{6,5},{7,4},{8,11},{9,10},{10,... | collective-permute-start | bytes 1179656 | tf_op jit(solution)/shard_map/ppermute | solution.py:20
  28.4 14.6 %collective-permute-start.6 = (bf16[192,1024]{1,0:T(8,128)(2,1)S(1)}, bf16[192,1024]{1,0:T(8,128)(2,1)S(1)}, u32[]{:S(2)}, u32[]{:S(2)}) collective-permute-start(bf16[192,1024]{1,0:T(8,128)(2,1)S(1)} %get-tuple-element.35), channel_id=1, source_target_pairs={{0,16},{16,32},{32,48},{48,0},{1,17},{17,33},{33,49},{49,1},{2,18}... | collective-permute-start | bytes 1179656 | tf_op jit(solution)/shard_map/ppermute | solution.py:26
  29.9 13.1 %collective-permute-start.7 = (bf16[192,1024]{1,0:T(8,128)(2,1)S(1)}, bf16[192,1024]{1,0:T(8,128)(2,1)S(1)}, u32[]{:S(2)}, u32[]{:S(2)}) collective-permute-start(bf16[192,1024]{1,0:T(8,128)(2,1)S(1)} %get-tuple-element.36), channel_id=1, source_target_pairs={{0,48},{16,0},{32,16},{48,32},{1,49},{17,1},{33,17},{49,33},{2,50}... | collective-permute-start | bytes 1179656 | tf_op jit(solution)/shard_map/ppermute | solution.py:26
  46.3 72.0 %all-to-all-start.1 = ((bf16[4,192,1792]{2,1,0:T(8,128)(2,1)}), bf16[4,192,1792]{2,1,0:T(8,128)(2,1)}, u32[]{:S(2)}, u32[]{:S(2)}) async-start(bf16[4,192,1792]{2,1,0:T(8,128)(2,1)} %copy-done.1), calls=%async_computation.1 | async-start | bytes 5505024 | tf_op jit(solution)/shard_map/all_to_all | solution.py:298
  50.9 15.7 %collective-permute-start.9 = (bf16[192,1024]{1,0:T(8,128)(2,1)}, bf16[192,1024]{1,0:T(8,128)(2,1)S(1)}, u32[]{:S(2)}, u32[]{:S(2)}) collective-permute-start(bf16[192,1024]{1,0:T(8,128)(2,1)} %copy-done.19), channel_id=1, source_target_pairs={{0,32},{16,48},{32,0},{48,16},{1,33},{17,49},{33,1},{49,17},{2,34}... | collective-permute-start | bytes 1179656 | tf_op jit(solution)/shard_map/ppermute | solution.py:26
  61.9 17.5 %collective-permute-start.8 = (bf16[192,768]{1,0:T(8,128)(2,1)S(1)}, bf16[192,768]{1,0:T(8,128)(2,1)S(1)}, u32[]{:S(2)}, u32[]{:S(2)}) collective-permute-start(bf16[192,768]{1,0:T(8,128)(2,1)S(1)} %get-tuple-element.37.dg.refs_4_), channel_id=1, source_target_pairs={{0,16},{16,32},{32,48},{48,0},{1,17},{17,33},{33,49},{49,1},{2,18}... | collective-permute-start | bytes 884744 | tf_op jit(solution)/shard_map/ppermute | solution.py:26
  62.5 27.2 %collective-permute-start.10 = (bf16[192,768]{1,0:T(8,128)(2,1)S(1)}, bf16[192,768]{1,0:T(8,128)(2,1)S(1)}, u32[]{:S(2)}, u32[]{:S(2)}) collective-permute-start(bf16[192,768]{1,0:T(8,128)(2,1)S(1)} %get-tuple-element.37.dg.refs_4_), channel_id=1, source_target_pairs={{0,32},{16,48},{32,0},{48,16},{1,33},{17,49},{33,1},{49,17},{2,34}... | collective-permute-start | bytes 884744 | tf_op jit(solution)/shard_map/ppermute | solution.py:26
  64.5 25.2 %collective-permute-start.11 = (bf16[192,768]{1,0:T(8,128)(2,1)S(1)}, bf16[192,768]{1,0:T(8,128)(2,1)S(1)}, u32[]{:S(2)}, u32[]{:S(2)}) collective-permute-start(bf16[192,768]{1,0:T(8,128)(2,1)S(1)} %get-tuple-element.37.dg.refs_4_), channel_id=1, source_target_pairs={{0,48},{16,0},{32,16},{48,32},{1,49},{17,1},{33,17},{49,33},{2,50}... | collective-permute-start | bytes 884744 | tf_op jit(solution)/shard_map/ppermute | solution.py:26
  65.3 31.3 %collective-permute-start.16 = (bf16[192,768]{1,0:T(8,128)(2,1)S(1)}, bf16[192,768]{1,0:T(8,128)(2,1)S(1)}, u32[]{:S(2)}, u32[]{:S(2)}) collective-permute-start(bf16[192,768]{1,0:T(8,128)(2,1)S(1)} %get-tuple-element.38.du.refs_4_), channel_id=1, source_target_pairs={{0,16},{16,32},{32,48},{48,0},{1,17},{17,33},{33,49},{49,1},{2,18}... | collective-permute-start | bytes 884744 | tf_op jit(solution)/shard_map/ppermute | solution.py:26
  66.6 31.5 %collective-permute-start.17 = (bf16[192,768]{1,0:T(8,128)(2,1)S(1)}, bf16[192,768]{1,0:T(8,128)(2,1)S(1)}, u32[]{:S(2)}, u32[]{:S(2)}) collective-permute-start(bf16[192,768]{1,0:T(8,128)(2,1)S(1)} %get-tuple-element.38.du.refs_4_), channel_id=1, source_target_pairs={{0,32},{16,48},{32,0},{48,16},{1,33},{17,49},{33,1},{49,17},{2,34}... | collective-permute-start | bytes 884744 | tf_op jit(solution)/shard_map/ppermute | solution.py:26
  79.4 18.8 %collective-permute-start.18 = (bf16[192,768]{1,0:T(8,128)(2,1)S(1)}, bf16[192,768]{1,0:T(8,128)(2,1)S(1)}, u32[]{:S(2)}, u32[]{:S(2)}) collective-permute-start(bf16[192,768]{1,0:T(8,128)(2,1)S(1)} %get-tuple-element.38.du.refs_4_), channel_id=1, source_target_pairs={{0,48},{16,0},{32,16},{48,32},{1,49},{17,1},{33,17},{49,33},{2,50}... | collective-permute-start | bytes 884744 | tf_op jit(solution)/shard_map/ppermute | solution.py:26
  92.0 14.1 %collective-permute-start.12 = (bf16[256,768]{1,0:T(8,128)(2,1)S(1)}, bf16[256,768]{1,0:T(8,128)(2,1)S(1)}, u32[]{:S(2)}, u32[]{:S(2)}) collective-permute-start(bf16[256,768]{1,0:T(8,128)(2,1)S(1)} %get-tuple-element.42), channel_id=1, source_target_pairs={{0,4},{4,8},{8,12},{12,0},{1,5},{5,9},{9,13},{13,1},{2,6},{6,10},{... | collective-permute-start | bytes 1179656 | tf_op jit(solution)/shard_map/ppermute | solution.py:26
  94.0 21.0 %collective-permute-start.13 = (bf16[256,768]{1,0:T(8,128)(2,1)S(1)}, bf16[256,768]{1,0:T(8,128)(2,1)S(1)}, u32[]{:S(2)}, u32[]{:S(2)}) collective-permute-start(bf16[256,768]{1,0:T(8,128)(2,1)S(1)} %get-tuple-element.43), channel_id=1, source_target_pairs={{0,8},{4,12},{8,0},{12,4},{1,9},{5,13},{9,1},{13,5},{2,10},{6,14},... | collective-permute-start | bytes 1179656 | tf_op jit(solution)/shard_map/ppermute | solution.py:26
  96.6 18.4 %collective-permute-start.14 = (bf16[256,768]{1,0:T(8,128)(2,1)S(1)}, bf16[256,768]{1,0:T(8,128)(2,1)S(1)}, u32[]{:S(2)}, u32[]{:S(2)}) collective-permute-start(bf16[256,768]{1,0:T(8,128)(2,1)S(1)} %get-tuple-element.44), channel_id=1, source_target_pairs={{0,12},{4,0},{8,4},{12,8},{1,13},{5,1},{9,5},{13,9},{2,14},{6,2},{... | collective-permute-start | bytes 1179656 | tf_op jit(solution)/shard_map/ppermute | solution.py:26
  100.8 24.7 %collective-permute-start.19 = (bf16[256,768]{1,0:T(8,128)(2,1)}, bf16[256,768]{1,0:T(8,128)(2,1)S(1)}, u32[]{:S(2)}, u32[]{:S(2)}) collective-permute-start(bf16[256,768]{1,0:T(8,128)(2,1)} %get-tuple-element.48), channel_id=1, source_target_pairs={{0,4},{4,8},{8,12},{12,0},{1,5},{5,9},{9,13},{13,1},{2,6},{6,10},{... | collective-permute-start | bytes 1179656 | tf_op jit(solution)/shard_map/ppermute | solution.py:26
  101.4 24.9 %collective-permute-start.20 = (bf16[256,768]{1,0:T(8,128)(2,1)}, bf16[256,768]{1,0:T(8,128)(2,1)S(1)}, u32[]{:S(2)}, u32[]{:S(2)}) collective-permute-start(bf16[256,768]{1,0:T(8,128)(2,1)} %get-tuple-element.49), channel_id=1, source_target_pairs={{0,8},{4,12},{8,0},{12,4},{1,9},{5,13},{9,1},{13,5},{2,10},{6,14},... | collective-permute-start | bytes 1179656 | tf_op jit(solution)/shard_map/ppermute | solution.py:26
  106.0 28.5 %collective-permute-start.21 = (bf16[256,768]{1,0:T(8,128)(2,1)}, bf16[256,768]{1,0:T(8,128)(2,1)}, u32[]{:S(2)}, u32[]{:S(2)}) collective-permute-start(bf16[256,768]{1,0:T(8,128)(2,1)} %get-tuple-element.50), channel_id=1, source_target_pairs={{0,12},{4,0},{8,4},{12,8},{1,13},{5,1},{9,5},{13,9},{2,14},{6,2},{... | collective-permute-start | bytes 1179656 | tf_op jit(solution)/shard_map/ppermute | solution.py:26
  117.2 20.8 %collective-permute-start.15 = (bf16[128,768]{1,0:T(8,128)(2,1)}, bf16[128,768]{1,0:T(8,128)(2,1)}, u32[]{:S(2)}, u32[]{:S(2)}) collective-permute-start(bf16[128,768]{1,0:T(8,128)(2,1)} %get-tuple-element.46), channel_id=1, source_target_pairs={{0,64},{64,0},{1,65},{65,1},{2,66},{66,2},{3,67},{67,3},{4,68},{68... | collective-permute-start | bytes 589832 | tf_op jit(solution)/shard_map/ppermute | solution.py:30
  123.7 15.2 %collective-permute-start.23 = (bf16[192,1024]{1,0:T(8,128)(2,1)}, bf16[192,1024]{1,0:T(8,128)(2,1)}, u32[]{:S(2)}, u32[]{:S(2)}) collective-permute-start(bf16[192,1024]{1,0:T(8,128)(2,1)} %get-tuple-element.54), channel_id=1, source_target_pairs={{0,16},{16,32},{32,48},{48,0},{1,17},{17,33},{33,49},{49,1},{2,18}... | collective-permute-start | bytes 1179656 | tf_op jit(solution)/shard_map/ppermute | solution.py:26
  126.3 12.7 %collective-permute-start.24 = (bf16[192,1024]{1,0:T(8,128)(2,1)}, bf16[192,1024]{1,0:T(8,128)(2,1)}, u32[]{:S(2)}, u32[]{:S(2)}) collective-permute-start(bf16[192,1024]{1,0:T(8,128)(2,1)} %get-tuple-element.55), channel_id=1, source_target_pairs={{0,32},{16,48},{32,0},{48,16},{1,33},{17,49},{33,1},{49,17},{2,34}... | collective-permute-start | bytes 1179656 | tf_op jit(solution)/shard_map/ppermute | solution.py:26
  127.0 11.9 %collective-permute-start.25 = (bf16[192,1024]{1,0:T(8,128)(2,1)}, bf16[192,1024]{1,0:T(8,128)(2,1)}, u32[]{:S(2)}, u32[]{:S(2)}) collective-permute-start(bf16[192,1024]{1,0:T(8,128)(2,1)} %get-tuple-element.56), channel_id=1, source_target_pairs={{0,48},{16,0},{32,16},{48,32},{1,49},{17,1},{33,17},{49,33},{2,50}... | collective-permute-start | bytes 1179656 | tf_op jit(solution)/shard_map/ppermute | solution.py:26
  129.7 34.4 %all-to-all-start = ((bf16[4,48,4096]{2,1,0:T(8,128)(2,1)}), bf16[4,48,4096]{2,1,0:T(8,128)(2,1)S(1)}, u32[]{:S(2)}, u32[]{:S(2)}) async-start(bf16[4,48,4096]{2,1,0:T(8,128)(2,1)} %shard_map.89.refs_8_), calls=%async_computation | async-start | bytes 3145728 | tf_op jit(solution)/shard_map/all_to_all | solution.py:309
  137.8 19.3 %collective-permute-start.22 = (bf16[128,768]{1,0:T(8,128)(2,1)S(1)}, bf16[128,768]{1,0:T(8,128)(2,1)S(1)}, u32[]{:S(2)}, u32[]{:S(2)}) collective-permute-start(bf16[128,768]{1,0:T(8,128)(2,1)S(1)} %get-tuple-element.52), channel_id=1, source_target_pairs={{0,64},{64,0},{1,65},{65,1},{2,66},{66,2},{3,67},{67,3},{4,68},{68... | collective-permute-start | bytes 589832 | tf_op jit(solution)/shard_map/ppermute | solution.py:30
  140.4 20.8 %collective-permute-start.26 = (bf16[96,1024]{1,0:T(8,128)(2,1)S(1)}, bf16[96,1024]{1,0:T(8,128)(2,1)S(1)}, u32[]{:S(2)}, u32[]{:S(2)}) collective-permute-start(bf16[96,1024]{1,0:T(8,128)(2,1)S(1)} %get-tuple-element.58), channel_id=1, source_target_pairs={{0,64},{64,0},{1,65},{65,1},{2,66},{66,2},{3,67},{67,3},{4,68},{68... | collective-permute-start | bytes 589832 | tf_op jit(solution)/shard_map/ppermute | solution.py:30
  161.3 6.7 %collective-permute-start.27 = (bf16[24,1024]{1,0:T(8,128)(2,1)S(1)}, bf16[24,1024]{1,0:T(8,128)(2,1)S(1)}, u32[]{:S(2)}, u32[]{:S(2)}) collective-permute-start(bf16[24,1024]{1,0:T(8,128)(2,1)S(1)} %get-tuple-element.75), channel_id=1, source_target_pairs={{0,12},{4,0},{8,4},{12,8},{1,13},{5,1},{9,5},{13,9},{2,14},{6,2},{... | collective-permute-start | bytes 147464 | tf_op jit(solution)/shard_map/ppermute | solution.py:26
  166.0 5.6 %collective-permute-start.28 = (bf16[24,1024]{1,0:T(8,128)(2,1)S(1)}, bf16[24,1024]{1,0:T(8,128)(2,1)S(1)}, u32[]{:S(2)}, u32[]{:S(2)}) collective-permute-start(bf16[24,1024]{1,0:T(8,128)(2,1)S(1)} %get-tuple-element.74), channel_id=1, source_target_pairs={{0,8},{4,12},{8,0},{12,4},{1,9},{5,13},{9,1},{13,5},{2,10},{6,14},... | collective-permute-start | bytes 147464 | tf_op jit(solution)/shard_map/ppermute | solution.py:26
  167.2 5.3 %collective-permute-start.29 = (bf16[24,1024]{1,0:T(8,128)(2,1)S(1)}, bf16[24,1024]{1,0:T(8,128)(2,1)S(1)}, u32[]{:S(2)}, u32[]{:S(2)}) collective-permute-start(bf16[24,1024]{1,0:T(8,128)(2,1)S(1)} %get-tuple-element.73), channel_id=1, source_target_pairs={{0,4},{4,8},{8,12},{12,0},{1,5},{5,9},{9,13},{13,1},{2,6},{6,10},{... | collective-permute-start | bytes 147464 | tf_op jit(solution)/shard_map/ppermute | solution.py:26
  (23 other events, 114.4 us)

commit v4 on v3

--- a/solution.py
+++ b/solution.py
@@ -77,97 +77,117 @@
         out[i, :, part:] = hidden[...]
 
 
-def act_step(x, wg, wu, hidden, slope, silu):
-    gpart = jnp.dot(x[...], wg[...], preferred_element_type=F32)
-    upart = jnp.dot(x[...], wu[...], preferred_element_type=F32)
-    sig = jax.nn.sigmoid(gpart)
-    soft = gpart * sig
-    hidden[...] = (soft * upart).astype(BF)
-    slope[...] = upart * (sig * (1.0 + gpart * (1.0 - sig)))
-    silu[...] = soft
+def fetch(pieces, buf, sems):
+    copies = [
+        pltpu.make_async_copy(piece, buf.at[i], sems.at[i]) for i, piece in enumerate(pieces)
+    ]
+    for copy in copies:
+        copy.start()
+    return copies
+
+
+def act_step(x, weights, hidden, slope, silu, buf, sems):
+    inner = hidden.shape[1]
+    step = buf.shape[2]
+    n = inner // step
+    copies = fetch(
+        [weights.at[:, pl.ds(h * inner + i * step, step)] for i in range(n) for h in range(2)],
+        buf,
+        sems,
+    )
+    for i in range(n):
+        cols = slice(i * step, i * step + step)
+        copies[2 * i].wait()
+        gpart = jnp.dot(x[...], buf[2 * i], preferred_element_type=F32)
+        copies[2 * i + 1].wait()
+        upart = jnp.dot(x[...], buf[2 * i + 1], preferred_element_type=F32)
+        sig = jax.nn.sigmoid(gpart)
+        soft = gpart * sig
+        hidden[:, cols] = (soft * upart).astype(BF)
+        slope[:, cols] = upart * (sig * (1.0 + gpart * (1.0 - sig)))
+        silu[:, cols] = soft
+
+
+def weigh(body, outs, ins, weights, scratch, flops, limit, after, scalars=0):
+    return pl.pallas_call(
+        body,
+        out_shape=outs,
+        in_specs=[SMEM] * scalars
+        + [VMEM] * ins
+        + [pl.BlockSpec(memory_space=pltpu.HBM)]
+        + [pl.BlockSpec(memory_space=pl.ANY)] * after,
+        out_specs=[VMEM] * len(outs),
+        scratch_shapes=scratch,
+        compiler_params=pltpu.CompilerParams(vmem_limit_bytes=limit * MB),
+        cost_estimate=pl.CostEstimate(
+            flops=flops, bytes_accessed=2 * weights.size, transcendentals=0
+        ),
+    )
 
 
 def act_call(X, gate_up, inner):
     rows, width = X.shape
     step = 256
-    n = inner // step
-    out = pl.BlockSpec((rows, step), lambda i: (0, i))
-    return pl.pallas_call(
-        act_step,
-        grid=(n,),
-        in_specs=[
-            pl.BlockSpec((rows, width), lambda i: (0, 0)),
-            pl.BlockSpec((width, step), lambda i: (0, i)),
-            pl.BlockSpec((width, step), lambda i: (0, i + n)),
-        ],
-        out_specs=[out, out, out],
-        out_shape=[shape(rows, inner), shape(rows, inner, F32), shape(rows, inner, F32)],
-        compiler_params=pltpu.CompilerParams(vmem_limit_bytes=48 * MB),
-        cost_estimate=pl.CostEstimate(
-            flops=4 * rows * width * inner, bytes_accessed=4 * width * inner, transcendentals=0
-        ),
-    )(X, gate_up, gate_up)
-
-
-def dh_step(g0, g1, g2, g3, wd, slope, silu, *rest):
-    dact_g, dact_u, whole = rest[-3:]
-
-    @pl.when(pl.program_id(0) == 0)
-    def _():
-        for k, piece in enumerate((g0, g1, g2, g3)):
-            whole[k * CAP : k * CAP + CAP, :] = piece[...]
-
-    dh = wide_dot(whole[...], wd[...])
-    dact_g[...] = (dh * slope[...]).astype(BF)
-    dact_u[...] = (dh * silu[...]).astype(BF)
+    n = 2 * inner // step
+    outs = [shape(rows, inner), shape(rows, inner, F32), shape(rows, inner, F32)]
+    scratch = [pltpu.VMEM((n, width, step), BF), pltpu.SemaphoreType.DMA((n,))]
+    flops = 4 * rows * width * inner
+    return weigh(act_step, outs, 1, gate_up, scratch, flops, 18, 0)(X, gate_up)
+
+
+def dh_step(g0, g1, g2, g3, slope, silu, weights, *rest):
+    dact_g, dact_u, whole, buf, sems = rest[-5:]
+    step = buf.shape[1]
+    n = buf.shape[0]
+    copies = fetch([weights.at[pl.ds(i * step, step), :] for i in range(n)], buf, sems)
+    for k, piece in enumerate((g0, g1, g2, g3)):
+        whole[k * CAP : k * CAP + CAP, :] = piece[...]
+    for i in range(n):
+        cols = slice(i * step, i * step + step)
+        copies[i].wait()
+        dh = wide_dot(whole[...], buf[i])
+        dact_g[:, cols] = (dh * slope[:, cols]).astype(BF)
+        dact_u[:, cols] = (dh * silu[:, cols]).astype(BF)
 
 
 def dh_call(gs, down_proj, slope, silu, after):
     inner, width = down_proj.shape
     rows = slope.shape[0]
     step = 256
-    part = pl.BlockSpec((rows, step), lambda i: (0, i))
-    return pl.pallas_call(
-        dh_step,
-        grid=(inner // step,),
-        in_specs=[pl.BlockSpec((CAP, width), lambda i: (0, 0))] * 4
-        + [pl.BlockSpec((step, width), lambda i: (i, 0)), part, part]
-        + [pl.BlockSpec(memory_space=pl.ANY)] * len(after),
-        out_specs=[part, part],
-        out_shape=[shape(rows, inner)] * 2,
-        scratch_shapes=[pltpu.VMEM((rows, width), BF)],
-        compiler_params=pltpu.CompilerParams(vmem_limit_bytes=48 * MB),
-        cost_estimate=pl.CostEstimate(
-            flops=2 * rows * width * inner, bytes_accessed=2 * width * inner, transcendentals=0
-        ),
-    )(*gs, down_proj, slope, silu, *after)
-
-
-def back_step(at, dg, du, wt, *rest):
-    out, inner = rest[-1], dg.shape[1]
-    got = wide_dot(dg[...], wt[:, :inner]) + wide_dot(du[...], wt[:, inner:])
-    for k in range(4):
-        out[jnp.bitwise_xor(at[3], k)] = got[k * CAP : k * CAP + CAP].astype(BF)
-
-
-def back_call(at, dg, du, gate_up, after):
+    n = inner // step
+    scratch = [
+        pltpu.VMEM((rows, width), BF),
+        pltpu.VMEM((n, step, width), BF),
+        pltpu.SemaphoreType.DMA((n,)),
+    ]
+    flops = 2 * rows * width * inner
+    return weigh(dh_step, [shape(rows, inner)] * 2, 6, down_proj, scratch, flops, 14, len(after))(
+        *gs, slope, silu, down_proj, *after
+    )
+
+
+def back_step(at, dg, du, weights, out, passed, buf, sems):
+    inner, step, n = dg.shape[1], buf.shape[1], buf.shape[0]
+    copies = fetch([weights.at[pl.ds(i * step, step), :] for i in range(n)], buf, sems)
+    passed[...] = du[...]
+    for i in range(n):
+        copies[i].wait()
+        got = wide_dot(dg[...], buf[i, :, :inner]) + wide_dot(du[...], buf[i, :, inner:])
+        for k in range(4):
+            out[jnp.bitwise_xor(at[3], k), :, i * step : i * step + step] = got[
+                k * CAP : k * CAP + CAP
+            ].astype(BF)
+
+
+def back_call(at, dg, du, gate_up):
     rows, inner = dg.shape
     width = gate_up.shape[0]
     step = 512
-    return pl.pallas_call(
-        back_step,
-        grid=(width // step,),
-        in_specs=[SMEM]
-        + [pl.BlockSpec((rows, inner), lambda i: (0, 0))] * 2
-        + [pl.BlockSpec((step, 2 * inner), lambda i: (i, 0))]
-        + [pl.BlockSpec(memory_space=pl.ANY)] * len(after),
-        out_specs=pl.BlockSpec((4, CAP, step), lambda i: (0, 0, i)),
-        out_shape=jax.ShapeDtypeStruct((4, CAP, width), BF),
-        compiler_params=pltpu.CompilerParams(vmem_limit_bytes=48 * MB),
-        cost_estimate=pl.CostEstimate(
-            flops=4 * rows * width * inner, bytes_accessed=4 * width * inner, transcendentals=0
-        ),
-    )(at, dg, du, gate_up, *after)
+    n = width // step
+    outs = [jax.ShapeDtypeStruct((4, CAP, width), BF), shape(rows, inner)]
+    scratch = [pltpu.VMEM((n, step, 2 * inner), BF), pltpu.SemaphoreType.DMA((n,))]
+    flops = 4 * rows * width * inner
+    return weigh(back_step, outs, 2, gate_up, scratch, flops, 18, 0, 1)(at, dg, du, gate_up)
 
 
 def tok_step(at, mask, arrived, out, whole):
@@ -294,18 +314,18 @@
     )(*gs, hidden, xa[1], xa[3])[0]
     dact_g, dact_u = dh_call(gs, down_proj, slope, silu, [sent])
     da_g = [shift(dact_g, "x", j) for j in range(4)]
-    da_u = [shift(dact_u, "x", j) for j in range(4)]
+    back, passed = back_call(at, dact_g, dact_u, gate_up)
+    da_u = [shift(passed, "x", j) for j in range(4)]
     both = lax.all_to_all(sent, "y", split_axis=0, concat_axis=0, tiled=True)
     def half(ds, after):
         parts = tile_call(at, xa, ds, after)
         return [parts[0]] + [shift(parts[j], "y", j) for j in (1, 2, 3)]
 
-    back = back_call(at, dact_g, dact_u, gate_up, [da_g[1]])
     gate = half(da_g, [back])
-    up = half(da_u, [])
-    parts = down_call(at, both, part, [up[0]])
+    parts = down_call(at, both, part, [gate[0]])
     down = [parts[0]] + [shift(parts[j], "x", j) for j in (1, 2, 3)]
 
+    up = half(da_u, [down[0]])
     arrived = lax.all_to_all(back, ("v", "c"), split_axis=0, concat_axis=0, tiled=True)
     token_grad = call(
         tok_step,
@@ -328,7 +348,7 @@
         keep, send = sum_call(at, parts, after)
         return (keep + swap_w(send).astype(F32)).astype(BF)
 
-    gate_up_grad = jnp.concatenate([last(gate, []), last(up, [])], axis=1)
+    gate_up_grad = jnp.concatenate([last(gate, []), last(up, [token_grad])], axis=1)
     return token_grad, gate_up_grad[None], down_grad[None]
 
 

time: 174 us -> 165 us (0.948)
  waiting for transfers between devices: 62.4 us -> 41.2 us
  local copies, waits for them, and re-layouts: 15.5 us -> 33.8 us
  starting transfers between devices: 50.2 us -> 44 us
    ppermute x3, waiting for transfers between devices: 18.6 us -> 0.01 us  [swap_w(): return lax.ppermute(a, 'w', [(0, 1), (1, 0)])]
    unnamed x53 -> x77, local copies, waits for them, and re-layouts: 12.8 us -> 31.1 us
    ppermute x21, starting transfers between devices: 29.9 us -> 23.8 us  [shift(): return lax.ppermute(a, axis, [(i, (i + j) % 4) for i in range(4)])]
    all_to_all x1, waiting for transfers between devices: 0.01 us -> 3.93 us  [shards(): both = lax.all_to_all(sent, 'y', split_axis=0, concat_axis=0, tiled=True)]
    ppermute x6, waiting for transfers between devices: 16.5 us -> 12.6 us  [swap_expert(): return lax.ppermute(a, ('v', 'c'), [(i, i ^ k) for i in range(4)])]
    pallas_call x3, Pallas kernels: 22 us -> 18.8 us  [the longest x1 7.52 us: back_call(): weigh(back_step, outs, 2, gate_up, scratch, flops, 18, 0, 1)]
    ppermute x21, waiting for transfers between devices: 27.3 us -> 24.6 us  [shift(): return lax.ppermute(a, axis, [(i, (i + j) % 4) for i in range(4)])]
  transfers between devices with their start and end apart: 32 -> 32, of which waited for: 10 -> 9; matrix products, arithmetic and copies ran while one was open for 2% -> 3% of each run, Pallas kernels for 22% -> 23%
where the time goes in v4:
time: 165 us; the launch traced here: 164 us
  starting transfers between devices  44 us (27%)
  waiting for transfers between devices  41.2 us (25%)
  Pallas kernels  37.6 us (23%)
  local copies, waits for them, and re-layouts  33.8 us (20%)
  other arithmetic  5.55 us (3%)
    unnamed x77, local copies, waits for them, and re-layouts  31.1 us
    ppermute x21, waiting for transfers between devices, shift(): return lax.ppermute(a, axis, [(i, (i + j) % 4) for i in range(4)])  24.6 us
    ppermute x21, starting transfers between devices, shift(): return lax.ppermute(a, axis, [(i, (i + j) % 4) for i in range(4)])  23.8 us
    ppermute x6, waiting for transfers between devices, swap_expert(): return lax.ppermute(a, ('v', 'c'), [(i, i ^ k) for i in range(4)])  12.6 us
    ppermute x6, starting transfers between devices, swap_expert(): return lax.ppermute(a, ('v', 'c'), [(i, i ^ k) for i in range(4)])  7.65 us
    pallas_call x1, Pallas kernels, back_call(): weigh(back_step, outs, 2, gate_up, scratch, flops, 18, 0, 1)  7.52 us
    pallas_call x1, Pallas kernels, act_call(): return weigh(act_step, outs, 1, gate_up, scratch, flops, 18, 0)(X, gate_up)  6.63 us
    pallas_call x2, Pallas kernels, tile_call(): call(tile_step, [shape(256, inner, F32)] + [shape(256, inner)] * 3, 9, [p...  6.47 us
  transfers between devices with their start and end apart: 32, of which 9 were waited for; matrix products, arithmetic and copies ran while one was open for 3% of the time, Pallas kernels for 23%

profile of v4, /device:TPU:0, one launch (start us, length us, event | category | flops | bytes accessed | tf_op | source)
XLA Modules:
  0.0 164.5 jit_solution(15539471067617948507)
XLA Ops:
  4.0 4.0 %collective-permute-start.4 = (bf16[48,4096]{1,0:T(8,128)(2,1)}, bf16[48,4096]{1,0:T(8,128)(2,1)}, u32[]{:S(2)}, u32[]{:S(2)}) collective-permute-start(bf16[48,4096]{1,0:T(8,128)(2,1)} %get-tuple-element.66), channel_id=1, source_target_pairs={{0,2},{1,3},{2,0},{3,1},{4,6},{5,7},{6,4},{7,5},{8,10},{9,11},{10,... | collective-permute-start | bytes 1179656 | tf_op jit(solution)/shard_map/ppermute | solution.py:20
  10.2 3.4 %collective-permute-start.1 = (bf16[48,4096]{1,0:T(8,128)(2,1)}, bf16[48,4096]{1,0:T(8,128)(2,1)S(1)}, u32[]{:S(2)}, u32[]{:S(2)}) collective-permute-start(bf16[48,4096]{1,0:T(8,128)(2,1)} %get-tuple-element.70), channel_id=1, source_target_pairs={{0,2},{1,3},{2,0},{3,1},{4,6},{5,7},{6,4},{7,5},{8,10},{9,11},{10,... | collective-permute-start | bytes 1179656 | tf_op jit(solution)/shard_map/ppermute | solution.py:20
  13.7 4.5 %collective-permute-done.4.x2 = bf16[48,4096]{1,0:T(8,128)(2,1)} collective-permute-done((bf16[48,4096]{1,0:T(8,128)(2,1)}, bf16[48,4096]{1,0:T(8,128)(2,1)}, u32[]{:S(2)}, u32[]{:S(2)}) %collective-permute-start.4) | collective-permute-done | bytes 393248 | tf_op jit(solution)/shard_map/ppermute | solution.py:20
  18.2 8.1 %collective-permute-done.5.x3 = bf16[48,4096]{1,0:T(8,128)(2,1)} collective-permute-done((bf16[48,4096]{1,0:T(8,128)(2,1)}, bf16[48,4096]{1,0:T(8,128)(2,1)}, u32[]{:S(2)}, u32[]{:S(2)}) %collective-permute-start.5) | collective-permute-done | bytes 393248 | tf_op jit(solution)/shard_map/ppermute | solution.py:20
  30.7 1.7 %collective-permute-start.7 = (bf16[192,1024]{1,0:T(8,128)(2,1)S(1)}, bf16[192,1024]{1,0:T(8,128)(2,1)S(1)}, u32[]{:S(2)}, u32[]{:S(2)}) collective-permute-start(bf16[192,1024]{1,0:T(8,128)(2,1)S(1)} %get-tuple-element.38), channel_id=1, source_target_pairs={{0,48},{16,0},{32,16},{48,32},{1,49},{17,1},{33,17},{49,33},{2,50}... | collective-permute-start | bytes 1179656 | tf_op jit(solution)/shard_map/ppermute | solution.py:26
  32.4 4.6 %copy-done.1 = bf16[1,4096,1536]{2,1,0:T(8,128)(2,1)S(1)} copy-done((bf16[1,4096,1536]{2,1,0:T(8,128)(2,1)S(1)}, bf16[1,4096,1536]{2,1,0:T(8,128)(2,1)}, u32[]{:S(2)}) %copy-start.1) | copy-done | bytes 12582936
  37.0 6.6 %shard_map.86 = (bf16[192,768]{1,0:T(8,128)(2,1)S(1)}, f32[192,768]{1,0:T(8,128)S(1)}, f32[192,768]{1,0:T(8,128)S(1)}) custom-call(bf16[192,4096]{1,0:T(8,128)(2,1)S(1)} %get-tuple-element.33.x, bf16[4096,1536]{1,0:T(8,128)(2,1)S(1)} %bitcast.40), custom_call_target="tpu_custom_call" | custom-call | flops 2415919104 | bytes 12582912 | tf_op jit(solution)/shard_map/pallas_call | solution.py:135
  44.7 1.5 copy-done.3
  47.7 4.6 %all-to-all-start.1 = ((bf16[4,192,1792]{2,1,0:T(8,128)(2,1)}), bf16[4,192,1792]{2,1,0:T(8,128)(2,1)}, u32[]{:S(2)}, u32[]{:S(2)}) async-start(bf16[4,192,1792]{2,1,0:T(8,128)(2,1)} %copy-done.3), calls=%async_computation.1 | async-start | bytes 5505024 | tf_op jit(solution)/shard_map/all_to_all | solution.py:319
  52.3 1.9 %collective-permute-start.8 = (bf16[192,1024]{1,0:T(8,128)(2,1)}, bf16[192,1024]{1,0:T(8,128)(2,1)}, u32[]{:S(2)}, u32[]{:S(2)}) collective-permute-start(bf16[192,1024]{1,0:T(8,128)(2,1)} %copy-done.30), channel_id=1, source_target_pairs={{0,32},{16,48},{32,0},{48,16},{1,33},{17,49},{33,1},{49,17},{2,34}... | collective-permute-start | bytes 1179656 | tf_op jit(solution)/shard_map/ppermute | solution.py:26
  54.2 1.8 %copy-done.4 = bf16[4,192,1792]{2,1,0:T(8,128)(2,1)S(1)} copy-done((bf16[4,192,1792]{2,1,0:T(8,128)(2,1)S(1)}, bf16[4,192,1792]{2,1,0:T(8,128)(2,1)}, u32[]{:S(2)}) %copy-start.4) | copy-done | bytes 2752536
  56.0 2.8 %copy-done.5 = bf16[1,768,4096]{2,1,0:T(8,128)(2,1)S(1)} copy-done((bf16[1,768,4096]{2,1,0:T(8,128)(2,1)S(1)}, bf16[1,768,4096]{2,1,0:T(8,128)(2,1)}, u32[]{:S(2)}) %copy-start.5) | copy-done | bytes 6291480
  59.9 4.7 %shard_map.88 = (bf16[192,768]{1,0:T(8,128)(2,1)}, bf16[192,768]{1,0:T(8,128)(2,1)S(1)}) custom-call(bf16[48,4096]{1,0:T(8,128)(2,1)S(1)} %get-tuple-element.72.g0, bf16[48,4096]{1,0:T(8,128)(2,1)S(1)} %collective-permute-done.g1, bf16[48,4096]{1,0:T(8,128)(2,1)S(1)} %collective-permute-done.1.g2, bf16[48,4096]{1,0:T(8,128)(2,1)S(1)} %collective-permute-done.2.g3, ...), custom_call_target="tpu_custom_call" | custom-call | flops 1207959552 | bytes 6291456 | tf_op jit(solution)/shard_map/pallas_call | solution.py:164
  64.5 1.8 %collective-permute-start.10 = (bf16[192,768]{1,0:T(8,128)(2,1)}, bf16[192,768]{1,0:T(8,128)(2,1)}, u32[]{:S(2)}, u32[]{:S(2)}) collective-permute-start(bf16[192,768]{1,0:T(8,128)(2,1)} %get-tuple-element.39.dg.refs_4_), channel_id=1, source_target_pairs={{0,32},{16,48},{32,0},{48,16},{1,33},{17,49},{33,1},{49,17},{2,34}... | collective-permute-start | bytes 884744 | tf_op jit(solution)/shard_map/ppermute | solution.py:26
  66.3 1.6 collective-permute-start.11
  68.4 4.6 %copy-done.2 = bf16[1,4096,1536]{2,1,0:T(8,128)(2,1)S(1)} copy-done((bf16[1,4096,1536]{2,1,0:T(8,128)(2,1)S(1)}, bf16[1,4096,1536]{2,1,0:T(8,128)(2,1)}, u32[]{:S(2)}) %copy-start.2) | copy-done | bytes 12582936
  72.9 7.5 %shard_map.89 = (bf16[4,48,4096]{2,1,0:T(8,128)(2,1)S(1)}, bf16[192,768]{1,0:T(8,128)(2,1)}) custom-call(s32[4]{0:T(128)S(1)} %pad_add_fusion.at, bf16[192,768]{1,0:T(8,128)(2,1)} %get-tuple-element.39.dg.refs_4_, bf16[192,768]{1,0:T(8,128)(2,1)S(1)} %get-tuple-element.40.du, bf16[4096,1536]{1,0:T(8,128)(2,1)S(1)} %bitcast.41), custom_call_target="tpu_custom_call" | custom-call | flops 2415919104 | bytes 12582912 | tf_op jit(solution)/shard_map/pallas_call | solution.py:190
  81.9 3.9 %all-to-all-done.1.both = bf16[4,192,1792]{2,1,0:T(8,128)(2,1)} async-done(((bf16[4,192,1792]{2,1,0:T(8,128)(2,1)}), bf16[4,192,1792]{2,1,0:T(8,128)(2,1)}, u32[]{:S(2)}, u32[]{:S(2)}) %all-to-all-start.1) | async-done | bytes 2752544 | tf_op jit(solution)/shard_map/all_to_all | solution.py:319
  85.8 4.9 %all-to-all-start = ((bf16[4,48,4096]{2,1,0:T(8,128)(2,1)}), bf16[4,48,4096]{2,1,0:T(8,128)(2,1)S(1)}, u32[]{:S(2)}, u32[]{:S(2)}) async-start(bf16[4,48,4096]{2,1,0:T(8,128)(2,1)} %copy-done.7), calls=%async_computation | async-start | bytes 3145728 | tf_op jit(solution)/shard_map/all_to_all | solution.py:329
  93.2 3.0 %shard_map.91 = (f32[256,768]{1,0:T(8,128)S(1)}, bf16[256,768]{1,0:T(8,128)(2,1)S(1)}, bf16[256,768]{1,0:T(8,128)(2,1)S(1)}, bf16[256,768]{1,0:T(8,128)(2,1)S(1)}) custom-call(s32[4]{0:T(128)S(1)} %pad_add_fusion.at, bf16[192,1024]{1,0:T(8,128)(2,1)S(1)} %copy-done.28, bf16[192,1024]{1,0:T(8,128)(2,1)S(1)} %copy-done.22, ...), custom_call_target="tpu_custom_call" | custom-call | flops 1207959552 | bytes 2752512 | tf_op jit(solution)/shard_map/pallas_call | solution.py:215
  96.9 2.0 %collective-permute-start.13 = (bf16[256,768]{1,0:T(8,128)(2,1)S(1)}, bf16[256,768]{1,0:T(8,128)(2,1)S(1)}, u32[]{:S(2)}, u32[]{:S(2)}) collective-permute-start(bf16[256,768]{1,0:T(8,128)(2,1)S(1)} %get-tuple-element.46), channel_id=1, source_target_pairs={{0,8},{4,12},{8,0},{12,4},{1,9},{5,13},{9,1},{13,5},{2,10},{6,14},... | collective-permute-start | bytes 1179656 | tf_op jit(solution)/shard_map/ppermute | solution.py:26
  99.6 2.3 %collective-permute-start.17 = (bf16[192,768]{1,0:T(8,128)(2,1)}, bf16[192,768]{1,0:T(8,128)(2,1)S(1)}, u32[]{:S(2)}, u32[]{:S(2)}) collective-permute-start(bf16[192,768]{1,0:T(8,128)(2,1)} %get-tuple-element.50.refs_4_), channel_id=1, source_target_pairs={{0,32},{16,48},{32,0},{48,16},{1,33},{17,49},{33,1},{49,17},{2,34}... | collective-permute-start | bytes 884744 | tf_op jit(solution)/shard_map/ppermute | solution.py:26
  102.6 4.3 %shard_map.93 = (f32[192,1024]{1,0:T(8,128)S(1)}, bf16[192,1024]{1,0:T(8,128)(2,1)S(1)}, bf16[192,1024]{1,0:T(8,128)(2,1)S(1)}, bf16[192,1024]{1,0:T(8,128)(2,1)}) custom-call(s32[4]{0:T(128)S(1)} %pad_add_fusion.at, bf16[4,192,1792]{2,1,0:T(8,128)(2,1)} %all-to-all-done.1.both, f32[256,768]{1,0:T(8,128)S(1)} %get-tuple-element.44.refs_0_.rest_0_), custom_call_target="tpu_custom_call" | custom-call | flops 1207959552 | bytes 2752512 | tf_op jit(solution)/shard_map/pallas_call | solution.py:244
  106.9 10.5 %collective-permute-done.12.refs_1_ = bf16[256,768]{1,0:T(8,128)(2,1)S(1)} collective-permute-done((bf16[256,768]{1,0:T(8,128)(2,1)S(1)}, bf16[256,768]{1,0:T(8,128)(2,1)S(1)}, u32[]{:S(2)}, u32[]{:S(2)}) %collective-permute-start.12) | collective-permute-done | bytes 393248 | tf_op jit(solution)/shard_map/ppermute | solution.py:26
  117.7 2.7 %collective-permute-start.24 = (bf16[192,1024]{1,0:T(8,128)(2,1)S(1)}, bf16[192,1024]{1,0:T(8,128)(2,1)S(1)}, u32[]{:S(2)}, u32[]{:S(2)}) collective-permute-start(bf16[192,1024]{1,0:T(8,128)(2,1)S(1)} %get-tuple-element.59), channel_id=1, source_target_pairs={{0,32},{16,48},{32,0},{48,16},{1,33},{17,49},{33,1},{49,17},{2,34}... | collective-permute-start | bytes 1179656 | tf_op jit(solution)/shard_map/ppermute | solution.py:26
  125.0 3.4 %shard_map.94 = (f32[256,768]{1,0:T(8,128)S(1)}, bf16[256,768]{1,0:T(8,128)(2,1)}, bf16[256,768]{1,0:T(8,128)(2,1)}, bf16[256,768]{1,0:T(8,128)(2,1)}) custom-call(s32[4]{0:T(128)S(1)} %pad_add_fusion.at, bf16[192,1024]{1,0:T(8,128)(2,1)S(1)} %copy-done.29, bf16[192,1024]{1,0:T(8,128)(2,1)S(1)} %copy-done.23, ...), custom_call_target="tpu_custom_call" | custom-call | flops 1207959552 | bytes 2752512 | tf_op jit(solution)/shard_map/pallas_call | solution.py:215
  129.4 8.4 %collective-permute-done.23.refs_1_ = bf16[192,1024]{1,0:T(8,128)(2,1)S(1)} collective-permute-done((bf16[192,1024]{1,0:T(8,128)(2,1)S(1)}, bf16[192,1024]{1,0:T(8,128)(2,1)S(1)}, u32[]{:S(2)}, u32[]{:S(2)}) %collective-permute-start.23) | collective-permute-done | bytes 393248 | tf_op jit(solution)/shard_map/ppermute | solution.py:26
  141.4 1.8 %shard_map.96 = (f32[96,1024]{1,0:T(8,128)S(1)}, bf16[96,1024]{1,0:T(8,128)(2,1)}) custom-call(s32[4]{0:T(128)S(1)} %pad_add_fusion.at, f32[192,1024]{1,0:T(8,128)S(1)} %get-tuple-element.51.refs_8_.refs_0_, bf16[192,1024]{1,0:T(8,128)(2,1)S(1)} %copy-done.18, bf16[192,1024]{1,0:T(8,128)(2,1)S(1)} %copy-done.20, ...), custom_call_target="tpu_custom_call" | custom-call | bytes 1966080 | tf_op jit(solution)/shard_map/pallas_call | solution.py:275
  145.0 1.7 %add_convert_fusion.2 = bf16[128,768]{1,0:T(8,128)(2,1)} fusion(f32[128,768]{1,0:T(8,128)S(1)} %copy-done.14, bf16[128,768]{1,0:T(8,128)(2,1)} %collective-permute-done.15), kind=kLoop, calls=%fused_computation.6 | loop fusion | flops 294912 | bytes 786432 | tf_op jit(solution)/shard_map/convert_element_type | solution.py:349
  146.8 1.9 %shard_map.90.refs_4_ = bf16[128,4096]{1,0:T(8,128)(2,1)} custom-call(s32[4]{0:T(128)S(1)} %pad_add_fusion.at, bf16[128,192]{1,0:T(8,128)(2,1)S(1)} %get-tuple-element.63.mask, bf16[4,48,4096]{2,1,0:T(8,128)(2,1)S(1)} %all-to-all-done.arrived), custom_call_target="tpu_custom_call" | custom-call | flops 201326592 | bytes 2621440 | tf_op jit(solution)/shard_map/pallas_call | solution.py:330
  155.1 2.7 %collective-permute-start.27 = (bf16[24,1024]{1,0:T(8,128)(2,1)S(1)}, bf16[24,1024]{1,0:T(8,128)(2,1)S(1)}, u32[]{:S(2)}, u32[]{:S(2)}) collective-permute-start(bf16[24,1024]{1,0:T(8,128)(2,1)S(1)} %get-tuple-element.79), channel_id=1, source_target_pairs={{0,12},{4,0},{8,4},{12,8},{1,13},{5,1},{9,5},{13,9},{2,14},{6,2},{... | collective-permute-start | bytes 147464 | tf_op jit(solution)/shard_map/ppermute | solution.py:26
  159.6 3.9 %collective-permute-done.28 = bf16[24,1024]{1,0:T(8,128)(2,1)S(1)} collective-permute-done((bf16[24,1024]{1,0:T(8,128)(2,1)S(1)}, bf16[24,1024]{1,0:T(8,128)(2,1)S(1)}, u32[]{:S(2)}, u32[]{:S(2)}) %collective-permute-start.28) | collective-permute-done | bytes 49184 | tf_op jit(solution)/shard_map/ppermute | solution.py:26
  (151 shorter events, 40.1 us)
Async XLA Ops:
  4.0 9.7 %collective-permute-start.3 = (bf16[48,4096]{1,0:T(8,128)(2,1)S(1)}, bf16[48,4096]{1,0:T(8,128)(2,1)S(1)}, u32[]{:S(2)}, u32[]{:S(2)}) collective-permute-start(bf16[48,4096]{1,0:T(8,128)(2,1)S(1)} %get-tuple-element.67), channel_id=1, source_target_pairs={{0,1},{1,0},{2,3},{3,2},{4,5},{5,4},{6,7},{7,6},{8,9},{9,8},{10,11... | collective-permute-start | bytes 1179656 | tf_op jit(solution)/shard_map/ppermute | solution.py:20
  4.0 14.2 %collective-permute-start.4 = (bf16[48,4096]{1,0:T(8,128)(2,1)}, bf16[48,4096]{1,0:T(8,128)(2,1)}, u32[]{:S(2)}, u32[]{:S(2)}) collective-permute-start(bf16[48,4096]{1,0:T(8,128)(2,1)} %get-tuple-element.66), channel_id=1, source_target_pairs={{0,2},{1,3},{2,0},{3,1},{4,6},{5,7},{6,4},{7,5},{8,10},{9,11},{10,... | collective-permute-start | bytes 1179656 | tf_op jit(solution)/shard_map/ppermute | solution.py:20
  7.9 18.3 %collective-permute-start.5 = (bf16[48,4096]{1,0:T(8,128)(2,1)}, bf16[48,4096]{1,0:T(8,128)(2,1)}, u32[]{:S(2)}, u32[]{:S(2)}) collective-permute-start(bf16[48,4096]{1,0:T(8,128)(2,1)} %get-tuple-element.65), channel_id=1, source_target_pairs={{0,3},{1,2},{2,1},{3,0},{4,7},{5,6},{6,5},{7,4},{8,11},{9,10},{10,... | collective-permute-start | bytes 1179656 | tf_op jit(solution)/shard_map/ppermute | solution.py:20
  10.1 34.4 %collective-permute-start = (bf16[48,4096]{1,0:T(8,128)(2,1)}, bf16[48,4096]{1,0:T(8,128)(2,1)S(1)}, u32[]{:S(2)}, u32[]{:S(2)}) collective-permute-start(bf16[48,4096]{1,0:T(8,128)(2,1)} %get-tuple-element.71), channel_id=1, source_target_pairs={{0,1},{1,0},{2,3},{3,2},{4,5},{5,4},{6,7},{7,6},{8,9},{9,8},{10,11... | collective-permute-start | bytes 1179656 | tf_op jit(solution)/shard_map/ppermute | solution.py:20
  10.2 34.3 %collective-permute-start.1 = (bf16[48,4096]{1,0:T(8,128)(2,1)}, bf16[48,4096]{1,0:T(8,128)(2,1)S(1)}, u32[]{:S(2)}, u32[]{:S(2)}) collective-permute-start(bf16[48,4096]{1,0:T(8,128)(2,1)} %get-tuple-element.70), channel_id=1, source_target_pairs={{0,2},{1,3},{2,0},{3,1},{4,6},{5,7},{6,4},{7,5},{8,10},{9,11},{10,... | collective-permute-start | bytes 1179656 | tf_op jit(solution)/shard_map/ppermute | solution.py:20
  13.7 30.8 %collective-permute-start.2 = (bf16[48,4096]{1,0:T(8,128)(2,1)}, bf16[48,4096]{1,0:T(8,128)(2,1)S(1)}, u32[]{:S(2)}, u32[]{:S(2)}) collective-permute-start(bf16[48,4096]{1,0:T(8,128)(2,1)} %get-tuple-element.69), channel_id=1, source_target_pairs={{0,3},{1,2},{2,1},{3,0},{4,7},{5,6},{6,5},{7,4},{8,11},{9,10},{10,... | collective-permute-start | bytes 1179656 | tf_op jit(solution)/shard_map/ppermute | solution.py:20
  29.2 15.3 %collective-permute-start.6 = (bf16[192,1024]{1,0:T(8,128)(2,1)S(1)}, bf16[192,1024]{1,0:T(8,128)(2,1)S(1)}, u32[]{:S(2)}, u32[]{:S(2)}) collective-permute-start(bf16[192,1024]{1,0:T(8,128)(2,1)S(1)} %get-tuple-element.37), channel_id=1, source_target_pairs={{0,16},{16,32},{32,48},{48,0},{1,17},{17,33},{33,49},{49,1},{2,18}... | collective-permute-start | bytes 1179656 | tf_op jit(solution)/shard_map/ppermute | solution.py:26
  30.7 13.8 %collective-permute-start.7 = (bf16[192,1024]{1,0:T(8,128)(2,1)S(1)}, bf16[192,1024]{1,0:T(8,128)(2,1)S(1)}, u32[]{:S(2)}, u32[]{:S(2)}) collective-permute-start(bf16[192,1024]{1,0:T(8,128)(2,1)S(1)} %get-tuple-element.38), channel_id=1, source_target_pairs={{0,48},{16,0},{32,16},{48,32},{1,49},{17,1},{33,17},{49,33},{2,50}... | collective-permute-start | bytes 1179656 | tf_op jit(solution)/shard_map/ppermute | solution.py:26
  47.7 38.1 %all-to-all-start.1 = ((bf16[4,192,1792]{2,1,0:T(8,128)(2,1)}), bf16[4,192,1792]{2,1,0:T(8,128)(2,1)}, u32[]{:S(2)}, u32[]{:S(2)}) async-start(bf16[4,192,1792]{2,1,0:T(8,128)(2,1)} %copy-done.3), calls=%async_computation.1 | async-start | bytes 5505024 | tf_op jit(solution)/shard_map/all_to_all | solution.py:319
  52.3 38.3 %collective-permute-start.8 = (bf16[192,1024]{1,0:T(8,128)(2,1)}, bf16[192,1024]{1,0:T(8,128)(2,1)}, u32[]{:S(2)}, u32[]{:S(2)}) collective-permute-start(bf16[192,1024]{1,0:T(8,128)(2,1)} %copy-done.30), channel_id=1, source_target_pairs={{0,32},{16,48},{32,0},{48,16},{1,33},{17,49},{33,1},{49,17},{2,34}... | collective-permute-start | bytes 1179656 | tf_op jit(solution)/shard_map/ppermute | solution.py:26
  64.5 26.1 %collective-permute-start.10 = (bf16[192,768]{1,0:T(8,128)(2,1)}, bf16[192,768]{1,0:T(8,128)(2,1)}, u32[]{:S(2)}, u32[]{:S(2)}) collective-permute-start(bf16[192,768]{1,0:T(8,128)(2,1)} %get-tuple-element.39.dg.refs_4_), channel_id=1, source_target_pairs={{0,32},{16,48},{32,0},{48,16},{1,33},{17,49},{33,1},{49,17},{2,34}... | collective-permute-start | bytes 884744 | tf_op jit(solution)/shard_map/ppermute | solution.py:26
  66.3 24.4 %collective-permute-start.11 = (bf16[192,768]{1,0:T(8,128)(2,1)}, bf16[192,768]{1,0:T(8,128)(2,1)}, u32[]{:S(2)}, u32[]{:S(2)}) collective-permute-start(bf16[192,768]{1,0:T(8,128)(2,1)} %get-tuple-element.39.dg.refs_4_), channel_id=1, source_target_pairs={{0,48},{16,0},{32,16},{48,32},{1,49},{17,1},{33,17},{49,33},{2,50}... | collective-permute-start | bytes 884744 | tf_op jit(solution)/shard_map/ppermute | solution.py:26
  67.9 22.8 %collective-permute-start.9 = (bf16[192,768]{1,0:T(8,128)(2,1)}, bf16[192,768]{1,0:T(8,128)(2,1)}, u32[]{:S(2)}, u32[]{:S(2)}) collective-permute-start(bf16[192,768]{1,0:T(8,128)(2,1)} %get-tuple-element.39.dg.refs_4_), channel_id=1, source_target_pairs={{0,16},{16,32},{32,48},{48,0},{1,17},{17,33},{33,49},{49,1},{2,18}... | collective-permute-start | bytes 884744 | tf_op jit(solution)/shard_map/ppermute | solution.py:26
  81.6 20.3 %collective-permute-start.16 = (bf16[192,768]{1,0:T(8,128)(2,1)}, bf16[192,768]{1,0:T(8,128)(2,1)}, u32[]{:S(2)}, u32[]{:S(2)}) collective-permute-start(bf16[192,768]{1,0:T(8,128)(2,1)} %get-tuple-element.50.refs_4_), channel_id=1, source_target_pairs={{0,16},{16,32},{32,48},{48,0},{1,17},{17,33},{33,49},{49,1},{2,18}... | collective-permute-start | bytes 884744 | tf_op jit(solution)/shard_map/ppermute | solution.py:26
  85.8 60.9 %all-to-all-start = ((bf16[4,48,4096]{2,1,0:T(8,128)(2,1)}), bf16[4,48,4096]{2,1,0:T(8,128)(2,1)S(1)}, u32[]{:S(2)}, u32[]{:S(2)}) async-start(bf16[4,48,4096]{2,1,0:T(8,128)(2,1)} %copy-done.7), calls=%async_computation | async-start | bytes 3145728 | tf_op jit(solution)/shard_map/all_to_all | solution.py:329
  96.2 21.2 %collective-permute-start.12 = (bf16[256,768]{1,0:T(8,128)(2,1)S(1)}, bf16[256,768]{1,0:T(8,128)(2,1)S(1)}, u32[]{:S(2)}, u32[]{:S(2)}) collective-permute-start(bf16[256,768]{1,0:T(8,128)(2,1)S(1)} %get-tuple-element.45), channel_id=1, source_target_pairs={{0,4},{4,8},{8,12},{12,0},{1,5},{5,9},{9,13},{13,1},{2,6},{6,10},{... | collective-permute-start | bytes 1179656 | tf_op jit(solution)/shard_map/ppermute | solution.py:26
  96.9 20.8 %collective-permute-start.13 = (bf16[256,768]{1,0:T(8,128)(2,1)S(1)}, bf16[256,768]{1,0:T(8,128)(2,1)S(1)}, u32[]{:S(2)}, u32[]{:S(2)}) collective-permute-start(bf16[256,768]{1,0:T(8,128)(2,1)S(1)} %get-tuple-element.46), channel_id=1, source_target_pairs={{0,8},{4,12},{8,0},{12,4},{1,9},{5,13},{9,1},{13,5},{2,10},{6,14},... | collective-permute-start | bytes 1179656 | tf_op jit(solution)/shard_map/ppermute | solution.py:26
  98.9 21.5 %collective-permute-start.14 = (bf16[256,768]{1,0:T(8,128)(2,1)S(1)}, bf16[256,768]{1,0:T(8,128)(2,1)S(1)}, u32[]{:S(2)}, u32[]{:S(2)}) collective-permute-start(bf16[256,768]{1,0:T(8,128)(2,1)S(1)} %get-tuple-element.47), channel_id=1, source_target_pairs={{0,12},{4,0},{8,4},{12,8},{1,13},{5,1},{9,5},{13,9},{2,14},{6,2},{... | collective-permute-start | bytes 1179656 | tf_op jit(solution)/shard_map/ppermute | solution.py:26
  99.6 24.3 %collective-permute-start.17 = (bf16[192,768]{1,0:T(8,128)(2,1)}, bf16[192,768]{1,0:T(8,128)(2,1)S(1)}, u32[]{:S(2)}, u32[]{:S(2)}) collective-permute-start(bf16[192,768]{1,0:T(8,128)(2,1)} %get-tuple-element.50.refs_4_), channel_id=1, source_target_pairs={{0,32},{16,48},{32,0},{48,16},{1,33},{17,49},{33,1},{49,17},{2,34}... | collective-permute-start | bytes 884744 | tf_op jit(solution)/shard_map/ppermute | solution.py:26
  101.9 23.1 %collective-permute-start.18 = (bf16[192,768]{1,0:T(8,128)(2,1)}, bf16[192,768]{1,0:T(8,128)(2,1)S(1)}, u32[]{:S(2)}, u32[]{:S(2)}) collective-permute-start(bf16[192,768]{1,0:T(8,128)(2,1)} %get-tuple-element.50.refs_4_), channel_id=1, source_target_pairs={{0,48},{16,0},{32,16},{48,32},{1,49},{17,1},{33,17},{49,33},{2,50}... | collective-permute-start | bytes 884744 | tf_op jit(solution)/shard_map/ppermute | solution.py:26
  117.4 20.4 %collective-permute-start.23 = (bf16[192,1024]{1,0:T(8,128)(2,1)S(1)}, bf16[192,1024]{1,0:T(8,128)(2,1)S(1)}, u32[]{:S(2)}, u32[]{:S(2)}) collective-permute-start(bf16[192,1024]{1,0:T(8,128)(2,1)S(1)} %get-tuple-element.58), channel_id=1, source_target_pairs={{0,16},{16,32},{32,48},{48,0},{1,17},{17,33},{33,49},{49,1},{2,18}... | collective-permute-start | bytes 1179656 | tf_op jit(solution)/shard_map/ppermute | solution.py:26
  117.7 20.9 %collective-permute-start.24 = (bf16[192,1024]{1,0:T(8,128)(2,1)S(1)}, bf16[192,1024]{1,0:T(8,128)(2,1)S(1)}, u32[]{:S(2)}, u32[]{:S(2)}) collective-permute-start(bf16[192,1024]{1,0:T(8,128)(2,1)S(1)} %get-tuple-element.59), channel_id=1, source_target_pairs={{0,32},{16,48},{32,0},{48,16},{1,33},{17,49},{33,1},{49,17},{2,34}... | collective-permute-start | bytes 1179656 | tf_op jit(solution)/shard_map/ppermute | solution.py:26
  120.4 18.9 %collective-permute-start.25 = (bf16[192,1024]{1,0:T(8,128)(2,1)}, bf16[192,1024]{1,0:T(8,128)(2,1)}, u32[]{:S(2)}, u32[]{:S(2)}) collective-permute-start(bf16[192,1024]{1,0:T(8,128)(2,1)} %get-tuple-element.60), channel_id=1, source_target_pairs={{0,48},{16,0},{32,16},{48,32},{1,49},{17,1},{33,17},{49,33},{2,50}... | collective-permute-start | bytes 1179656 | tf_op jit(solution)/shard_map/ppermute | solution.py:26
  124.0 21.0 %collective-permute-start.15 = (bf16[128,768]{1,0:T(8,128)(2,1)}, bf16[128,768]{1,0:T(8,128)(2,1)}, u32[]{:S(2)}, u32[]{:S(2)}) collective-permute-start(bf16[128,768]{1,0:T(8,128)(2,1)} %get-tuple-element.49), channel_id=1, source_target_pairs={{0,64},{64,0},{1,65},{65,1},{2,66},{66,2},{3,67},{67,3},{4,68},{68... | collective-permute-start | bytes 589832 | tf_op jit(solution)/shard_map/ppermute | solution.py:30
  129.4 19.6 %collective-permute-start.19 = (bf16[256,768]{1,0:T(8,128)(2,1)}, bf16[256,768]{1,0:T(8,128)(2,1)}, u32[]{:S(2)}, u32[]{:S(2)}) collective-permute-start(bf16[256,768]{1,0:T(8,128)(2,1)} %get-tuple-element.53), channel_id=1, source_target_pairs={{0,4},{4,8},{8,12},{12,0},{1,5},{5,9},{9,13},{13,1},{2,6},{6,10},{... | collective-permute-start | bytes 1179656 | tf_op jit(solution)/shard_map/ppermute | solution.py:26
  138.6 10.4 %collective-permute-start.20 = (bf16[256,768]{1,0:T(8,128)(2,1)}, bf16[256,768]{1,0:T(8,128)(2,1)}, u32[]{:S(2)}, u32[]{:S(2)}) collective-permute-start(bf16[256,768]{1,0:T(8,128)(2,1)} %get-tuple-element.54), channel_id=1, source_target_pairs={{0,8},{4,12},{8,0},{12,4},{1,9},{5,13},{9,1},{13,5},{2,10},{6,14},... | collective-permute-start | bytes 1179656 | tf_op jit(solution)/shard_map/ppermute | solution.py:26
  139.3 11.0 %collective-permute-start.21 = (bf16[256,768]{1,0:T(8,128)(2,1)}, bf16[256,768]{1,0:T(8,128)(2,1)}, u32[]{:S(2)}, u32[]{:S(2)}) collective-permute-start(bf16[256,768]{1,0:T(8,128)(2,1)} %get-tuple-element.55), channel_id=1, source_target_pairs={{0,12},{4,0},{8,4},{12,8},{1,13},{5,1},{9,5},{13,9},{2,14},{6,2},{... | collective-permute-start | bytes 1179656 | tf_op jit(solution)/shard_map/ppermute | solution.py:26
  144.0 10.1 %collective-permute-start.26 = (bf16[96,1024]{1,0:T(8,128)(2,1)}, bf16[96,1024]{1,0:T(8,128)(2,1)}, u32[]{:S(2)}, u32[]{:S(2)}) collective-permute-start(bf16[96,1024]{1,0:T(8,128)(2,1)} %get-tuple-element.62), channel_id=1, source_target_pairs={{0,64},{64,0},{1,65},{65,1},{2,66},{66,2},{3,67},{67,3},{4,68},{68... | collective-permute-start | bytes 589832 | tf_op jit(solution)/shard_map/ppermute | solution.py:30
  153.0 5.8 %collective-permute-start.22 = (bf16[128,768]{1,0:T(8,128)(2,1)S(1)}, bf16[128,768]{1,0:T(8,128)(2,1)S(1)}, u32[]{:S(2)}, u32[]{:S(2)}) collective-permute-start(bf16[128,768]{1,0:T(8,128)(2,1)S(1)} %get-tuple-element.57), channel_id=1, source_target_pairs={{0,64},{64,0},{1,65},{65,1},{2,66},{66,2},{3,67},{67,3},{4,68},{68... | collective-permute-start | bytes 589832 | tf_op jit(solution)/shard_map/ppermute | solution.py:30
  155.1 4.5 %collective-permute-start.27 = (bf16[24,1024]{1,0:T(8,128)(2,1)S(1)}, bf16[24,1024]{1,0:T(8,128)(2,1)S(1)}, u32[]{:S(2)}, u32[]{:S(2)}) collective-permute-start(bf16[24,1024]{1,0:T(8,128)(2,1)S(1)} %get-tuple-element.79), channel_id=1, source_target_pairs={{0,12},{4,0},{8,4},{12,8},{1,13},{5,1},{9,5},{13,9},{2,14},{6,2},{... | collective-permute-start | bytes 147464 | tf_op jit(solution)/shard_map/ppermute | solution.py:26
  157.8 5.7 %collective-permute-start.28 = (bf16[24,1024]{1,0:T(8,128)(2,1)S(1)}, bf16[24,1024]{1,0:T(8,128)(2,1)S(1)}, u32[]{:S(2)}, u32[]{:S(2)}) collective-permute-start(bf16[24,1024]{1,0:T(8,128)(2,1)S(1)} %get-tuple-element.78), channel_id=1, source_target_pairs={{0,8},{4,12},{8,0},{12,4},{1,9},{5,13},{9,1},{13,5},{2,10},{6,14},... | collective-permute-start | bytes 147464 | tf_op jit(solution)/shard_map/ppermute | solution.py:26
  157.8 5.8 %collective-permute-start.29 = (bf16[24,1024]{1,0:T(8,128)(2,1)S(1)}, bf16[24,1024]{1,0:T(8,128)(2,1)S(1)}, u32[]{:S(2)}, u32[]{:S(2)}) collective-permute-start(bf16[24,1024]{1,0:T(8,128)(2,1)S(1)} %get-tuple-element.77), channel_id=1, source_target_pairs={{0,4},{4,8},{8,12},{12,0},{1,5},{5,9},{9,13},{13,1},{2,6},{6,10},{... | collective-permute-start | bytes 147464 | tf_op jit(solution)/shard_map/ppermute | solution.py:26
  (35 other events, 136.7 us)
